TPU v7x, 32 devices: a whole 2x2x4 slice. The times are simulated.
32 devices in a mesh: groups: 2 (over y), rows: 4 (over z), cols: 2 (over x), sub: 2 (over core).
Axes of the slice: x: 2, y: 2, z: 4, core: 2. Of those that a mesh axis runs over, the one named last changes fastest.
Arguments:
- displace: float32 [6, 65536], P(None, ('groups', 'rows', 'cols', 'sub')), parts along dimension 1, may hold values from -6 to 6
- velocity: float32 [6, 65536], P(None, ('groups', 'rows', 'cols', 'sub')), parts along dimension 1, may hold values from -6 to 6
- nodal_mass: float32 [65536], P(('groups', 'rows', 'cols', 'sub')), parts along dimension 0, may hold values from 0.5 to 2
- send_list: int32 [12, 6, 1024], P('rows', 'cols', ('groups', 'sub')), parts along dimension 2, may hold values from 0 to 2047
- beam_slots: int32 [6, 65536], P(None, ('groups', 'rows', 'cols', 'sub')), parts along dimension 1, may hold values from 0 to 8703, as said below
- shape_values: float32 [6, 65536], P(None, ('groups', 'rows', 'cols', 'sub')), parts along dimension 1, as said below
- beam_kind: int32 [65536], P(('groups', 'rows', 'cols', 'sub')), parts along dimension 0, may hold values from 0 to 7
- cluster_weight: float32 [65536], P(('groups', 'rows', 'cols', 'sub')), parts along dimension 0, may hold values from 0.5 to 5
- stiffness: float32 [8, 12, 12], replicated, may hold values from -1.75 to 1.75
Outputs:
- field_out: float32 [6, 65536], P(None, ('groups', 'rows', 'cols', 'sub')), parts along dimension 1
- velocity_out: float32 [6, 65536], P(None, ('groups', 'rows', 'cols', 'sub')), parts along dimension 1
There are 2 independent parts, one for each index of `groups`. A program takes and returns all parts, laid end to end along the dimension named above; an argument that names none is the same for every part. Nothing has to cross between parts.
Inputs may be any that keep to these rules, and one draw needn't show every extreme that they name: `beam_slots`: below 2 * 2048 a slot is a repnode of the device's own block; above it the slot lies in a received list, never in list (1, 1). `shape_values`: Positive; the three values of each beam end sum to one.
All inputs are finite; a program needn't handle non-finite values.
Results may differ from a plain program's by a relative error of at most 0.0003.
Values sent between devices are 32-bit elements; how exact they have to be, the bound alone decides.
No kernel may reach another device: no remote copies, remote signals or barrier semaphores. Data moves between devices by JAX's collectives and lax.ppermute only.
A program may use at most 64 MiB of HBM per device.

v0:
```python
import jax
import jax.numpy as jnp
from jax import lax
from jax.sharding import PartitionSpec as P

STEPS = 2


def extended(block, sides, width):
    for axis, dim in sides:
        count = lax.axis_size(axis)
        forward = [(i, i + 1) for i in range(count - 1)]
        backward = [(target, source) for source, target in forward]
        low = lax.ppermute(
            lax.slice_in_dim(block, block.shape[dim] - width, None, axis=dim), axis, forward
        )
        high = lax.ppermute(lax.slice_in_dim(block, 0, width, axis=dim), axis, backward)
        block = jnp.concatenate([low, block, high], axis=dim)
    return block


def beam_forces(buffer, slot_pick, shape_pick, kind_pick, weight, stiffness):
    beam_count = slot_pick.shape[1]
    gathered = jnp.take(buffer, slot_pick, axis=1) * shape_pick[None]
    beam_ends = gathered.reshape(6, 2, 3, beam_count).sum(axis=2)
    beam_vec = beam_ends.transpose(1, 0, 2).reshape(12, beam_count)
    per_kind = jnp.einsum("tij,jb->tib", stiffness, beam_vec, precision=lax.Precision.HIGHEST)
    selector = (
        kind_pick[None, :] == jnp.arange(stiffness.shape[0], dtype=jnp.int32)[:, None]
    ).astype(jnp.float32)
    beam_force = jnp.sum(per_kind * selector[:, None, :], axis=0)
    end_force = beam_force.reshape(2, 6, beam_count).transpose(1, 0, 2)
    scaled = shape_pick.reshape(2, 3, beam_count) * weight[None, None, :]
    per_slot = end_force[:, :, None, :] * scaled[None]
    contrib = jnp.zeros((6, buffer.shape[1]), jnp.float32)
    return contrib.at[:, slot_pick.reshape(-1)].add(per_slot.reshape(6, -1))


def shards(
    displace,
    velocity,
    nodal_mass,
    send_list,
    beam_slots,
    shape_values,
    beam_kind,
    cluster_weight,
    stiffness,
):
    list_len = send_list.shape[2]
    flat_list = send_list.reshape(-1)
    field_now = displace
    velocity_now = velocity
    for _ in range(STEPS):
        outgoing = (
            jnp.take(field_now, flat_list, axis=1).reshape(6, 3, 3, list_len).transpose(1, 2, 0, 3)
        )
        padded = extended(outgoing, (("rows", 0), ("cols", 1)), 1)
        arrived = padded[::-2, ::-2]
        local_pair, near_pair = (
            lax.all_gather(field_now, "sub", axis=1, tiled=True),
            lax.all_gather(arrived[None], "sub", axis=0, tiled=True),
        )
        local_count = local_pair.shape[1]
        buffer = jnp.concatenate(
            [local_pair, near_pair.transpose(3, 0, 1, 2, 4).reshape(6, -1)], axis=1
        )
        contrib = beam_forces(
            buffer, beam_slots, shape_values, beam_kind, cluster_weight, stiffness
        )
        local_part = contrib[:, :local_count]
        near_part = contrib[:, local_count:].reshape(6, -1, 3, 3, list_len).transpose(1, 2, 3, 0, 4)
        own_local, own_near = (
            lax.psum_scatter(local_part, "sub", scatter_dimension=1, tiled=True),
            lax.psum_scatter(near_part, "sub", scatter_dimension=0, tiled=True),
        )
        padded_back = extended(own_near[0, ::-1, ::-1], (("rows", 0), ("cols", 1)), 1)
        returned = padded_back[::2, ::2]
        net_force = own_local.at[:, flat_list].add(returned.transpose(2, 0, 1, 3).reshape(6, -1))
        velocity_now = 0.98 * velocity_now - 0.2 * net_force / nodal_mass[None, :]
        field_now = field_now + 0.2 * velocity_now
    return (field_now, velocity_now)


def solution(mesh):
    in_specs = (
        P(None, ("groups", "rows", "cols", "sub")),
        P(None, ("groups", "rows", "cols", "sub")),
        P(("groups", "rows", "cols", "sub")),
        P("rows", "cols", ("groups", "sub")),
        P(None, ("groups", "rows", "cols", "sub")),
        P(None, ("groups", "rows", "cols", "sub")),
        P(("groups", "rows", "cols", "sub")),
        P(("groups", "rows", "cols", "sub")),
        P(),
    )
    out_specs = (
        P(None, ("groups", "rows", "cols", "sub")),
        P(None, ("groups", "rows", "cols", "sub")),
    )
    return jax.shard_map(shards, mesh=mesh, in_specs=in_specs, out_specs=out_specs, check_vma=False)
```

profile of v0, /device:TPU:8, one launch (start us, length us, event | category | flops | bytes accessed | tf_op | source)
XLA Modules:
  0.0 419.3 jit_solution(8391544501794990642)
XLA Ops:
  7.3 0.8 reshape.167
  8.1 1.2 copy.139
  9.3 3.9 gather_fusion
  13.2 1.2 broadcast_select_fusion.1
  14.8 3.5 collective-permute-start
  18.3 2.4 collective-permute-start.1
  20.9 3.1 collective-permute-done.1
  24.1 1.3 collective-permute-start.3
  25.4 4.5 %collective-permute-start.2 = (f32[5,1,6,256]{3,1,2,0:T(1,128)S(1)}, f32[5,1,6,256]{3,1,2,0:T(1,128)S(1)}, u32[]{:S(2)}, u32[]{:S(2)}) collective-permute-start(f32[5,1,6,256]{3,1,2,0:T(1,128)S(1)} %copy.141), channel_id=1, source_target_pairs={{0,2},{1,3},{4,6},{5,7},{8,10},{9,11},{12,14},{13,15},{16,18},{17,... | collective-permute-start | bytes 92168 | tf_op jit(solution)/shard_map/ppermute | solution.py:14
  30.1 1.9 all_gather.12
  32.1 1.9 all-gather
  34.1 2.9 copy.145
  36.9 43.6 %gather_fusion.1 = f32[12288,6]{1,0:T(8,128)} fusion(f32[6,8704]{0,1:T(8,128)} %copy.145, s32[12288]{0:T(1024)S(1)} %broadcast_clamp_fusion), kind=kCustom, calls=%fused_computation.1.clone | custom fusion | bytes 638976 | tf_op jit(solution)/shard_map/jit(_take)/gather | solution.py:24
  80.5 10.9 %bitcast_multiply_fusion.3 = f32[6,6,2048]{0,2,1:T(8,128)} fusion(f32[6,2048,6]{2,1,0:T(8,128)} %bitcast.92, f32[6,2048]{1,0:T(8,128)S(1)} %copy-done.1, pred[6,2048]{1,0:T(8,128)(4,1)S(1)} %compare_and_fusion), kind=kLoop, calls=%fused_computation.15 | loop fusion | flops 147456 | bytes 651264 | tf_op jit(solution)/shard_map/mul | solution.py:24
  91.4 3.5 reduce_sum.36
  95.6 1.0 fusion.8
  97.2 4.4 %bitcast_multiply_fusion.2 = f32[6,12288]{0,1:T(8,128)} fusion(f32[12288]{0:T(1024)S(1)} %mul.103, f32[6,2,2048]{0,2,1:T(8,128)S(1)} %copy.148), kind=kLoop, calls=%fused_computation.14 | loop fusion | flops 73728 | bytes 442368 | tf_op jit(solution)/shard_map/mul | solution.py:34
  101.6 62.4 %scatter_custom_fusion = f32[6,8704]{0,1:T(8,128)} fusion(s32[12288]{0:T(1024)S(1)} %bitcast.111, f32[6,12288]{0,1:T(8,128)} %bitcast_multiply_fusion.2, f32[]{:T(128)} %constant.23.clone.1), kind=kCustom, calls=%fused_computation.12 | custom fusion | flops 73728 | bytes 503812 | tf_op jit(solution)/shard_map/scatter-add | solution.py:36
  164.0 1.7 slice-done.1
  165.7 1.3 copy.149
  167.2 3.1 slice.138
  170.3 5.1 %reduce-scatter.7.cloned.1.call-done = f32[1,3,3,6,256]{4,3,2,1,0:T(8,128)} async-done(((f32[2,3,3,6,256]{4,3,2,1,0:T(8,128)}), f32[1,3,3,6,256]{4,3,2,1,0:T(8,128)}) %reduce-scatter.7.cloned.1.call-update) | async-done | bytes 55312 | tf_op jit(solution)/shard_map/reduce_scatter | solution.py:75
  175.4 0.8 fusion.16
  176.2 2.2 collective-permute-start.5
  178.4 3.6 collective-permute-start.4
  182.1 0.9 reverse_bitcast_fusion.1
  183.0 1.2 collective-permute-done.4
  184.2 1.3 collective-permute-start.7
  185.5 4.7 %collective-permute-start.6 = (f32[5,1,6,256]{3,1,2,0:T(1,128)S(1)}, f32[5,1,6,256]{3,1,2,0:T(1,128)S(1)}, u32[]{:S(2)}, u32[]{:S(2)}) collective-permute-start(f32[5,1,6,256]{3,1,2,0:T(1,128)S(1)} %copy.150), channel_id=1, source_target_pairs={{0,2},{1,3},{4,6},{5,7},{8,10},{9,11},{12,14},{13,15},{16,18},{17,... | collective-permute-start | bytes 92168 | tf_op jit(solution)/shard_map/ppermute | solution.py:14
  190.3 1.3 collective-permute-done.6
  192.1 15.2 %scatter_fusion = f32[6,2048]{0,1:T(8,128)} fusion(f32[6,2048]{0,1:T(8,128)} %reduce-scatter.5.cloned.1.call-done, s32[2304]{0:T(1024)S(1)} %fusion.13, f32[2304,6]{1,0:T(8,128)S(1)} %copy.154), kind=kCustom, calls=%fused_computation.5 | custom fusion | flops 13824 | bytes 175104 | tf_op jit(solution)/shard_map/scatter-add | solution.py:79
  207.4 1.5 copy.155
  209.3 3.9 gather_fusion.2
  213.2 1.2 broadcast_select_fusion
  214.8 3.6 collective-permute-start.8
  218.5 2.2 collective-permute-start.9
  220.7 3.5 collective-permute-done.9
  224.3 1.3 collective-permute-start.11
  225.6 4.5 %collective-permute-start.10 = (f32[5,1,6,256]{3,1,2,0:T(1,128)S(1)}, f32[5,1,6,256]{3,1,2,0:T(1,128)S(1)}, u32[]{:S(2)}, u32[]{:S(2)}) collective-permute-start(f32[5,1,6,256]{3,1,2,0:T(1,128)S(1)} %copy.158), channel_id=1, source_target_pairs={{0,2},{1,3},{4,6},{5,7},{8,10},{9,11},{12,14},{13,15},{16,18},{17,... | collective-permute-start | bytes 92168 | tf_op jit(solution)/shard_map/ppermute | solution.py:14
  230.2 1.9 all_gather.14
  232.1 2.0 copy.163
  234.1 1.9 all-gather.1
  236.7 4.7 %pad_maximum_fusion = f32[6,8704]{0,1:T(8,128)} fusion(f32[6,4608]{0,1:T(8,128)S(1)} %bitcast.88, f32[6,4096]{0,1:T(8,128)} %copy.163), kind=kLoop, calls=%fused_computation.16 | loop fusion | flops 52224 | bytes 417792 | tf_op jit(solution)/shard_map/concatenate | solution.py:65
  241.4 43.6 %gather_fusion.3 = f32[12288,6]{1,0:T(8,128)} fusion(f32[6,8704]{0,1:T(8,128)} %pad_maximum_fusion, s32[12288]{0:T(1024)S(1)} %broadcast_clamp_fusion), kind=kCustom, calls=%fused_computation.3.clone | custom fusion | bytes 638976 | tf_op jit(solution)/shard_map/jit(_take)/gather | solution.py:24
  285.0 10.9 %bitcast_multiply_fusion.1 = f32[6,6,2048]{0,2,1:T(8,128)} fusion(f32[6,2048,6]{2,1,0:T(8,128)} %bitcast.91, f32[6,2048]{1,0:T(8,128)S(1)} %copy-done.1, pred[6,2048]{1,0:T(8,128)(4,1)S(1)} %compare_and_fusion), kind=kLoop, calls=%fused_computation.11 | loop fusion | flops 147456 | bytes 651264 | tf_op jit(solution)/shard_map/mul | solution.py:24
  295.9 3.5 reduce_sum.38
  300.1 1.0 fusion.9
  301.7 4.4 %bitcast_multiply_fusion = f32[6,12288]{0,1:T(8,128)} fusion(f32[6,2,2048]{0,2,1:T(8,128)S(1)} %copy.166, f32[12288]{0:T(1024)S(1)} %mul.103), kind=kLoop, calls=%fused_computation.10 | loop fusion | flops 73728 | bytes 442368 | tf_op jit(solution)/shard_map/mul | solution.py:34
  306.1 62.4 %scatter_custom_fusion.2 = f32[6,8704]{0,1:T(8,128)} fusion(s32[12288]{0:T(1024)S(1)} %bitcast.112, f32[6,12288]{0,1:T(8,128)} %bitcast_multiply_fusion, f32[]{:T(128)} %constant.23.clone.1), kind=kCustom, calls=%fused_computation.8 | custom fusion | flops 73728 | bytes 503812 | tf_op jit(solution)/shard_map/scatter-add | solution.py:36
  368.5 1.7 slice-done
  370.2 1.3 copy.167
  371.6 3.1 slice.144
  374.7 3.9 reduce-scatter.11.cloned.1.call-done
  378.6 0.8 fusion.14
  379.3 2.2 collective-permute-start.13
  381.6 3.6 collective-permute-start.12
  385.2 0.9 reverse_bitcast_fusion
  386.1 1.2 collective-permute-done.12
  387.3 1.3 collective-permute-start.15
  388.7 4.5 %collective-permute-start.14 = (f32[5,1,6,256]{3,1,2,0:T(1,128)S(1)}, f32[5,1,6,256]{3,1,2,0:T(1,128)S(1)}, u32[]{:S(2)}, u32[]{:S(2)}) collective-permute-start(f32[5,1,6,256]{3,1,2,0:T(1,128)S(1)} %copy.168), channel_id=1, source_target_pairs={{0,2},{1,3},{4,6},{5,7},{8,10},{9,11},{12,14},{13,15},{16,18},{17,... | collective-permute-start | bytes 92168 | tf_op jit(solution)/shard_map/ppermute | solution.py:14
  393.3 1.5 collective-permute-done.14
  395.3 15.2 %scatter_fusion.1 = f32[6,2048]{0,1:T(8,128)} fusion(f32[6,2048]{0,1:T(8,128)} %reduce-scatter.9.cloned.1.call-done, s32[2304]{0:T(1024)S(1)} %fusion.13, f32[2304,6]{1,0:T(8,128)S(1)} %copy.172), kind=kCustom, calls=%fused_computation.7 | custom fusion | flops 13824 | bytes 175104 | tf_op jit(solution)/shard_map/scatter-add | solution.py:79
  410.5 1.5 copy.173
  412.0 0.7 multiply_add_fusion
  (108 shorter events, 6.4 us)
Async XLA Ops:
  7.2 88.4 %copy-start = (f32[8,12,12]{2,0,1:T(8,128)S(1)}, f32[8,12,12]{2,0,1:T(8,128)}, u32[]{:S(2)}) copy-start(f32[8,12,12]{2,0,1:T(8,128)} %param.21) | copy-start | bytes 13828
  7.2 22.9 %copy-start.3 = (f32[6,2048]{1,0:T(8,128)S(1)}, f32[6,2048]{1,0:T(8,128)}, u32[]{:S(2)}) copy-start(f32[6,2048]{1,0:T(8,128)} %param.13) | copy-start | bytes 147460
  7.2 13.5 %copy-start.2 = (s32[6,2048]{1,0:T(8,128)S(1)}, s32[6,2048]{1,0:T(8,128)}, u32[]{:S(2)}) copy-start(s32[6,2048]{1,0:T(8,128)} %param.17) | copy-start | bytes 147460
  7.2 22.8 %copy-start.7 = (s32[2048]{0:T(1024)S(1)}, s32[2048]{0:T(1024)}, u32[]{:S(2)}) copy-start(s32[2048]{0:T(1024)} %param.19) | copy-start | bytes 24580
  7.2 22.8 %copy-start.1 = (f32[6,2048]{1,0:T(8,128)S(1)}, f32[6,2048]{1,0:T(8,128)}, u32[]{:S(2)}) copy-start(f32[6,2048]{1,0:T(8,128)} %param.18) | copy-start | bytes 147460
  7.2 22.8 %copy-start.8 = (f32[2048]{0:T(1024)S(1)}, f32[2048]{0:T(1024)}, u32[]{:S(2)}) copy-start(f32[2048]{0:T(1024)} %param.20) | copy-start | bytes 24580
  7.2 168.2 %reduce-scatter.7.cloned.1.call-start = ((), (), s32[]{:S(2)}) async-start(), calls=%async_computation.5 | async-start | bytes 221184 | tf_op jit(solution)/shard_map/reduce_scatter | solution.py:75
  14.8 6.1 %collective-permute-start = (f32[1,3,6,256]{3,2,1,0:T(8,128)S(1)}, f32[1,3,6,256]{3,2,1,0:T(8,128)S(1)}, u32[]{:S(2)}, u32[]{:S(2)}) collective-permute-start(f32[1,3,6,256]{3,2,1,0:T(8,128)S(1)} %get-tuple-element.30), channel_id=1, source_target_pairs={{0,4},{4,8},{8,12},{1,5},{5,9},{9,13},{2,6},{6,10},{10,14},{3,7},{... | collective-permute-start | bytes 55304 | tf_op jit(solution)/shard_map/ppermute | solution.py:14
  18.3 5.7 %collective-permute-start.1 = (f32[1,3,6,256]{3,2,1,0:T(8,128)S(1)}, f32[1,3,6,256]{3,2,1,0:T(8,128)S(1)}, u32[]{:S(2)}, u32[]{:S(2)}) collective-permute-start(f32[1,3,6,256]{3,2,1,0:T(8,128)S(1)} %get-tuple-element.31), channel_id=1, source_target_pairs={{4,0},{8,4},{12,8},{5,1},{9,5},{13,9},{6,2},{10,6},{14,10},{7,3},{... | collective-permute-start | bytes 55304 | tf_op jit(solution)/shard_map/ppermute | solution.py:17
  24.1 7.9 %collective-permute-start.3 = (f32[5,1,6,256]{3,1,2,0:T(1,128)S(1)}, f32[5,1,6,256]{3,1,2,0:T(1,128)S(1)}, u32[]{:S(2)}, u32[]{:S(2)}) collective-permute-start(f32[5,1,6,256]{3,1,2,0:T(1,128)S(1)} %copy.142), channel_id=1, source_target_pairs={{2,0},{3,1},{6,4},{7,5},{10,8},{11,9},{14,12},{15,13},{18,16},{19,... | collective-permute-start | bytes 92168 | tf_op jit(solution)/shard_map/ppermute | solution.py:17
  25.4 6.6 %collective-permute-start.2 = (f32[5,1,6,256]{3,1,2,0:T(1,128)S(1)}, f32[5,1,6,256]{3,1,2,0:T(1,128)S(1)}, u32[]{:S(2)}, u32[]{:S(2)}) collective-permute-start(f32[5,1,6,256]{3,1,2,0:T(1,128)S(1)} %copy.141), channel_id=1, source_target_pairs={{0,2},{1,3},{4,6},{5,7},{8,10},{9,11},{12,14},{13,15},{16,18},{17,... | collective-permute-start | bytes 92168 | tf_op jit(solution)/shard_map/ppermute | solution.py:14
  164.0 1.7 slice-start.1
  164.0 3.1 copy-start.5
  167.1 25.1 %reduce-scatter.5.cloned.1.call-start = ((), (), s32[]{:S(2)}) async-start(), calls=%async_computation.4 | async-start | bytes 3145728 | tf_op jit(solution)/shard_map/reduce_scatter | solution.py:74
  170.2 38.7 %copy-start.4 = (f32[6,2048]{1,0:T(8,128)S(1)}, f32[6,2048]{1,0:T(8,128)}, u32[]{:S(2)}) copy-start(f32[6,2048]{1,0:T(8,128)} %param.14) | copy-start | bytes 147460
  170.2 38.7 %copy-start.6 = (f32[2048]{0:T(1024)S(1)}, f32[2048]{0:T(1024)}, u32[]{:S(2)}) copy-start(f32[2048]{0:T(1024)} %param.15) | copy-start | bytes 24580
  170.2 208.3 %reduce-scatter.11.cloned.1.call-start = ((), (), s32[]{:S(2)}) async-start(), calls=%async_computation.7 | async-start | bytes 221184 | tf_op jit(solution)/shard_map/reduce_scatter | solution.py:75
  176.2 6.8 %collective-permute-start.5 = (f32[1,3,6,256]{3,2,1,0:T(8,128)S(1)}, f32[1,3,6,256]{3,2,1,0:T(8,128)S(1)}, u32[]{:S(2)}, u32[]{:S(2)}) collective-permute-start(f32[1,3,6,256]{3,2,1,0:T(8,128)S(1)} %reverse_bitcast_fusion.4), channel_id=1, source_target_pairs={{4,0},{8,4},{12,8},{5,1},{9,5},{13,9},{6,2},{10,6},{14,10},{7,3},{... | collective-permute-start | bytes 55304 | tf_op jit(solution)/shard_map/ppermute | solution.py:17
  178.4 5.7 %collective-permute-start.4 = (f32[1,3,6,256]{3,2,1,0:T(8,128)S(1)}, f32[1,3,6,256]{3,2,1,0:T(8,128)S(1)}, u32[]{:S(2)}, u32[]{:S(2)}) collective-permute-start(f32[1,3,6,256]{3,2,1,0:T(8,128)S(1)} %reverse_bitcast_fusion.5), channel_id=1, source_target_pairs={{0,4},{4,8},{8,12},{1,5},{5,9},{9,13},{2,6},{6,10},{10,14},{3,7},{... | collective-permute-start | bytes 55304 | tf_op jit(solution)/shard_map/ppermute | solution.py:14
  184.2 6.1 %collective-permute-start.7 = (f32[5,1,6,256]{3,1,2,0:T(1,128)S(1)}, f32[5,1,6,256]{3,1,2,0:T(1,128)S(1)}, u32[]{:S(2)}, u32[]{:S(2)}) collective-permute-start(f32[5,1,6,256]{3,1,2,0:T(1,128)S(1)} %copy.151), channel_id=1, source_target_pairs={{2,0},{3,1},{6,4},{7,5},{10,8},{11,9},{14,12},{15,13},{18,16},{19,... | collective-permute-start | bytes 92168 | tf_op jit(solution)/shard_map/ppermute | solution.py:17
  185.5 6.1 %collective-permute-start.6 = (f32[5,1,6,256]{3,1,2,0:T(1,128)S(1)}, f32[5,1,6,256]{3,1,2,0:T(1,128)S(1)}, u32[]{:S(2)}, u32[]{:S(2)}) collective-permute-start(f32[5,1,6,256]{3,1,2,0:T(1,128)S(1)} %copy.150), channel_id=1, source_target_pairs={{0,2},{1,3},{4,6},{5,7},{8,10},{9,11},{12,14},{13,15},{16,18},{17,... | collective-permute-start | bytes 92168 | tf_op jit(solution)/shard_map/ppermute | solution.py:14
  214.8 5.9 %collective-permute-start.8 = (f32[1,3,6,256]{3,2,1,0:T(8,128)S(1)}, f32[1,3,6,256]{3,2,1,0:T(8,128)S(1)}, u32[]{:S(2)}, u32[]{:S(2)}) collective-permute-start(f32[1,3,6,256]{3,2,1,0:T(8,128)S(1)} %get-tuple-element.26), channel_id=1, source_target_pairs={{0,4},{4,8},{8,12},{1,5},{5,9},{9,13},{2,6},{6,10},{10,14},{3,7},{... | collective-permute-start | bytes 55304 | tf_op jit(solution)/shard_map/ppermute | solution.py:14
  218.5 5.7 %collective-permute-start.9 = (f32[1,3,6,256]{3,2,1,0:T(8,128)S(1)}, f32[1,3,6,256]{3,2,1,0:T(8,128)S(1)}, u32[]{:S(2)}, u32[]{:S(2)}) collective-permute-start(f32[1,3,6,256]{3,2,1,0:T(8,128)S(1)} %get-tuple-element.27), channel_id=1, source_target_pairs={{4,0},{8,4},{12,8},{5,1},{9,5},{13,9},{6,2},{10,6},{14,10},{7,3},{... | collective-permute-start | bytes 55304 | tf_op jit(solution)/shard_map/ppermute | solution.py:17
  224.3 9.8 %collective-permute-start.11 = (f32[5,1,6,256]{3,1,2,0:T(1,128)S(1)}, f32[5,1,6,256]{3,1,2,0:T(1,128)S(1)}, u32[]{:S(2)}, u32[]{:S(2)}) collective-permute-start(f32[5,1,6,256]{3,1,2,0:T(1,128)S(1)} %copy.159), channel_id=1, source_target_pairs={{2,0},{3,1},{6,4},{7,5},{10,8},{11,9},{14,12},{15,13},{18,16},{19,... | collective-permute-start | bytes 92168 | tf_op jit(solution)/shard_map/ppermute | solution.py:17
  225.6 8.4 %collective-permute-start.10 = (f32[5,1,6,256]{3,1,2,0:T(1,128)S(1)}, f32[5,1,6,256]{3,1,2,0:T(1,128)S(1)}, u32[]{:S(2)}, u32[]{:S(2)}) collective-permute-start(f32[5,1,6,256]{3,1,2,0:T(1,128)S(1)} %copy.158), channel_id=1, source_target_pairs={{0,2},{1,3},{4,6},{5,7},{8,10},{9,11},{12,14},{13,15},{16,18},{17,... | collective-permute-start | bytes 92168 | tf_op jit(solution)/shard_map/ppermute | solution.py:14
  368.5 1.7 slice-start
  371.6 23.7 %reduce-scatter.9.cloned.1.call-start = ((), (), s32[]{:S(2)}) async-start(), calls=%async_computation.6 | async-start | bytes 3145728 | tf_op jit(solution)/shard_map/reduce_scatter | solution.py:74
  379.3 6.8 %collective-permute-start.13 = (f32[1,3,6,256]{3,2,1,0:T(8,128)S(1)}, f32[1,3,6,256]{3,2,1,0:T(8,128)S(1)}, u32[]{:S(2)}, u32[]{:S(2)}) collective-permute-start(f32[1,3,6,256]{3,2,1,0:T(8,128)S(1)} %reverse_bitcast_fusion.2), channel_id=1, source_target_pairs={{4,0},{8,4},{12,8},{5,1},{9,5},{13,9},{6,2},{10,6},{14,10},{7,3},{... | collective-permute-start | bytes 55304 | tf_op jit(solution)/shard_map/ppermute | solution.py:17
  381.6 5.7 %collective-permute-start.12 = (f32[1,3,6,256]{3,2,1,0:T(8,128)S(1)}, f32[1,3,6,256]{3,2,1,0:T(8,128)S(1)}, u32[]{:S(2)}, u32[]{:S(2)}) collective-permute-start(f32[1,3,6,256]{3,2,1,0:T(8,128)S(1)} %reverse_bitcast_fusion.3), channel_id=1, source_target_pairs={{0,4},{4,8},{8,12},{1,5},{5,9},{9,13},{2,6},{6,10},{10,14},{3,7},{... | collective-permute-start | bytes 55304 | tf_op jit(solution)/shard_map/ppermute | solution.py:14
  387.3 5.9 %collective-permute-start.15 = (f32[5,1,6,256]{3,1,2,0:T(1,128)S(1)}, f32[5,1,6,256]{3,1,2,0:T(1,128)S(1)}, u32[]{:S(2)}, u32[]{:S(2)}) collective-permute-start(f32[5,1,6,256]{3,1,2,0:T(1,128)S(1)} %copy.169), channel_id=1, source_target_pairs={{2,0},{3,1},{6,4},{7,5},{10,8},{11,9},{14,12},{15,13},{18,16},{19,... | collective-permute-start | bytes 92168 | tf_op jit(solution)/shard_map/ppermute | solution.py:17
  388.7 6.1 %collective-permute-start.14 = (f32[5,1,6,256]{3,1,2,0:T(1,128)S(1)}, f32[5,1,6,256]{3,1,2,0:T(1,128)S(1)}, u32[]{:S(2)}, u32[]{:S(2)}) collective-permute-start(f32[5,1,6,256]{3,1,2,0:T(1,128)S(1)} %copy.168), channel_id=1, source_target_pairs={{0,2},{1,3},{4,6},{5,7},{8,10},{9,11},{12,14},{13,15},{16,18},{17,... | collective-permute-start | bytes 92168 | tf_op jit(solution)/shard_map/ppermute | solution.py:14
Sparse Core Ops, SparseCore 0:
  167.2 8.2 reduce-scatter.6
  177.7 10.7 reduce-scatter.4
  371.7 6.8 reduce-scatter.10
  380.8 10.7 reduce-scatter.8
where the time goes:
time: 422 us; the launch traced here: 419 us
  other arithmetic  201 us (48%)
  local copies, waits for them, and re-layouts  126 us (30%)
  starting transfers between devices  47.1 us (11%)
  waiting for transfers between devices  21 us (5%)
  between operations  14.5 us (3%)
  blocking collectives  7.63 us (2%)
    scatter-add x2, other arithmetic, beam_forces(): return contrib.at[:, slot_pick.reshape(-1)].add(per_slot.reshape(6, -1))  125 us
    gather x2, local copies, waits for them, and re-layouts, beam_forces(): gathered = jnp.take(buffer, slot_pick, axis=1) * shape_pick[None]  87.2 us
    ppermute x8, starting transfers between devices, extended(): lax.ppermute(lax.slice_in_dim(block, block.shape[dim] - width, None, axis...  32.7 us
    scatter-add x2, other arithmetic, shards(): own_local.at[:, flat_list]  30.4 us
    mul x2, other arithmetic, beam_forces(): gathered = jnp.take(buffer, slot_pick, axis=1) * shape_pick[None]  21.8 us
    ppermute x8, starting transfers between devices, extended(): lax.ppermute(lax.slice_in_dim(block, 0, width, axis=dim), axis, backward)  14.2 us
    reduce_scatter x2, waiting for transfers between devices, shards(): lax.psum_scatter(near_part, 'sub', scatter_dimension=0, tiled=True)  9.03 us
    mul x2, other arithmetic, beam_forces(): per_slot = end_force[:, :, None, :] * scaled[None]  8.77 us
  transfers between devices with their start and end apart: 20, of which 8 were waited for; matrix products, arithmetic and copies ran while one was open for 3% of the time, Pallas kernels for 0%

commit v1 on v0

v1 whole, which is shorter than its diff:
```python
import functools

import jax
import jax.numpy as jnp
from jax import lax
from jax.experimental import pallas as pl
from jax.experimental.pallas import tpu as pltpu
from jax.sharding import PartitionSpec as P

STEPS = 2
F32 = jnp.float32
BF16 = jnp.bfloat16
VMEM = pl.BlockSpec(memory_space=pltpu.VMEM)


def lane_pick(row, lanes):
    return jnp.take_along_axis(row, lanes, axis=1, mode="promise_in_bounds")


def spread(row):
    return jnp.broadcast_to(row, (8, 128))


def pick_lists(field, picks_ref, outs):
    picks = [picks_ref[0:8, :], picks_ref[8:16, :]]
    lanes = [p & 127 for p in picks]
    rows = [lax.shift_right_logical(p, 7) for p in picks]
    found = [[jnp.zeros((8, 128), F32) for _ in range(2)] for _ in range(6)]
    for k in range(8):
        for half in range(2):
            hit = [r == 2 * k + half for r in rows]
            for c in range(6):
                row = spread(field[2 * c + half, k : k + 1, :])
                for v in range(2):
                    found[c][v] = jnp.where(hit[v], lane_pick(row, lanes[v]), found[c][v])
    for c in range(8):
        both = jnp.concatenate(found[c], axis=0) if c < 6 else jnp.zeros((16, 128), F32)
        at = 0
        for out in outs:
            size = out.shape[0]
            out[:, c, :] = both[at : at + size, :]
            at += size


def one_hot_matmul(acc_ref, a_ref, b_ref):
    return lax.dot_general(
        a_ref[...], b_ref[...], (((1,), (1,)), ((), ())), preferred_element_type=F32
    )


def split(value):
    high = value.astype(BF16).astype(F32)
    return high, value - high


def lists_kernel(field_ref, picks_ref, *outs):
    pick_lists(field_ref, picks_ref, outs)


def beam_kernel(
    n,
    field_ref,
    near_ref,
    other_ref,
    slots_ref,
    shape_ref,
    kind_ref,
    weight_ref,
    stiff_ref,
    own_ref,
    own_near_ref,
    send_ref,
    ends_ref,
    val_ref,
    a_ref,
    b_ref,
    acc_ref,
):
    def gather_end(at, carry):
        e, h = at // 2, at % 2
        slots = [slots_ref[3 * e + k, h] for k in range(3)]
        lanes = [s & 127 for s in slots]
        rows = [lax.shift_right_logical(s, 7) for s in slots]
        found = [[jnp.zeros((8, 128), F32) for _ in range(3)] for _ in range(6)]
        tables = []
        for rel in range(8):
            for half in range(2):
                tables.append((rel, half, lambda c, k=rel, h2=half: field_ref[2 * c + h2, k : k + 1, :]))
                tables.append((8 + rel, half, lambda c, k=rel, h2=half: other_ref[2 * c + h2, k : k + 1, :]))
        for d in range(n):
            for half in range(2):
                tables.append((16 + d, half, lambda c, k=2 * d + half: near_ref[k, c : c + 1, :]))
                tables.append((24 + d, half, lambda c, k=2 * d + half: other_ref[12 + k, c : c + 1, :]))
        for rel, half, load in tables:
            hit = [r == 2 * rel + half for r in rows]
            for c in range(6):
                row = spread(load(c))
                for k in range(3):
                    found[c][k] = jnp.where(hit[k], lane_pick(row, lanes[k]), found[c][k])
        shapes = [shape_ref[3 * e + k, h] for k in range(3)]
        for c in range(6):
            ends_ref[h, e * 6 + c] = sum(found[c][k] * shapes[k] for k in range(3))
        return carry

    lax.fori_loop(0, 4, gather_end, 0)

    def forces(h, carry):
        kind = kind_ref[h]
        weight = weight_ref[h]
        vec = [ends_ref[h, j] for j in range(12)]
        for e in range(2):
            scaled = [shape_ref[3 * e + k, h] * weight for k in range(3)]
            for i in range(6):
                total = jnp.zeros((8, 128), F32)
                for j in range(12):
                    at = (6 * e + i) * 12 + j
                    total += lane_pick(spread(stiff_ref[at : at + 1, :]), kind) * vec[j]
                for k in range(3):
                    high, low = split(scaled[k] * total)
                    val_ref[3 * e + k, 0, i, h] = high
                    val_ref[3 * e + k, 1, i, h] = low
        return carry

    lax.fori_loop(0, 2, forces, 0)

    acc_ref[...] = jnp.zeros_like(acc_ref)
    iota_hi = lax.broadcasted_iota(jnp.int32, (32, 128), 0)
    iota_lo = lax.broadcasted_iota(jnp.int32, (256, 128), 0)

    def scatter(j, carry):
        for h in range(2):
            for q in range(8):
                slot = slots_ref[j, h, q : q + 1, :]
                hit = iota_hi == lax.shift_right_logical(slot, 8)
                at = (8 * h + q) * 128
                for part in range(2):
                    for c in range(6):
                        row = val_ref[j, part, c, h, q : q + 1, :]
                        a_ref[part * 192 + c * 32 : part * 192 + (c + 1) * 32, at : at + 128] = jnp.where(
                            hit, jnp.broadcast_to(row, (32, 128)), 0.0
                        ).astype(BF16)
                b_ref[:, at : at + 128] = jnp.where(iota_lo == (slot & 255), 1.0, 0.0).astype(BF16)
        acc_ref[...] += one_hot_matmul(acc_ref, a_ref, b_ref)
        return carry

    lax.fori_loop(0, 6, scatter, 0)
    for c in range(6):
        total = acc_ref[c * 32 : (c + 1) * 32, :] + acc_ref[192 + c * 32 : 192 + (c + 1) * 32, :]
        for half in range(2):
            part = total[:, half * 128 : (half + 1) * 128]
            own_ref[2 * c + half] = part[0:8]
            send_ref[2 * c + half] = part[8:16]
            for d in range(n):
                own_near_ref[2 * d + half, c : c + 1, :] = part[16 + d : 17 + d]
                send_ref[12 + 2 * d + half, c : c + 1, :] = part[24 + d : 25 + d]
    for k in range(2 * n):
        own_near_ref[k, 6:8, :] = jnp.zeros((2, 128), F32)
        send_ref[12 + k, 6:8, :] = jnp.zeros((2, 128), F32)


def update_kernel(
    n_returns,
    last,
    own_ref,
    recv_ref,
    field_ref,
    velocity_ref,
    mass_ref,
    picks_ref,
    *refs,
):
    returns, refs = refs[:n_returns], refs[n_returns:]
    new_field_ref, new_velocity_ref = refs[0], refs[1]
    a_ref, b_ref = refs[-2], refs[-1]
    outs = refs[2:-2]
    iota_hi = lax.broadcasted_iota(jnp.int32, (8, 128), 0)
    iota_lo = lax.broadcasted_iota(jnp.int32, (256, 128), 0)
    p = 0
    for ret in returns:
        for k in range(ret.shape[0]):
            pick = picks_ref[p : p + 1, :]
            hit = iota_hi == lax.shift_right_logical(pick, 8)
            at = p * 128
            value = ret[k]
            parts = [[], []]
            for part, piece in enumerate(split(value)):
                for c in range(6):
                    parts[part].append(jnp.where(hit, spread(piece[c : c + 1, :]), 0.0))
            a_ref[:, at : at + 128] = jnp.concatenate(parts[0] + parts[1], axis=0).astype(BF16)
            b_ref[:, at : at + 128] = jnp.where(iota_lo == (pick & 255), 1.0, 0.0).astype(BF16)
            p += 1
    back = one_hot_matmul(None, a_ref, b_ref)
    back = back[:48] + back[48:]
    for c in range(6):
        for half in range(2):
            at = 2 * c + half
            force = (
                own_ref[at] + recv_ref[at] + back[c * 8 : (c + 1) * 8, half * 128 : (half + 1) * 128]
            )
            velocity = 0.98 * velocity_ref[at] - 0.2 * force / mass_ref[half]
            new_velocity_ref[at] = velocity
            new_field_ref[at] = field_ref[at] + 0.2 * velocity
    if not last:
        pick_lists(new_field_ref, picks_ref, outs)


def pairs(count, shift):
    out = []
    for i in range(shift, count - 1, 2):
        out += [(i, i + 1), (i + 1, i)]
    return out


def f32_out(*shape):
    return jax.ShapeDtypeStruct(shape, F32)


def params():
    return pltpu.CompilerParams(vmem_limit_bytes=48 * 1024 * 1024)


def shards(
    displace,
    velocity,
    nodal_mass,
    send_list,
    beam_slots,
    shape_values,
    beam_kind,
    cluster_weight,
    stiffness,
):
    list_len = send_list.shape[2]
    cols = lax.axis_size("cols")
    U = 2 if cols <= 2 else 3
    n = 3 * U - 1
    kinds = stiffness.shape[0]
    r_odd = lax.axis_index("rows") % 2
    c_odd = lax.axis_index("cols") % 2
    s = lax.axis_index("sub")
    row_perm = [pairs(lax.axis_size("rows"), 0), pairs(lax.axis_size("rows"), 1)]
    col_perm = [pairs(cols, 0), pairs(cols, 1)][: U - 1]
    sub_perm = [(0, 1), (1, 0)]

    def blocked(x):
        return x.reshape(6, 8, 2, 128).transpose(0, 2, 1, 3).reshape(12, 8, 128)

    def flat(x):
        return x.reshape(6, 2, 8, 128).transpose(0, 2, 1, 3).reshape(6, 2048)

    row_order = jnp.where(r_odd == 0, send_list[::-1], send_list)
    ordered = jnp.where(c_odd == 0, row_order[:, ::-1], row_order)
    rows_of = [ordered[0], ordered[2], ordered[1]]
    col_at = [1, 0, 2][:U]
    picks = [rows_of[t][u] for t in range(2) for u in col_at] + [rows_of[2][u] for u in col_at[1:]]
    picks = jnp.stack(picks).reshape(2 * n, 128)
    if 2 * n < 16:
        picks = jnp.concatenate([picks, jnp.zeros((16 - 2 * n, 128), jnp.int32)], axis=0)

    slots = beam_slots.reshape(6, 2, 8, 128)
    hi = slots >> 8
    remote = hi - 16
    sender = (remote >= 9).astype(jnp.int32)
    direction = remote - 9 * sender
    a = (direction >= 3).astype(jnp.int32) + (direction >= 6).astype(jnp.int32)
    b = direction - 3 * a
    a = jnp.where(r_odd == 0, a, 2 - a)
    b = jnp.where(c_odd == 0, b, 2 - b)
    t = jnp.where(a == 1, 2, a >> 1)
    u = jnp.where(b == 1, 0, (b >> 1) + 1)
    order = jnp.where(t == 2, 2 * U + u - 1, t * U + u)
    rel_near = 16 + 8 * (sender ^ s) + order
    rel_near = jnp.where(u < U, rel_near, 64)
    rel = jnp.where(hi < 16, hi ^ (8 * s), rel_near)
    slots = rel * 256 + (slots & 255)

    shapes = shape_values.reshape(6, 2, 8, 128)
    kind = beam_kind.reshape(2, 8, 128)
    weight = cluster_weight.reshape(2, 8, 128)
    stiff = jnp.pad(stiffness.reshape(kinds, 144).T, ((0, 0), (0, 128 - kinds)))
    mass = nodal_mass.reshape(8, 2, 128).transpose(1, 0, 2)

    field = blocked(displace)
    speed = blocked(velocity)
    list_outs = [f32_out(2 * U, 8, 128), f32_out(2 * U, 8, 128), f32_out(2 * U - 2, 8, 128)]
    outgoing = pl.pallas_call(
        lists_kernel,
        out_shape=list_outs,
        in_specs=[VMEM] * 2,
        out_specs=[VMEM] * 3,
        compiler_params=params(),
    )(field, picks)
    for step in range(STEPS):
        to_rows, own_row = outgoing[:2], outgoing[2]
        arrived = [lax.ppermute(x, "rows", perm) for x, perm in zip(to_rows, row_perm)]
        near = [[x[0:2]] for x in arrived] + [[]]
        for u in range(1, U):
            at = 2 * u
            message = jnp.concatenate(
                [arrived[0][at : at + 2], arrived[1][at : at + 2], own_row[at - 2 : at]], axis=0
            )
            got = lax.ppermute(message, "cols", col_perm[u - 1])
            for t in range(3):
                near[t].append(got[2 * t : 2 * t + 2])
        near = jnp.concatenate(near[0] + near[1] + near[2], axis=0)
        other = lax.ppermute(jnp.concatenate([field, near], axis=0), "sub", sub_perm)
        own, own_near, send = pl.pallas_call(
            functools.partial(beam_kernel, n),
            out_shape=[f32_out(12, 8, 128), f32_out(2 * n, 8, 128), f32_out(12 + 2 * n, 8, 128)],
            in_specs=[VMEM] * 8,
            out_specs=[VMEM] * 3,
            scratch_shapes=[
                pltpu.VMEM((2, 12, 8, 128), F32),
                pltpu.VMEM((6, 2, 6, 2, 8, 128), F32),
                pltpu.VMEM((384, 2048), BF16),
                pltpu.VMEM((256, 2048), BF16),
                pltpu.VMEM((384, 256), F32),
            ],
            compiler_params=params(),
        )(field, near, other, slots, shapes, kind, weight, stiff)
        recv = lax.ppermute(send, "sub", sub_perm)
        total = own_near + recv[12:]

        def listed(t, u):
            at = 2 * (t * U + u) if t < 2 else 2 * (2 * U + u - 1)
            return total[at : at + 2]

        back_rows = [[listed(0, 0)], [listed(1, 0)]]
        back_own = []
        for u in range(1, U):
            message = jnp.concatenate([listed(t, u) for t in range(3)], axis=0)
            got = lax.ppermute(message, "cols", col_perm[u - 1])
            back_rows[0].append(got[0:2])
            back_rows[1].append(got[2:4])
            back_own.append(got[4:6])
        returns = [
            lax.ppermute(jnp.concatenate(x, axis=0), "rows", perm)
            for x, perm in zip(back_rows, row_perm)
        ] + [jnp.concatenate(back_own, axis=0)]
        last = step == STEPS - 1
        outs = pl.pallas_call(
            functools.partial(update_kernel, 3, last),
            out_shape=[f32_out(12, 8, 128)] * 2 + ([] if last else list_outs),
            in_specs=[VMEM] * 9,
            out_specs=[VMEM] * (2 if last else 5),
            scratch_shapes=[pltpu.VMEM((96, 256 * n), BF16), pltpu.VMEM((256, 256 * n), BF16)],
            compiler_params=params(),
        )(own, recv, field, speed, mass, picks, *returns)
        field, speed = outs[:2]
        outgoing = outs[2:]
    return flat(field), flat(speed)


def solution(mesh):
    whole = ("groups", "rows", "cols", "sub")
    in_specs = (
        P(None, whole),
        P(None, whole),
        P(whole),
        P("rows", "cols", ("groups", "sub")),
        P(None, whole),
        P(None, whole),
        P(whole),
        P(whole),
        P(),
    )
    out_specs = (P(None, whole), P(None, whole))
    return jax.shard_map(shards, mesh=mesh, in_specs=in_specs, out_specs=out_specs, check_vma=False)
```

time: 422 us -> 88.1 us (0.21)
  other arithmetic: 201 us -> 0.18 us
  local copies, waits for them, and re-layouts: 126 us -> 7.9 us
  Pallas kernels: 0 us -> 33.1 us
  starting transfers between devices: 47.1 us -> 19.7 us
  between operations: 14.5 us -> 1.09 us
  blocking collectives: 7.63 us -> 0 us
    scatter-add x4 -> x0, other arithmetic: 155 us -> none  [the longest x2 125 us: beam_forces(): return contrib.at[:, slot_pick.reshape(-1)].add(per_slot.reshape(6, -1))]
    gather x4 -> x0, local copies, waits for them, and re-layouts: 95 us -> none  [the longest x2 87.2 us: beam_forces(): gathered = jnp.take(buffer, slot_pick, axis=1) * shape_pick[None]]
    pallas_call x0 -> x5, Pallas kernels: none -> 33.1 us  [the longest x2 31.7 us: shards(): pl.pallas_call(functools.partial(beam_kernel, n), out_shape=[f32_out(12,...]
    mul x5 -> x0, other arithmetic: 30.6 us -> none  [the longest x2 21.8 us: beam_forces(): gathered = jnp.take(buffer, slot_pick, axis=1) * shape_pick[None]]
    ppermute x16, starting transfers between devices: 46.9 us -> 19.7 us  [the longest x4 7.1 us: shards(): lax.ppermute(x, 'rows', perm)]
    ppermute x16, waiting for transfers between devices: 11.9 us -> 24.5 us  [the longest x4 7.65 us: shards(): got = lax.ppermute(message, 'cols', col_perm[u - 1])]
    slice x26 -> x11, local copies, waits for them, and re-layouts: 11.3 us -> 1.41 us  [the longest x4 1.38 us: shards(): arrived[1][at:at + 2]]
    reduce_scatter x4 -> x0, waiting for transfers between devices: 9.07 us -> none  [the longest x2 9.03 us: shards(): lax.psum_scatter(near_part, 'sub', scatter_dimension=0, tiled=True)]
  transfers between devices with their start and end apart: 20 -> 16, of which waited for: 8 -> 14; matrix products, arithmetic and copies ran while one was open for 3% -> 0% of each run, Pallas kernels for 0% -> 0%
where the time goes in v1:
time: 88.1 us; the launch traced here: 86.5 us
  Pallas kernels  33.1 us (38%)
  waiting for transfers between devices  24.5 us (28%)
  starting transfers between devices  19.7 us (22%)
  local copies, waits for them, and re-layouts  7.9 us (9%)
  between operations  1.09 us (1%)
    pallas_call x2, Pallas kernels, shards(): pl.pallas_call(functools.partial(beam_kernel, n), out_shape=[f32_out(12,...  31.7 us
    ppermute x4, waiting for transfers between devices, shards(): got = lax.ppermute(message, 'cols', col_perm[u - 1])  7.65 us
    ppermute x4, starting transfers between devices, shards(): lax.ppermute(x, 'rows', perm)  7.1 us
    ppermute x4, waiting for transfers between devices, shards(): lax.ppermute(jnp.concatenate(x, axis=0), 'rows', perm)  6.78 us
    ppermute x4, starting transfers between devices, shards(): got = lax.ppermute(message, 'cols', col_perm[u - 1])  6.09 us
    ppermute x4, starting transfers between devices, shards(): lax.ppermute(jnp.concatenate(x, axis=0), 'rows', perm)  5.99 us
    ppermute x4, waiting for transfers between devices, shards(): lax.ppermute(x, 'rows', perm)  5.32 us
    unnamed x36, local copies, waits for them, and re-layouts  4.67 us
  transfers between devices with their start and end apart: 16, of which 14 were waited for; matrix products, arithmetic and copies ran while one was open for 0% of the time, Pallas kernels for 0%

profile of v1, /device:TPU:8, one launch (start us, length us, event | category | flops | bytes accessed | tf_op | source)
XLA Modules:
  0.0 86.5 jit_solution(15637358676515920487)
XLA Ops:
  0.6 0.0 copy-start.7
  0.7 0.7 copy-done.7
  1.4 0.1 rev.7
  1.5 0.7 copy-done.3
  2.2 0.0 copy-start.2
  2.3 0.3 shard_map.104
  2.6 0.1 collective-permute-start
  2.6 5.0 %collective-permute-start.1 = (f32[4,8,128]{2,1,0:T(8,128)S(1)}, f32[4,8,128]{2,1,0:T(8,128)S(1)}, u32[]{:S(2)}, u32[]{:S(2)}) collective-permute-start(f32[4,8,128]{2,1,0:T(8,128)S(1)} %get-tuple-element.19), channel_id=1, source_target_pairs={{4,8},{8,4},{5,9},{9,5},{6,10},{10,6},{7,11},{11,7},{20,24},{24,20... | collective-permute-start | bytes 49160 | tf_op jit(solution)/shard_map/ppermute | solution.py:295
  7.7 0.0 copy-done.2
  7.8 1.6 %collective-permute-done.1 = f32[4,8,128]{2,1,0:T(8,128)S(1)} collective-permute-done((f32[4,8,128]{2,1,0:T(8,128)S(1)}, f32[4,8,128]{2,1,0:T(8,128)S(1)}, u32[]{:S(2)}, u32[]{:S(2)}) %collective-permute-start.1) | collective-permute-done | bytes 16416 | tf_op jit(solution)/shard_map/ppermute | solution.py:295
  9.4 0.6 copy-done.8
  10.0 0.0 collective-permute-done
  10.0 0.7 slice-done
  10.7 1.5 %collective-permute-start.2 = (f32[6,8,128]{2,1,0:T(8,128)S(1)}, f32[6,8,128]{2,1,0:T(8,128)S(1)}, u32[]{:S(2)}, u32[]{:S(2)}) collective-permute-start(f32[6,8,128]{2,1,0:T(8,128)S(1)} %pad_maximum_fusion.2), channel_id=1, source_target_pairs={{0,2},{2,0},{1,3},{3,1},{4,6},{6,4},{5,7},{7,5},{8,10},{10,8},{9,1... | collective-permute-start | bytes 73736 | tf_op jit(solution)/shard_map/ppermute | solution.py:302
  12.2 0.1 bitcast_add_fusion.slots_ref
  12.3 0.7 copy-done.6
  13.0 0.0 copy-start.4
  13.0 0.1 reshape.68
  13.1 0.1 copy.18
  13.2 0.6 copy-done.4
  13.9 0.0 copy-start.9
  13.9 0.6 collective-permute-done.2
  14.5 0.1 copy-done.9
  14.6 0.0 collective-permute-start.3
  14.6 0.0 copy-start
  14.6 0.0 copy-start.1
  14.7 1.2 %collective-permute-done.3.other_ref = f32[22,8,128]{2,1,0:T(8,128)S(1)} collective-permute-done((f32[22,8,128]{2,1,0:T(8,128)S(1)}, f32[22,8,128]{2,1,0:T(8,128)S(1)}, u32[]{:S(2)}, u32[]{:S(2)}) %collective-permute-start.3) | collective-permute-done | bytes 90144 | tf_op jit(solution)/shard_map/ppermute | solution.py:306
  15.9 0.0 copy-done
  15.9 0.0 copy-done.1
  15.9 15.8 %shard_map.105 = (f32[12,8,128]{2,1,0:T(8,128)S(1)}, f32[10,8,128]{2,1,0:T(8,128)S(1)}, f32[22,8,128]{2,1,0:T(8,128)S(1)}) custom-call(f32[12,8,128]{2,1,0:T(8,128)S(1)} %bitcast.65, f32[10,8,128]{2,1,0:T(8,128)S(1)} %pad_maximum_fusion.near_ref, f32[22,8,128]{2,1,0:T(8,128)S(1)} %collective-permute-done.3.other_ref, ...), custom_call_target="tpu_custom_call" | custom-call | tf_op jit(solution)/shard_map/pallas_call | solution.py:307
  31.8 0.2 collective-permute-start.4
  32.0 1.1 %collective-permute-done.4.recv_ref = f32[22,8,128]{2,1,0:T(8,128)S(1)} collective-permute-done((f32[22,8,128]{2,1,0:T(8,128)S(1)}, f32[22,8,128]{2,1,0:T(8,128)S(1)}, u32[]{:S(2)}, u32[]{:S(2)}) %collective-permute-start.4) | collective-permute-done | bytes 90144 | tf_op jit(solution)/shard_map/ppermute | solution.py:321
  33.2 0.0 copy-start.5
  33.2 1.6 %collective-permute-start.5 = (f32[6,8,128]{2,1,0:T(8,128)S(1)}, f32[6,8,128]{2,1,0:T(8,128)S(1)}, u32[]{:S(2)}, u32[]{:S(2)}) collective-permute-start(f32[6,8,128]{2,1,0:T(8,128)S(1)} %pad_maximum_fusion.3), channel_id=1, source_target_pairs={{0,2},{2,0},{1,3},{3,1},{4,6},{6,4},{5,7},{7,5},{8,10},{10,8},{9,1... | collective-permute-start | bytes 73736 | tf_op jit(solution)/shard_map/ppermute | solution.py:332
  34.7 2.3 %collective-permute-done.5 = f32[6,8,128]{2,1,0:T(8,128)S(1)} collective-permute-done((f32[6,8,128]{2,1,0:T(8,128)S(1)}, f32[6,8,128]{2,1,0:T(8,128)S(1)}, u32[]{:S(2)}, u32[]{:S(2)}) %collective-permute-start.5) | collective-permute-done | bytes 24608 | tf_op jit(solution)/shard_map/ppermute | solution.py:332
  37.1 3.9 %collective-permute-start.7 = (f32[4,8,128]{2,1,0:T(8,128)S(1)}, f32[4,8,128]{2,1,0:T(8,128)S(1)}, u32[]{:S(2)}, u32[]{:S(2)}) collective-permute-start(f32[4,8,128]{2,1,0:T(8,128)S(1)} %pad_maximum_fusion.7), channel_id=1, source_target_pairs={{4,8},{8,4},{5,9},{9,5},{6,10},{10,6},{7,11},{11,7},{20,24},{24,20... | collective-permute-start | bytes 49160 | tf_op jit(solution)/shard_map/ppermute | solution.py:337
  41.0 0.0 copy-start.12
  41.0 0.1 collective-permute-start.6
  41.1 0.6 copy-done.12
  41.8 0.9 %collective-permute-done.7.refs_1_ = f32[4,8,128]{2,1,0:T(8,128)S(1)} collective-permute-done((f32[4,8,128]{2,1,0:T(8,128)S(1)}, f32[4,8,128]{2,1,0:T(8,128)S(1)}, u32[]{:S(2)}, u32[]{:S(2)}) %collective-permute-start.7) | collective-permute-done | bytes 16416 | tf_op jit(solution)/shard_map/ppermute | solution.py:337
  42.7 2.1 %collective-permute-done.6.refs_0_ = f32[4,8,128]{2,1,0:T(8,128)S(1)} collective-permute-done((f32[4,8,128]{2,1,0:T(8,128)S(1)}, f32[4,8,128]{2,1,0:T(8,128)S(1)}, u32[]{:S(2)}, u32[]{:S(2)}) %collective-permute-start.6) | collective-permute-done | bytes 16416 | tf_op jit(solution)/shard_map/ppermute | solution.py:337
  44.8 0.7 shard_map.106
  45.5 0.1 collective-permute-start.8
  45.6 1.9 %collective-permute-start.9 = (f32[4,8,128]{2,1,0:T(8,128)S(1)}, f32[4,8,128]{2,1,0:T(8,128)S(1)}, u32[]{:S(2)}, u32[]{:S(2)}) collective-permute-start(f32[4,8,128]{2,1,0:T(8,128)S(1)} %get-tuple-element.26), channel_id=1, source_target_pairs={{4,8},{8,4},{5,9},{9,5},{6,10},{10,6},{7,11},{11,7},{20,24},{24,20... | collective-permute-start | bytes 49160 | tf_op jit(solution)/shard_map/ppermute | solution.py:295
  47.6 3.7 %collective-permute-done.9 = f32[4,8,128]{2,1,0:T(8,128)S(1)} collective-permute-done((f32[4,8,128]{2,1,0:T(8,128)S(1)}, f32[4,8,128]{2,1,0:T(8,128)S(1)}, u32[]{:S(2)}, u32[]{:S(2)}) %collective-permute-start.9) | collective-permute-done | bytes 16416 | tf_op jit(solution)/shard_map/ppermute | solution.py:295
  51.3 0.6 copy-done.10
  51.9 0.0 collective-permute-done.8
  51.9 0.7 slice-done.1
  52.6 1.5 %collective-permute-start.10 = (f32[6,8,128]{2,1,0:T(8,128)S(1)}, f32[6,8,128]{2,1,0:T(8,128)S(1)}, u32[]{:S(2)}, u32[]{:S(2)}) collective-permute-start(f32[6,8,128]{2,1,0:T(8,128)S(1)} %pad_maximum_fusion.4), channel_id=1, source_target_pairs={{0,2},{2,0},{1,3},{3,1},{4,6},{6,4},{5,7},{7,5},{8,10},{10,8},{9,1... | collective-permute-start | bytes 73736 | tf_op jit(solution)/shard_map/ppermute | solution.py:302
  54.0 2.3 %collective-permute-done.10 = f32[6,8,128]{2,1,0:T(8,128)S(1)} collective-permute-done((f32[6,8,128]{2,1,0:T(8,128)S(1)}, f32[6,8,128]{2,1,0:T(8,128)S(1)}, u32[]{:S(2)}, u32[]{:S(2)}) %collective-permute-start.10) | collective-permute-done | bytes 24608 | tf_op jit(solution)/shard_map/ppermute | solution.py:302
  56.4 0.1 collective-permute-start.11
  56.5 1.3 %collective-permute-done.11.other_ref = f32[22,8,128]{2,1,0:T(8,128)S(1)} collective-permute-done((f32[22,8,128]{2,1,0:T(8,128)S(1)}, f32[22,8,128]{2,1,0:T(8,128)S(1)}, u32[]{:S(2)}, u32[]{:S(2)}) %collective-permute-start.11) | collective-permute-done | bytes 90144 | tf_op jit(solution)/shard_map/ppermute | solution.py:306
  57.8 15.9 %shard_map.107 = (f32[12,8,128]{2,1,0:T(8,128)S(1)}, f32[10,8,128]{2,1,0:T(8,128)S(1)}, f32[22,8,128]{2,1,0:T(8,128)S(1)}) custom-call(f32[12,8,128]{2,1,0:T(8,128)S(1)} %get-tuple-element.24.field_ref, f32[10,8,128]{2,1,0:T(8,128)S(1)} %pad_maximum_fusion.1.near_ref, f32[22,8,128]{2,1,0:T(8,128)S(1)} %collective-permute-done.11.other_ref, ...), custom_call_target="tpu_custom_call" | custom-call | tf_op jit(solution)/shard_map/pallas_call | solution.py:307
  73.7 0.2 collective-permute-start.12
  73.9 1.1 %collective-permute-done.12.recv_ref = f32[22,8,128]{2,1,0:T(8,128)S(1)} collective-permute-done((f32[22,8,128]{2,1,0:T(8,128)S(1)}, f32[22,8,128]{2,1,0:T(8,128)S(1)}, u32[]{:S(2)}, u32[]{:S(2)}) %collective-permute-start.12) | collective-permute-done | bytes 90144 | tf_op jit(solution)/shard_map/ppermute | solution.py:321
  75.0 1.5 %collective-permute-start.13 = (f32[6,8,128]{2,1,0:T(8,128)S(1)}, f32[6,8,128]{2,1,0:T(8,128)S(1)}, u32[]{:S(2)}, u32[]{:S(2)}) collective-permute-start(f32[6,8,128]{2,1,0:T(8,128)S(1)} %pad_maximum_fusion.5), channel_id=1, source_target_pairs={{0,2},{2,0},{1,3},{3,1},{4,6},{6,4},{5,7},{7,5},{8,10},{10,8},{9,1... | collective-permute-start | bytes 73736 | tf_op jit(solution)/shard_map/ppermute | solution.py:332
  76.6 2.3 %collective-permute-done.13 = f32[6,8,128]{2,1,0:T(8,128)S(1)} collective-permute-done((f32[6,8,128]{2,1,0:T(8,128)S(1)}, f32[6,8,128]{2,1,0:T(8,128)S(1)}, u32[]{:S(2)}, u32[]{:S(2)}) %collective-permute-start.13) | collective-permute-done | bytes 24608 | tf_op jit(solution)/shard_map/ppermute | solution.py:332
  78.9 1.9 %collective-permute-start.15 = (f32[4,8,128]{2,1,0:T(8,128)S(1)}, f32[4,8,128]{2,1,0:T(8,128)S(1)}, u32[]{:S(2)}, u32[]{:S(2)}) collective-permute-start(f32[4,8,128]{2,1,0:T(8,128)S(1)} %pad_maximum_fusion.9), channel_id=1, source_target_pairs={{4,8},{8,4},{5,9},{9,5},{6,10},{10,6},{7,11},{11,7},{20,24},{24,20... | collective-permute-start | bytes 49160 | tf_op jit(solution)/shard_map/ppermute | solution.py:337
  80.9 0.1 collective-permute-start.14
  81.0 3.6 %collective-permute-done.15.refs_1_ = f32[4,8,128]{2,1,0:T(8,128)S(1)} collective-permute-done((f32[4,8,128]{2,1,0:T(8,128)S(1)}, f32[4,8,128]{2,1,0:T(8,128)S(1)}, u32[]{:S(2)}, u32[]{:S(2)}) %collective-permute-start.15) | collective-permute-done | bytes 16416 | tf_op jit(solution)/shard_map/ppermute | solution.py:337
  84.6 0.1 collective-permute-done.14.refs_0_
  84.7 0.4 shard_map.108
  85.1 0.7 reshape.73
  85.8 0.7 reshape.75
  (55 shorter events, 0.4 us)
Async XLA Ops:
  0.6 0.7 copy-start.7
  1.4 0.8 copy-start.3
  2.2 5.4 %copy-start.2 = (s32[6,2048]{1,0:T(8,128)S(1)}, s32[6,2048]{1,0:T(8,128)}, u32[]{:S(2)}) copy-start(s32[6,2048]{1,0:T(8,128)} %param.13) | copy-start | bytes 147460
  2.6 7.4 %collective-permute-start = (f32[4,8,128]{2,1,0:T(8,128)S(1)}, f32[4,8,128]{2,1,0:T(8,128)S(1)}, u32[]{:S(2)}, u32[]{:S(2)}) collective-permute-start(f32[4,8,128]{2,1,0:T(8,128)S(1)} %get-tuple-element.18), channel_id=1, source_target_pairs={{0,4},{4,0},{8,12},{12,8},{1,5},{5,1},{9,13},{13,9},{2,6},{6,2},{1... | collective-permute-start | bytes 49160 | tf_op jit(solution)/shard_map/ppermute | solution.py:295
  2.6 6.7 %collective-permute-start.1 = (f32[4,8,128]{2,1,0:T(8,128)S(1)}, f32[4,8,128]{2,1,0:T(8,128)S(1)}, u32[]{:S(2)}, u32[]{:S(2)}) collective-permute-start(f32[4,8,128]{2,1,0:T(8,128)S(1)} %get-tuple-element.19), channel_id=1, source_target_pairs={{4,8},{8,4},{5,9},{9,5},{6,10},{10,6},{7,11},{11,7},{20,24},{24,20... | collective-permute-start | bytes 49160 | tf_op jit(solution)/shard_map/ppermute | solution.py:295
  9.4 0.6 copy-start.8
  10.0 0.7 slice-start
  10.7 3.8 %collective-permute-start.2 = (f32[6,8,128]{2,1,0:T(8,128)S(1)}, f32[6,8,128]{2,1,0:T(8,128)S(1)}, u32[]{:S(2)}, u32[]{:S(2)}) collective-permute-start(f32[6,8,128]{2,1,0:T(8,128)S(1)} %pad_maximum_fusion.2), channel_id=1, source_target_pairs={{0,2},{2,0},{1,3},{3,1},{4,6},{6,4},{5,7},{7,5},{8,10},{10,8},{9,1... | collective-permute-start | bytes 73736 | tf_op jit(solution)/shard_map/ppermute | solution.py:302
  12.2 0.8 copy-start.6
  13.0 0.8 copy-start.4
  13.9 0.7 copy-start.9
  14.6 1.3 %collective-permute-start.3 = (f32[22,8,128]{2,1,0:T(8,128)S(1)}, f32[22,8,128]{2,1,0:T(8,128)S(1)}, u32[]{:S(2)}, u32[]{:S(2)}) collective-permute-start(f32[22,8,128]{2,1,0:T(8,128)S(1)} %get-tuple-element.53), channel_id=1, source_target_pairs={{0,1},{1,0},{2,3},{3,2},{4,5},{5,4},{6,7},{7,6},{8,9},{9,8},{10,11... | collective-permute-start | bytes 270344 | tf_op jit(solution)/shard_map/ppermute | solution.py:306
  14.6 1.3 %copy-start = (s32[2048]{0:T(1024)S(1)}, s32[2048]{0:T(1024)}, u32[]{:S(2)}) copy-start(s32[2048]{0:T(1024)} %param.15) | copy-start | bytes 24580
  14.6 1.3 %copy-start.1 = (f32[2048]{0:T(1024)S(1)}, f32[2048]{0:T(1024)}, u32[]{:S(2)}) copy-start(f32[2048]{0:T(1024)} %param.16) | copy-start | bytes 24580
  31.8 1.4 %collective-permute-start.4 = (f32[22,8,128]{2,1,0:T(8,128)S(1)}, f32[22,8,128]{2,1,0:T(8,128)S(1)}, u32[]{:S(2)}, u32[]{:S(2)}) collective-permute-start(f32[22,8,128]{2,1,0:T(8,128)S(1)} %get-tuple-element.22), channel_id=1, source_target_pairs={{0,1},{1,0},{2,3},{3,2},{4,5},{5,4},{6,7},{7,6},{8,9},{9,8},{10,11... | collective-permute-start | bytes 270344 | tf_op jit(solution)/shard_map/ppermute | solution.py:321
  33.2 8.6 %copy-start.5 = (f32[6,2048]{1,0:T(8,128)S(1)}, f32[6,2048]{1,0:T(8,128)}, u32[]{:S(2)}) copy-start(f32[6,2048]{1,0:T(8,128)} %param.10) | copy-start | bytes 147460
  33.2 3.9 %collective-permute-start.5 = (f32[6,8,128]{2,1,0:T(8,128)S(1)}, f32[6,8,128]{2,1,0:T(8,128)S(1)}, u32[]{:S(2)}, u32[]{:S(2)}) collective-permute-start(f32[6,8,128]{2,1,0:T(8,128)S(1)} %pad_maximum_fusion.3), channel_id=1, source_target_pairs={{0,2},{2,0},{1,3},{3,1},{4,6},{6,4},{5,7},{7,5},{8,10},{10,8},{9,1... | collective-permute-start | bytes 73736 | tf_op jit(solution)/shard_map/ppermute | solution.py:332
  37.1 5.6 %collective-permute-start.7 = (f32[4,8,128]{2,1,0:T(8,128)S(1)}, f32[4,8,128]{2,1,0:T(8,128)S(1)}, u32[]{:S(2)}, u32[]{:S(2)}) collective-permute-start(f32[4,8,128]{2,1,0:T(8,128)S(1)} %pad_maximum_fusion.7), channel_id=1, source_target_pairs={{4,8},{8,4},{5,9},{9,5},{6,10},{10,6},{7,11},{11,7},{20,24},{24,20... | collective-permute-start | bytes 49160 | tf_op jit(solution)/shard_map/ppermute | solution.py:337
  41.0 0.7 copy-start.12
  41.0 3.8 %collective-permute-start.6 = (f32[4,8,128]{2,1,0:T(8,128)S(1)}, f32[4,8,128]{2,1,0:T(8,128)S(1)}, u32[]{:S(2)}, u32[]{:S(2)}) collective-permute-start(f32[4,8,128]{2,1,0:T(8,128)S(1)} %pad_maximum_fusion.6), channel_id=1, source_target_pairs={{0,4},{4,0},{8,12},{12,8},{1,5},{5,1},{9,13},{13,9},{2,6},{6,2},{1... | collective-permute-start | bytes 49160 | tf_op jit(solution)/shard_map/ppermute | solution.py:337
  45.5 6.3 %collective-permute-start.8 = (f32[4,8,128]{2,1,0:T(8,128)S(1)}, f32[4,8,128]{2,1,0:T(8,128)S(1)}, u32[]{:S(2)}, u32[]{:S(2)}) collective-permute-start(f32[4,8,128]{2,1,0:T(8,128)S(1)} %get-tuple-element.25), channel_id=1, source_target_pairs={{0,4},{4,0},{8,12},{12,8},{1,5},{5,1},{9,13},{13,9},{2,6},{6,2},{1... | collective-permute-start | bytes 49160 | tf_op jit(solution)/shard_map/ppermute | solution.py:295
  45.6 5.6 %collective-permute-start.9 = (f32[4,8,128]{2,1,0:T(8,128)S(1)}, f32[4,8,128]{2,1,0:T(8,128)S(1)}, u32[]{:S(2)}, u32[]{:S(2)}) collective-permute-start(f32[4,8,128]{2,1,0:T(8,128)S(1)} %get-tuple-element.26), channel_id=1, source_target_pairs={{4,8},{8,4},{5,9},{9,5},{6,10},{10,6},{7,11},{11,7},{20,24},{24,20... | collective-permute-start | bytes 49160 | tf_op jit(solution)/shard_map/ppermute | solution.py:295
  51.3 0.6 copy-start.10
  51.9 0.7 slice-start.1
  52.6 3.8 %copy-start.11 = (f32[4,8,128]{2,1,0:T(8,128)S(1)}, f32[4,8,128]{2,1,0:T(8,128)}, u32[]{:S(2)}) copy-start(f32[4,8,128]{2,1,0:T(8,128)} %copy-done.10) | copy-start | bytes 49156
  52.6 3.8 %collective-permute-start.10 = (f32[6,8,128]{2,1,0:T(8,128)S(1)}, f32[6,8,128]{2,1,0:T(8,128)S(1)}, u32[]{:S(2)}, u32[]{:S(2)}) collective-permute-start(f32[6,8,128]{2,1,0:T(8,128)S(1)} %pad_maximum_fusion.4), channel_id=1, source_target_pairs={{0,2},{2,0},{1,3},{3,1},{4,6},{6,4},{5,7},{7,5},{8,10},{10,8},{9,1... | collective-permute-start | bytes 73736 | tf_op jit(solution)/shard_map/ppermute | solution.py:302
  56.4 1.4 %collective-permute-start.11 = (f32[22,8,128]{2,1,0:T(8,128)S(1)}, f32[22,8,128]{2,1,0:T(8,128)S(1)}, u32[]{:S(2)}, u32[]{:S(2)}) collective-permute-start(f32[22,8,128]{2,1,0:T(8,128)S(1)} %get-tuple-element.46), channel_id=1, source_target_pairs={{0,1},{1,0},{2,3},{3,2},{4,5},{5,4},{6,7},{7,6},{8,9},{9,8},{10,11... | collective-permute-start | bytes 270344 | tf_op jit(solution)/shard_map/ppermute | solution.py:306
  73.7 1.4 %collective-permute-start.12 = (f32[22,8,128]{2,1,0:T(8,128)S(1)}, f32[22,8,128]{2,1,0:T(8,128)S(1)}, u32[]{:S(2)}, u32[]{:S(2)}) collective-permute-start(f32[22,8,128]{2,1,0:T(8,128)S(1)} %get-tuple-element.29), channel_id=1, source_target_pairs={{0,1},{1,0},{2,3},{3,2},{4,5},{5,4},{6,7},{7,6},{8,9},{9,8},{10,11... | collective-permute-start | bytes 270344 | tf_op jit(solution)/shard_map/ppermute | solution.py:321
  75.0 3.9 %collective-permute-start.13 = (f32[6,8,128]{2,1,0:T(8,128)S(1)}, f32[6,8,128]{2,1,0:T(8,128)S(1)}, u32[]{:S(2)}, u32[]{:S(2)}) collective-permute-start(f32[6,8,128]{2,1,0:T(8,128)S(1)} %pad_maximum_fusion.5), channel_id=1, source_target_pairs={{0,2},{2,0},{1,3},{3,1},{4,6},{6,4},{5,7},{7,5},{8,10},{10,8},{9,1... | collective-permute-start | bytes 73736 | tf_op jit(solution)/shard_map/ppermute | solution.py:332
  78.9 5.6 %collective-permute-start.15 = (f32[4,8,128]{2,1,0:T(8,128)S(1)}, f32[4,8,128]{2,1,0:T(8,128)S(1)}, u32[]{:S(2)}, u32[]{:S(2)}) collective-permute-start(f32[4,8,128]{2,1,0:T(8,128)S(1)} %pad_maximum_fusion.9), channel_id=1, source_target_pairs={{4,8},{8,4},{5,9},{9,5},{6,10},{10,6},{7,11},{11,7},{20,24},{24,20... | collective-permute-start | bytes 49160 | tf_op jit(solution)/shard_map/ppermute | solution.py:337
  80.9 3.8 %collective-permute-start.14 = (f32[4,8,128]{2,1,0:T(8,128)S(1)}, f32[4,8,128]{2,1,0:T(8,128)S(1)}, u32[]{:S(2)}, u32[]{:S(2)}) collective-permute-start(f32[4,8,128]{2,1,0:T(8,128)S(1)} %pad_maximum_fusion.8), channel_id=1, source_target_pairs={{0,4},{4,0},{8,12},{12,8},{1,5},{5,1},{9,13},{13,9},{2,6},{6,2},{1... | collective-permute-start | bytes 49160 | tf_op jit(solution)/shard_map/ppermute | solution.py:337

commit v2 on v1

v2 whole, which is shorter than its diff:
```python
import functools

import jax
import jax.numpy as jnp
from jax import lax
from jax.experimental import pallas as pl
from jax.experimental.pallas import tpu as pltpu
from jax.sharding import PartitionSpec as P

STEPS = 2
F32 = jnp.float32
BF16 = jnp.bfloat16
VMEM = pl.BlockSpec(memory_space=pltpu.VMEM)


def lane_pick(row, lanes):
    return jnp.take_along_axis(row, lanes, axis=1, mode="promise_in_bounds")


def spread(row):
    return jnp.broadcast_to(row, (8, 128))


def split(value):
    high = value.astype(BF16).astype(F32)
    return high, value - high


def padded(tile):
    return jnp.concatenate([tile, jnp.zeros((8 - tile.shape[0], 128), F32)], axis=0)


def pick_lists(field_ref, picks_ref, outs):
    picks = [picks_ref[0:8, :], picks_ref[8:16, :]]
    lanes = [p & 127 for p in picks]
    rows = [lax.shift_right_logical(p, 7) for p in picks]
    found = [[jnp.zeros((8, 128), F32) for _ in range(2)] for _ in range(6)]
    for tile in range(16):
        hit = [r == tile for r in rows]
        for c in range(6):
            row = spread(field_ref[tile, c : c + 1, :])
            for v in range(2):
                found[c][v] = jnp.where(hit[v], lane_pick(row, lanes[v]), found[c][v])
    for c in range(8):
        both = jnp.concatenate(found[c], axis=0) if c < 6 else jnp.zeros((16, 128), F32)
        at = 0
        for out in outs:
            size = out.shape[0]
            out[:, c, :] = both[at : at + size, :]
            at += size


def lists_kernel(displace_ref, picks_ref, field_ref, *outs):
    for tile in range(16):
        field_ref[tile] = padded(displace_ref[:, tile * 128 : (tile + 1) * 128])
    pick_lists(field_ref, picks_ref, outs)


def one_hot(lanes):
    iota = lax.broadcasted_iota(jnp.int32, (256, 128), 0)
    return jnp.where(iota == lanes, 1.0, 0.0).astype(BF16)


def times_one_hot(values, hot):
    return lax.dot_general(values, hot, (((1,), (1,)), ((), ())), preferred_element_type=F32)


def beam_kernel(
    n,
    kinds,
    field_ref,
    near_ref,
    other_ref,
    slots_ref,
    shape_ref,
    kind_ref,
    weight_ref,
    stiff_ref,
    own_ref,
    own_near_ref,
    send_ref,
    table_ref,
    hot_ref,
    x_ref,
    vec_ref,
    cat_ref,
    force_ref,
    a_ref,
    acc_ref,
):
    rows = 16 + 2 * n
    low_at = rows * 8

    def tile_of(row, half):
        if row < 8:
            return field_ref[2 * row + half]
        if row < 16:
            return other_ref[2 * (row - 8) + half]
        if row < 16 + n:
            return near_ref[2 * (row - 16) + half]
        return other_ref[2 * (row - 8 - n) + half]

    for row in range(0, rows, 2):
        for half in range(2):
            high, low = split(jnp.concatenate([tile_of(row, half), tile_of(row + 1, half)], axis=0))
            table_ref[row * 8 : row * 8 + 16, half * 128 : (half + 1) * 128] = high.astype(BF16)
            table_ref[low_at + row * 8 : low_at + row * 8 + 16, half * 128 : (half + 1) * 128] = low.astype(BF16)

    def gather(g, carry):
        col = pl.multiple_of(g * 256, 256)
        start = pl.multiple_of(g * 1536, 1536)
        slots = slots_ref[:, pl.ds(col, 256)]
        shape = shape_ref[:, pl.ds(col, 256)]
        for bb in range(2):
            for j in range(6):
                slot = slots[j : j + 1, bb * 128 : (bb + 1) * 128]
                hot_ref[:, pl.ds(start + (bb * 6 + j) * 128, 128)] = one_hot(slot & 255)
        x_ref[...] = jnp.dot(table_ref[...], hot_ref[:, pl.ds(start, 1536)], preferred_element_type=F32)
        for bb in range(2):
            for e in range(2):
                end = jnp.zeros((8, 128), F32)
                for k in range(3):
                    j = 3 * e + k
                    hi = spread(lax.shift_right_logical(slots[j : j + 1, bb * 128 : (bb + 1) * 128], 8))
                    at = (bb * 6 + j) * 128
                    found = jnp.zeros((8, 128), F32)
                    for row in range(rows):
                        both = (
                            x_ref[row * 8 : row * 8 + 8, at : at + 128]
                            + x_ref[low_at + row * 8 : low_at + row * 8 + 8, at : at + 128]
                        )
                        found = jnp.where(hi == row, both, found)
                    end += found * spread(shape[j : j + 1, bb * 128 : (bb + 1) * 128])
                vec_ref[e * 8 : (e + 1) * 8, pl.ds(col + bb * 128, 128)] = end
        return carry

    lax.fori_loop(0, 8, gather, 0)

    v1, rest = split(vec_ref[...])
    v2, v3 = split(rest)
    for at, piece in enumerate((v1, v2, v1, v2, v3, v1)):
        cat_ref[at * 16 : (at + 1) * 16, :] = piece.astype(BF16)
    s1, rest = split(stiff_ref[...])
    s2, s3 = split(rest)
    block = lax.broadcasted_iota(jnp.int32, s1.shape, 1) // 16
    stiff = jnp.where((block == 2) | (block == 3), s2, jnp.where(block == 5, s3, s1)).astype(BF16)
    force_ref[...] = jnp.dot(stiff, cat_ref[...], preferred_element_type=F32)

    acc_ref[...] = jnp.zeros_like(acc_ref)

    def scatter(g, carry):
        col = pl.multiple_of(g * 256, 256)
        start = pl.multiple_of(g * 1536, 1536)
        slots = slots_ref[:, pl.ds(col, 256)]
        shape = shape_ref[:, pl.ds(col, 256)]
        for bb in range(2):
            kind = spread(kind_ref[pl.ds(2 * g + bb, 1), :])
            weight = weight_ref[pl.ds(2 * g + bb, 1), :]
            for e in range(2):
                force = jnp.zeros((8, 128), F32)
                for t in range(kinds):
                    force = jnp.where(
                        kind == t,
                        force_ref[t * 16 + e * 8 : t * 16 + e * 8 + 8, pl.ds(col + bb * 128, 128)],
                        force,
                    )
                for k in range(3):
                    j = 3 * e + k
                    at = (bb * 6 + j) * 128
                    hi = spread(lax.shift_right_logical(slots[j : j + 1, bb * 128 : (bb + 1) * 128], 8))
                    high, low = split(force * spread(shape[j : j + 1, bb * 128 : (bb + 1) * 128] * weight))
                    for row in range(0, rows, 2):
                        hit = [hi == row, hi == row + 1]
                        for base, piece in ((0, high), (low_at, low)):
                            a_ref[base + row * 8 : base + row * 8 + 16, at : at + 128] = jnp.concatenate(
                                [jnp.where(hit[0], piece, 0.0), jnp.where(hit[1], piece, 0.0)], axis=0
                            ).astype(BF16)
        acc_ref[...] += times_one_hot(a_ref[...], hot_ref[:, pl.ds(start, 1536)])
        return carry

    lax.fori_loop(0, 8, scatter, 0)
    for row in range(rows):
        total = acc_ref[row * 8 : row * 8 + 8, :] + acc_ref[low_at + row * 8 : low_at + row * 8 + 8, :]
        for half in range(2):
            part = total[:, half * 128 : (half + 1) * 128]
            if row < 8:
                own_ref[2 * row + half] = part
            elif row < 16:
                send_ref[2 * (row - 8) + half] = part
            elif row < 16 + n:
                own_near_ref[2 * (row - 16) + half] = part
            else:
                send_ref[2 * (row - 8 - n) + half] = part


def update_kernel(n_returns, last, own_ref, recv_ref, field_ref, velocity_ref, mass_ref, picks_ref, *refs):
    returns, refs = refs[:n_returns], refs[n_returns:]
    new_field_ref, new_velocity_ref = refs[0], refs[1]
    a_ref, b_ref = refs[-2], refs[-1]
    outs = refs[2:-2]
    p = 0
    for ret in returns:
        for tile in range(ret.shape[0]):
            pick = picks_ref[p : p + 1, :]
            hi = spread(lax.shift_right_logical(pick, 8))
            at = p * 128
            for base, piece in zip((0, 64), split(ret[tile])):
                a_ref[base : base + 64, at : at + 128] = jnp.concatenate(
                    [jnp.where(hi == row, piece, 0.0) for row in range(8)], axis=0
                ).astype(BF16)
            b_ref[:, at : at + 128] = one_hot(pick & 255)
            p += 1
    back = times_one_hot(a_ref[...], b_ref[...])
    back = back[:64] + back[64:]
    for tile in range(16):
        row, half = tile // 2, tile % 2
        cols = slice(tile * 128, (tile + 1) * 128)
        force = own_ref[tile] + recv_ref[tile] + back[row * 8 : row * 8 + 8, half * 128 : (half + 1) * 128]
        velocity = 0.98 * velocity_ref[:, cols] - 0.2 * force[0:6] / mass_ref[:, cols]
        new_velocity_ref[:, cols] = velocity
        field = field_ref[tile][0:6] + 0.2 * velocity
        if last:
            new_field_ref[:, cols] = field
        else:
            new_field_ref[tile] = padded(field)
    if not last:
        pick_lists(new_field_ref, picks_ref, outs)


def pairs(count, shift):
    out = []
    for i in range(shift, count - 1, 2):
        out += [(i, i + 1), (i + 1, i)]
    return out


def f32_out(*shape):
    return jax.ShapeDtypeStruct(shape, F32)


def params():
    return pltpu.CompilerParams(vmem_limit_bytes=48 * 1024 * 1024)


def shards(
    displace,
    velocity,
    nodal_mass,
    send_list,
    beam_slots,
    shape_values,
    beam_kind,
    cluster_weight,
    stiffness,
):
    list_len = send_list.shape[2]
    cols = lax.axis_size("cols")
    U = 2 if cols <= 2 else 3
    n = 3 * U - 1
    rows = 16 + 2 * n
    kinds = stiffness.shape[0]
    r_odd = lax.axis_index("rows") % 2
    c_odd = lax.axis_index("cols") % 2
    s = lax.axis_index("sub")
    row_perm = [pairs(lax.axis_size("rows"), 0), pairs(lax.axis_size("rows"), 1)]
    col_perm = [pairs(cols, 0), pairs(cols, 1)][: U - 1]
    sub_perm = [(0, 1), (1, 0)]

    row_order = jnp.where(r_odd == 0, send_list[::-1], send_list)
    ordered = jnp.where(c_odd == 0, row_order[:, ::-1], row_order)
    rows_of = [ordered[0], ordered[2], ordered[1]]
    col_at = [1, 0, 2][:U]
    picks = [rows_of[t][u] for t in range(2) for u in col_at] + [rows_of[2][u] for u in col_at[1:]]
    picks = jnp.stack(picks).reshape(2 * n, 128)
    if 2 * n < 16:
        picks = jnp.concatenate([picks, jnp.zeros((16 - 2 * n, 128), jnp.int32)], axis=0)

    slots = beam_slots
    hi = slots >> 8
    remote = hi - 16
    sender = (remote >= 9).astype(jnp.int32)
    direction = remote - 9 * sender
    a = (direction >= 3).astype(jnp.int32) + (direction >= 6).astype(jnp.int32)
    b = direction - 3 * a
    a = jnp.where(r_odd == 0, a, 2 - a)
    b = jnp.where(c_odd == 0, b, 2 - b)
    t = jnp.where(a == 1, 2, a >> 1)
    u = jnp.where(b == 1, 0, (b >> 1) + 1)
    order = jnp.where(t == 2, 2 * U + u - 1, t * U + u)
    rel_near = 16 + n * (sender ^ s) + order
    rel_near = jnp.where(u < U, rel_near, 64)
    rel = jnp.where(hi < 16, hi ^ (8 * s), rel_near)
    slots = rel * 256 + (slots & 255)

    kind = beam_kind.reshape(16, 128)
    weight = cluster_weight.reshape(16, 128)
    stiff = jnp.pad(stiffness.reshape(kinds, 2, 6, 2, 6), ((0, 0), (0, 0), (0, 2), (0, 0), (0, 2)))
    stiff = jnp.tile(stiff.reshape(kinds * 16, 16), (1, 6))
    mass = nodal_mass.reshape(1, -1)

    speed = velocity
    list_outs = [f32_out(2 * U, 8, 128), f32_out(2 * U, 8, 128), f32_out(2 * U - 2, 8, 128)]
    field, *outgoing = pl.pallas_call(
        lists_kernel,
        out_shape=[f32_out(16, 8, 128)] + list_outs,
        in_specs=[VMEM] * 2,
        out_specs=[VMEM] * 4,
        compiler_params=params(),
    )(displace, picks)
    for step in range(STEPS):
        to_rows, own_row = outgoing[:2], outgoing[2]
        arrived = [lax.ppermute(x, "rows", perm) for x, perm in zip(to_rows, row_perm)]
        near = [[x[0:2]] for x in arrived] + [[]]
        for u in range(1, U):
            at = 2 * u
            message = jnp.concatenate(
                [arrived[0][at : at + 2], arrived[1][at : at + 2], own_row[at - 2 : at]], axis=0
            )
            got = lax.ppermute(message, "cols", col_perm[u - 1])
            for t in range(3):
                near[t].append(got[2 * t : 2 * t + 2])
        near = jnp.concatenate(near[0] + near[1] + near[2], axis=0)
        other = lax.ppermute(jnp.concatenate([field, near], axis=0), "sub", sub_perm)
        own, own_near, send = pl.pallas_call(
            functools.partial(beam_kernel, n, kinds),
            out_shape=[f32_out(16, 8, 128), f32_out(2 * n, 8, 128), f32_out(16 + 2 * n, 8, 128)],
            in_specs=[VMEM] * 8,
            out_specs=[VMEM] * 3,
            scratch_shapes=[
                pltpu.VMEM((16 * rows, 256), BF16),
                pltpu.VMEM((256, 12288), BF16),
                pltpu.VMEM((16 * rows, 1536), F32),
                pltpu.VMEM((16, 2048), F32),
                pltpu.VMEM((96, 2048), BF16),
                pltpu.VMEM((16 * kinds, 2048), F32),
                pltpu.VMEM((16 * rows, 1536), BF16),
                pltpu.VMEM((16 * rows, 256), F32),
            ],
            compiler_params=params(),
        )(field, near, other, slots, shape_values, kind, weight, stiff)
        recv = lax.ppermute(send, "sub", sub_perm)
        total = own_near + recv[16:]

        def listed(t, u):
            at = 2 * (t * U + u) if t < 2 else 2 * (2 * U + u - 1)
            return total[at : at + 2]

        back_rows = [[listed(0, 0)], [listed(1, 0)]]
        back_own = []
        for u in range(1, U):
            message = jnp.concatenate([listed(t, u) for t in range(3)], axis=0)
            got = lax.ppermute(message, "cols", col_perm[u - 1])
            back_rows[0].append(got[0:2])
            back_rows[1].append(got[2:4])
            back_own.append(got[4:6])
        returns = [
            lax.ppermute(jnp.concatenate(x, axis=0), "rows", perm)
            for x, perm in zip(back_rows, row_perm)
        ] + [jnp.concatenate(back_own, axis=0)]
        last = step == STEPS - 1
        outs = pl.pallas_call(
            functools.partial(update_kernel, 3, last),
            out_shape=[f32_out(6, 2048)] * 2 if last else [f32_out(16, 8, 128), f32_out(6, 2048)] + list_outs,
            in_specs=[VMEM] * 9,
            out_specs=[VMEM] * (2 if last else 5),
            scratch_shapes=[pltpu.VMEM((128, 256 * n), BF16), pltpu.VMEM((256, 256 * n), BF16)],
            compiler_params=params(),
        )(own, recv, field, speed, mass, picks, *returns)
        field, speed = outs[:2]
        outgoing = outs[2:]
    return field, speed


def solution(mesh):
    whole = ("groups", "rows", "cols", "sub")
    in_specs = (
        P(None, whole),
        P(None, whole),
        P(whole),
        P("rows", "cols", ("groups", "sub")),
        P(None, whole),
        P(None, whole),
        P(whole),
        P(whole),
        P(),
    )
    out_specs = (P(None, whole), P(None, whole))
    return jax.shard_map(shards, mesh=mesh, in_specs=in_specs, out_specs=out_specs, check_vma=False)
```

time: 88.1 us -> 74.7 us (0.85)
  Pallas kernels: 33.1 us -> 25.2 us
  waiting for transfers between devices: 24.5 us -> 20 us
  local copies, waits for them, and re-layouts: 7.9 us -> 3.68 us
  starting transfers between devices: 19.7 us -> 23.7 us
    pallas_call x3, Pallas kernels: 32 us -> 23.5 us  [the longest x2 23.2 us: shards(): pl.pallas_call(functools.partial(beam_kernel, n, kinds), out_shape=[f32_o...]
    ppermute x4, waiting for transfers between devices: 6.78 us -> 3.39 us  [shards(): lax.ppermute(jnp.concatenate(x, axis=0), 'rows', perm)]
    unnamed x36 -> x31, local copies, waits for them, and re-layouts: 4.67 us -> 2.37 us
    ppermute x4, starting transfers between devices: 7.1 us -> 9.1 us  [shards(): lax.ppermute(x, 'rows', perm)]
    ppermute x4, waiting for transfers between devices: 5.32 us -> 3.37 us  [shards(): lax.ppermute(x, 'rows', perm)]
    ppermute x4, starting transfers between devices: 5.99 us -> 7.85 us  [shards(): lax.ppermute(jnp.concatenate(x, axis=0), 'rows', perm)]
    reshape x9 -> x1, local copies, waits for them, and re-layouts: 1.62 us -> 0.11 us  [shards(): stiffness.reshape(kinds, 2, 6, 2, 6)]
  transfers between devices with their start and end apart: 16 -> 16, of which waited for: 14 -> 12; matrix products, arithmetic and copies ran while one was open for 0% -> 1% of each run, Pallas kernels for 0% -> 0%
where the time goes in v2:
time: 74.7 us; the launch traced here: 73.8 us
  Pallas kernels  25.2 us (34%)
  starting transfers between devices  23.7 us (32%)
  waiting for transfers between devices  20 us (27%)
  local copies, waits for them, and re-layouts  3.68 us (5%)
  between operations  1.03 us (1%)
    pallas_call x2, Pallas kernels, shards(): pl.pallas_call(functools.partial(beam_kernel, n, kinds), out_shape=[f32_o...  23.2 us
    ppermute x4, starting transfers between devices, shards(): lax.ppermute(x, 'rows', perm)  9.1 us
    ppermute x4, waiting for transfers between devices, shards(): got = lax.ppermute(message, 'cols', col_perm[u - 1])  8.4 us
    ppermute x4, starting transfers between devices, shards(): lax.ppermute(jnp.concatenate(x, axis=0), 'rows', perm)  7.85 us
    ppermute x4, starting transfers between devices, shards(): got = lax.ppermute(message, 'cols', col_perm[u - 1])  6.16 us
    ppermute x4, waiting for transfers between devices, shards(): lax.ppermute(jnp.concatenate(x, axis=0), 'rows', perm)  3.39 us
    ppermute x4, waiting for transfers between devices, shards(): lax.ppermute(x, 'rows', perm)  3.37 us
    ppermute x2, waiting for transfers between devices, shards(): lax.ppermute(jnp.concatenate([field, near], axis=0), 'sub', sub_perm)  2.55 us
  transfers between devices with their start and end apart: 16, of which 12 were waited for; matrix products, arithmetic and copies ran while one was open for 1% of the time, Pallas kernels for 0%

profile of v2, /device:TPU:8, one launch (start us, length us, event | category | flops | bytes accessed | tf_op | source)
XLA Modules:
  0.0 73.8 jit_solution(9608323169850077123)
XLA Ops:
  0.6 0.0 copy-start.7
  0.7 0.7 copy-done.7
  1.4 0.0 copy-start.1
  1.4 0.1 rev.7
  1.5 0.7 copy-done.1
  2.2 0.3 shard_map.104
  2.5 0.1 collective-permute-start
  2.6 5.0 %collective-permute-start.1 = (f32[4,8,128]{2,1,0:T(8,128)S(1)}, f32[4,8,128]{2,1,0:T(8,128)S(1)}, u32[]{:S(2)}, u32[]{:S(2)}) collective-permute-start(f32[4,8,128]{2,1,0:T(8,128)S(1)} %get-tuple-element.19), channel_id=1, source_target_pairs={{4,8},{8,4},{5,9},{9,5},{6,10},{10,6},{7,11},{11,7},{20,24},{24,20... | collective-permute-start | bytes 49160 | tf_op jit(solution)/shard_map/ppermute | solution.py:312
  7.6 0.0 copy-start.6
  7.6 1.7 %collective-permute-done.1 = f32[4,8,128]{2,1,0:T(8,128)S(1)} collective-permute-done((f32[4,8,128]{2,1,0:T(8,128)S(1)}, f32[4,8,128]{2,1,0:T(8,128)S(1)}, u32[]{:S(2)}, u32[]{:S(2)}) %collective-permute-start.1) | collective-permute-done | bytes 16416 | tf_op jit(solution)/shard_map/ppermute | solution.py:312
  9.3 0.0 collective-permute-done
  9.3 0.0 copy-start.8
  9.3 1.6 %collective-permute-start.2 = (f32[6,8,128]{2,1,0:T(8,128)S(1)}, f32[6,8,128]{2,1,0:T(8,128)S(1)}, u32[]{:S(2)}, u32[]{:S(2)}) collective-permute-start(f32[6,8,128]{2,1,0:T(8,128)S(1)} %pad_maximum_fusion.2), channel_id=1, source_target_pairs={{0,2},{2,0},{1,3},{3,1},{4,6},{6,4},{5,7},{7,5},{8,10},{10,8},{9,1... | collective-permute-start | bytes 73736 | tf_op jit(solution)/shard_map/ppermute | solution.py:319
  10.9 0.0 copy-done.6
  10.9 0.1 and_add_fusion.slots_ref
  11.0 0.0 copy-done.8
  11.0 0.1 reshape.31
  11.1 0.3 copy.14
  11.5 0.2 tile.10
  11.7 0.1 copy.12.stiff_ref
  11.8 1.4 %collective-permute-done.2 = f32[6,8,128]{2,1,0:T(8,128)S(1)} collective-permute-done((f32[6,8,128]{2,1,0:T(8,128)S(1)}, f32[6,8,128]{2,1,0:T(8,128)S(1)}, u32[]{:S(2)}, u32[]{:S(2)}) %collective-permute-start.2) | collective-permute-done | bytes 24608 | tf_op jit(solution)/shard_map/ppermute | solution.py:319
  13.2 0.0 copy-start
  13.2 0.1 collective-permute-start.3
  13.3 0.0 copy-start.4
  13.3 0.0 copy-start.5
  13.4 1.3 %collective-permute-done.3.other_ref = f32[26,8,128]{2,1,0:T(8,128)S(1)} collective-permute-done((f32[26,8,128]{2,1,0:T(8,128)S(1)}, f32[26,8,128]{2,1,0:T(8,128)S(1)}, u32[]{:S(2)}, u32[]{:S(2)}) %collective-permute-start.3) | collective-permute-done | bytes 106528 | tf_op jit(solution)/shard_map/ppermute | solution.py:323
  14.6 0.0 copy-done
  14.6 0.0 copy-done.4
  14.6 0.0 copy-done.5
  14.6 11.6 %shard_map.105 = (f32[16,8,128]{2,1,0:T(8,128)S(1)}, f32[10,8,128]{2,1,0:T(8,128)S(1)}, f32[26,8,128]{2,1,0:T(8,128)S(1)}) custom-call(f32[16,8,128]{2,1,0:T(8,128)S(1)} %get-tuple-element.17.field_ref, f32[10,8,128]{2,1,0:T(8,128)S(1)} %pad_maximum_fusion.near_ref, f32[26,8,128]{2,1,0:T(8,128)S(1)} %collective-permute-done.3.other_ref, ...), custom_call_target="tpu_custom_call" | custom-call | tf_op jit(solution)/shard_map/pallas_call | solution.py:324
  26.2 0.2 collective-permute-start.4
  26.5 1.2 %collective-permute-done.4.recv_ref = f32[26,8,128]{2,1,0:T(8,128)S(1)} collective-permute-done((f32[26,8,128]{2,1,0:T(8,128)S(1)}, f32[26,8,128]{2,1,0:T(8,128)S(1)}, u32[]{:S(2)}, u32[]{:S(2)}) %collective-permute-start.4) | collective-permute-done | bytes 106528 | tf_op jit(solution)/shard_map/ppermute | solution.py:341
  27.7 0.0 copy-start.2
  27.7 1.6 %collective-permute-start.5 = (f32[6,8,128]{2,1,0:T(8,128)S(1)}, f32[6,8,128]{2,1,0:T(8,128)S(1)}, u32[]{:S(2)}, u32[]{:S(2)}) collective-permute-start(f32[6,8,128]{2,1,0:T(8,128)S(1)} %pad_maximum_fusion.3), channel_id=1, source_target_pairs={{0,2},{2,0},{1,3},{3,1},{4,6},{6,4},{5,7},{7,5},{8,10},{10,8},{9,1... | collective-permute-start | bytes 73736 | tf_op jit(solution)/shard_map/ppermute | solution.py:352
  29.2 2.3 %collective-permute-done.5 = f32[6,8,128]{2,1,0:T(8,128)S(1)} collective-permute-done((f32[6,8,128]{2,1,0:T(8,128)S(1)}, f32[6,8,128]{2,1,0:T(8,128)S(1)}, u32[]{:S(2)}, u32[]{:S(2)}) %collective-permute-start.5) | collective-permute-done | bytes 24608 | tf_op jit(solution)/shard_map/ppermute | solution.py:352
  31.6 0.0 collective-permute-start.6
  31.6 0.0 copy-start.3
  31.6 3.9 %collective-permute-start.7 = (f32[4,8,128]{2,1,0:T(8,128)S(1)}, f32[4,8,128]{2,1,0:T(8,128)S(1)}, u32[]{:S(2)}, u32[]{:S(2)}) collective-permute-start(f32[4,8,128]{2,1,0:T(8,128)S(1)} %pad_maximum_fusion.7), channel_id=1, source_target_pairs={{4,8},{8,4},{5,9},{9,5},{6,10},{10,6},{7,11},{11,7},{20,24},{24,20... | collective-permute-start | bytes 49160 | tf_op jit(solution)/shard_map/ppermute | solution.py:357
  35.5 0.0 collective-permute-done.6.refs_0_
  35.5 1.7 %collective-permute-done.7.refs_1_ = f32[4,8,128]{2,1,0:T(8,128)S(1)} collective-permute-done((f32[4,8,128]{2,1,0:T(8,128)S(1)}, f32[4,8,128]{2,1,0:T(8,128)S(1)}, u32[]{:S(2)}, u32[]{:S(2)}) %collective-permute-start.7) | collective-permute-done | bytes 16416 | tf_op jit(solution)/shard_map/ppermute | solution.py:357
  37.2 0.0 copy-done.2
  37.2 0.0 copy-done.3
  37.2 0.7 shard_map.106
  37.9 0.1 collective-permute-start.8
  38.0 3.9 %collective-permute-start.9 = (f32[4,8,128]{2,1,0:T(8,128)S(1)}, f32[4,8,128]{2,1,0:T(8,128)S(1)}, u32[]{:S(2)}, u32[]{:S(2)}) collective-permute-start(f32[4,8,128]{2,1,0:T(8,128)S(1)} %get-tuple-element.26), channel_id=1, source_target_pairs={{4,8},{8,4},{5,9},{9,5},{6,10},{10,6},{7,11},{11,7},{20,24},{24,20... | collective-permute-start | bytes 49160 | tf_op jit(solution)/shard_map/ppermute | solution.py:312
  42.0 1.7 %collective-permute-done.9 = f32[4,8,128]{2,1,0:T(8,128)S(1)} collective-permute-done((f32[4,8,128]{2,1,0:T(8,128)S(1)}, f32[4,8,128]{2,1,0:T(8,128)S(1)}, u32[]{:S(2)}, u32[]{:S(2)}) %collective-permute-start.9) | collective-permute-done | bytes 16416 | tf_op jit(solution)/shard_map/ppermute | solution.py:312
  43.7 0.6 copy-done.9
  44.3 0.0 collective-permute-done.8
  44.3 0.7 slice-done
  45.0 1.5 %collective-permute-start.10 = (f32[6,8,128]{2,1,0:T(8,128)S(1)}, f32[6,8,128]{2,1,0:T(8,128)S(1)}, u32[]{:S(2)}, u32[]{:S(2)}) collective-permute-start(f32[6,8,128]{2,1,0:T(8,128)S(1)} %pad_maximum_fusion.4), channel_id=1, source_target_pairs={{0,2},{2,0},{1,3},{3,1},{4,6},{6,4},{5,7},{7,5},{8,10},{10,8},{9,1... | collective-permute-start | bytes 73736 | tf_op jit(solution)/shard_map/ppermute | solution.py:319
  46.5 2.3 %collective-permute-done.10 = f32[6,8,128]{2,1,0:T(8,128)S(1)} collective-permute-done((f32[6,8,128]{2,1,0:T(8,128)S(1)}, f32[6,8,128]{2,1,0:T(8,128)S(1)}, u32[]{:S(2)}, u32[]{:S(2)}) %collective-permute-start.10) | collective-permute-done | bytes 24608 | tf_op jit(solution)/shard_map/ppermute | solution.py:319
  48.8 0.0 copy-done.10
  48.8 0.1 collective-permute-start.11
  48.9 1.3 %collective-permute-done.11.other_ref = f32[26,8,128]{2,1,0:T(8,128)S(1)} collective-permute-done((f32[26,8,128]{2,1,0:T(8,128)S(1)}, f32[26,8,128]{2,1,0:T(8,128)S(1)}, u32[]{:S(2)}, u32[]{:S(2)}) %collective-permute-start.11) | collective-permute-done | bytes 106528 | tf_op jit(solution)/shard_map/ppermute | solution.py:323
  50.2 11.6 %shard_map.107 = (f32[16,8,128]{2,1,0:T(8,128)S(1)}, f32[10,8,128]{2,1,0:T(8,128)S(1)}, f32[26,8,128]{2,1,0:T(8,128)S(1)}) custom-call(f32[16,8,128]{2,1,0:T(8,128)S(1)} %get-tuple-element.24.field_ref, f32[10,8,128]{2,1,0:T(8,128)S(1)} %pad_maximum_fusion.1.near_ref, f32[26,8,128]{2,1,0:T(8,128)S(1)} %collective-permute-done.11.other_ref, ...), custom_call_target="tpu_custom_call" | custom-call | tf_op jit(solution)/shard_map/pallas_call | solution.py:324
  61.8 0.2 collective-permute-start.12
  62.0 1.2 %collective-permute-done.12.recv_ref = f32[26,8,128]{2,1,0:T(8,128)S(1)} collective-permute-done((f32[26,8,128]{2,1,0:T(8,128)S(1)}, f32[26,8,128]{2,1,0:T(8,128)S(1)}, u32[]{:S(2)}, u32[]{:S(2)}) %collective-permute-start.12) | collective-permute-done | bytes 106528 | tf_op jit(solution)/shard_map/ppermute | solution.py:341
  63.2 1.6 %collective-permute-start.13 = (f32[6,8,128]{2,1,0:T(8,128)S(1)}, f32[6,8,128]{2,1,0:T(8,128)S(1)}, u32[]{:S(2)}, u32[]{:S(2)}) collective-permute-start(f32[6,8,128]{2,1,0:T(8,128)S(1)} %pad_maximum_fusion.5), channel_id=1, source_target_pairs={{0,2},{2,0},{1,3},{3,1},{4,6},{6,4},{5,7},{7,5},{8,10},{10,8},{9,1... | collective-permute-start | bytes 73736 | tf_op jit(solution)/shard_map/ppermute | solution.py:352
  64.8 2.3 %collective-permute-done.13 = f32[6,8,128]{2,1,0:T(8,128)S(1)} collective-permute-done((f32[6,8,128]{2,1,0:T(8,128)S(1)}, f32[6,8,128]{2,1,0:T(8,128)S(1)}, u32[]{:S(2)}, u32[]{:S(2)}) %collective-permute-start.13) | collective-permute-done | bytes 24608 | tf_op jit(solution)/shard_map/ppermute | solution.py:352
  67.1 0.0 collective-permute-start.14
  67.1 3.9 %collective-permute-start.15 = (f32[4,8,128]{2,1,0:T(8,128)S(1)}, f32[4,8,128]{2,1,0:T(8,128)S(1)}, u32[]{:S(2)}, u32[]{:S(2)}) collective-permute-start(f32[4,8,128]{2,1,0:T(8,128)S(1)} %pad_maximum_fusion.9), channel_id=1, source_target_pairs={{4,8},{8,4},{5,9},{9,5},{6,10},{10,6},{7,11},{11,7},{20,24},{24,20... | collective-permute-start | bytes 49160 | tf_op jit(solution)/shard_map/ppermute | solution.py:357
  71.1 0.0 collective-permute-done.14.refs_0_
  71.1 1.7 %collective-permute-done.15.refs_1_ = f32[4,8,128]{2,1,0:T(8,128)S(1)} collective-permute-done((f32[4,8,128]{2,1,0:T(8,128)S(1)}, f32[4,8,128]{2,1,0:T(8,128)S(1)}, u32[]{:S(2)}, u32[]{:S(2)}) %collective-permute-start.15) | collective-permute-done | bytes 16416 | tf_op jit(solution)/shard_map/ppermute | solution.py:357
  72.8 1.1 %shard_map.108 = (f32[6,2048]{1,0:T(8,128)}, f32[6,2048]{1,0:T(8,128)}) custom-call(f32[16,8,128]{2,1,0:T(8,128)S(1)} %get-tuple-element.28.own_ref, f32[26,8,128]{2,1,0:T(8,128)S(1)} %collective-permute-done.12.recv_ref, f32[16,8,128]{2,1,0:T(8,128)S(1)} %get-tuple-element.24.field_ref, f32[6,2048]{1,0:T(8,128)S(1)} %get-tuple-element.30.velocity_ref, ...), custom_call_target="tpu_custom_call" | custom-call | tf_op jit(solution)/shard_map/pallas_call | solution.py:361
  (40 shorter events, 0.2 us)
Async XLA Ops:
  0.6 0.7 copy-start.7
  1.4 0.8 %copy-start.1 = (f32[6,2048]{1,0:T(8,128)S(1)}, f32[6,2048]{1,0:T(8,128)}, u32[]{:S(2)}) copy-start(f32[6,2048]{1,0:T(8,128)} %displace_ref.1) | copy-start | bytes 147460
  2.5 6.8 %collective-permute-start = (f32[4,8,128]{2,1,0:T(8,128)S(1)}, f32[4,8,128]{2,1,0:T(8,128)S(1)}, u32[]{:S(2)}, u32[]{:S(2)}) collective-permute-start(f32[4,8,128]{2,1,0:T(8,128)S(1)} %get-tuple-element.18), channel_id=1, source_target_pairs={{0,4},{4,0},{8,12},{12,8},{1,5},{5,1},{9,13},{13,9},{2,6},{6,2},{1... | collective-permute-start | bytes 49160 | tf_op jit(solution)/shard_map/ppermute | solution.py:312
  2.6 6.7 %collective-permute-start.1 = (f32[4,8,128]{2,1,0:T(8,128)S(1)}, f32[4,8,128]{2,1,0:T(8,128)S(1)}, u32[]{:S(2)}, u32[]{:S(2)}) collective-permute-start(f32[4,8,128]{2,1,0:T(8,128)S(1)} %get-tuple-element.19), channel_id=1, source_target_pairs={{4,8},{8,4},{5,9},{9,5},{6,10},{10,6},{7,11},{11,7},{20,24},{24,20... | collective-permute-start | bytes 49160 | tf_op jit(solution)/shard_map/ppermute | solution.py:312
  7.6 3.3 %copy-start.6 = (s32[6,2048]{1,0:T(8,128)S(1)}, s32[6,2048]{1,0:T(8,128)}, u32[]{:S(2)}) copy-start(s32[6,2048]{1,0:T(8,128)} %param.13) | copy-start | bytes 147460
  9.3 1.7 %copy-start.8 = (f32[8,12,12]{2,0,1:T(8,128)S(1)}, f32[8,12,12]{2,0,1:T(8,128)}, u32[]{:S(2)}) copy-start(f32[8,12,12]{2,0,1:T(8,128)} %param.17) | copy-start | bytes 13828
  9.3 3.9 %collective-permute-start.2 = (f32[6,8,128]{2,1,0:T(8,128)S(1)}, f32[6,8,128]{2,1,0:T(8,128)S(1)}, u32[]{:S(2)}, u32[]{:S(2)}) collective-permute-start(f32[6,8,128]{2,1,0:T(8,128)S(1)} %pad_maximum_fusion.2), channel_id=1, source_target_pairs={{0,2},{2,0},{1,3},{3,1},{4,6},{6,4},{5,7},{7,5},{8,10},{10,8},{9,1... | collective-permute-start | bytes 73736 | tf_op jit(solution)/shard_map/ppermute | solution.py:319
  13.2 1.4 %copy-start = (f32[6,2048]{1,0:T(8,128)S(1)}, f32[6,2048]{1,0:T(8,128)}, u32[]{:S(2)}) copy-start(f32[6,2048]{1,0:T(8,128)} %shape_ref.3) | copy-start | bytes 147460
  13.2 1.4 %collective-permute-start.3 = (f32[26,8,128]{2,1,0:T(8,128)S(1)}, f32[26,8,128]{2,1,0:T(8,128)S(1)}, u32[]{:S(2)}, u32[]{:S(2)}) collective-permute-start(f32[26,8,128]{2,1,0:T(8,128)S(1)} %get-tuple-element.48), channel_id=1, source_target_pairs={{0,1},{1,0},{2,3},{3,2},{4,5},{5,4},{6,7},{7,6},{8,9},{9,8},{10,11... | collective-permute-start | bytes 319496 | tf_op jit(solution)/shard_map/ppermute | solution.py:323
  13.3 1.3 %copy-start.4 = (s32[2048]{0:T(1024)S(1)}, s32[2048]{0:T(1024)}, u32[]{:S(2)}) copy-start(s32[2048]{0:T(1024)} %param.15) | copy-start | bytes 24580
  13.3 1.3 %copy-start.5 = (f32[2048]{0:T(1024)S(1)}, f32[2048]{0:T(1024)}, u32[]{:S(2)}) copy-start(f32[2048]{0:T(1024)} %param.16) | copy-start | bytes 24580
  26.2 1.4 %collective-permute-start.4 = (f32[26,8,128]{2,1,0:T(8,128)S(1)}, f32[26,8,128]{2,1,0:T(8,128)S(1)}, u32[]{:S(2)}, u32[]{:S(2)}) collective-permute-start(f32[26,8,128]{2,1,0:T(8,128)S(1)} %get-tuple-element.22), channel_id=1, source_target_pairs={{0,1},{1,0},{2,3},{3,2},{4,5},{5,4},{6,7},{7,6},{8,9},{9,8},{10,11... | collective-permute-start | bytes 319496 | tf_op jit(solution)/shard_map/ppermute | solution.py:341
  27.7 9.6 %copy-start.2 = (f32[6,2048]{1,0:T(8,128)S(1)}, f32[6,2048]{1,0:T(8,128)}, u32[]{:S(2)}) copy-start(f32[6,2048]{1,0:T(8,128)} %velocity_ref.1) | copy-start | bytes 147460
  27.7 3.9 %collective-permute-start.5 = (f32[6,8,128]{2,1,0:T(8,128)S(1)}, f32[6,8,128]{2,1,0:T(8,128)S(1)}, u32[]{:S(2)}, u32[]{:S(2)}) collective-permute-start(f32[6,8,128]{2,1,0:T(8,128)S(1)} %pad_maximum_fusion.3), channel_id=1, source_target_pairs={{0,2},{2,0},{1,3},{3,1},{4,6},{6,4},{5,7},{7,5},{8,10},{10,8},{9,1... | collective-permute-start | bytes 73736 | tf_op jit(solution)/shard_map/ppermute | solution.py:352
  31.6 4.0 %collective-permute-start.6 = (f32[4,8,128]{2,1,0:T(8,128)S(1)}, f32[4,8,128]{2,1,0:T(8,128)S(1)}, u32[]{:S(2)}, u32[]{:S(2)}) collective-permute-start(f32[4,8,128]{2,1,0:T(8,128)S(1)} %pad_maximum_fusion.6), channel_id=1, source_target_pairs={{0,4},{4,0},{8,12},{12,8},{1,5},{5,1},{9,13},{13,9},{2,6},{6,2},{1... | collective-permute-start | bytes 49160 | tf_op jit(solution)/shard_map/ppermute | solution.py:357
  31.6 5.7 %copy-start.3 = (f32[2048]{0:T(1024)S(1)}, f32[2048]{0:T(1024)}, u32[]{:S(2)}) copy-start(f32[2048]{0:T(1024)} %param.11) | copy-start | bytes 24580
  31.6 5.6 %collective-permute-start.7 = (f32[4,8,128]{2,1,0:T(8,128)S(1)}, f32[4,8,128]{2,1,0:T(8,128)S(1)}, u32[]{:S(2)}, u32[]{:S(2)}) collective-permute-start(f32[4,8,128]{2,1,0:T(8,128)S(1)} %pad_maximum_fusion.7), channel_id=1, source_target_pairs={{4,8},{8,4},{5,9},{9,5},{6,10},{10,6},{7,11},{11,7},{20,24},{24,20... | collective-permute-start | bytes 49160 | tf_op jit(solution)/shard_map/ppermute | solution.py:357
  37.9 6.3 %collective-permute-start.8 = (f32[4,8,128]{2,1,0:T(8,128)S(1)}, f32[4,8,128]{2,1,0:T(8,128)S(1)}, u32[]{:S(2)}, u32[]{:S(2)}) collective-permute-start(f32[4,8,128]{2,1,0:T(8,128)S(1)} %get-tuple-element.25), channel_id=1, source_target_pairs={{0,4},{4,0},{8,12},{12,8},{1,5},{5,1},{9,13},{13,9},{2,6},{6,2},{1... | collective-permute-start | bytes 49160 | tf_op jit(solution)/shard_map/ppermute | solution.py:312
  38.0 5.6 %collective-permute-start.9 = (f32[4,8,128]{2,1,0:T(8,128)S(1)}, f32[4,8,128]{2,1,0:T(8,128)S(1)}, u32[]{:S(2)}, u32[]{:S(2)}) collective-permute-start(f32[4,8,128]{2,1,0:T(8,128)S(1)} %get-tuple-element.26), channel_id=1, source_target_pairs={{4,8},{8,4},{5,9},{9,5},{6,10},{10,6},{7,11},{11,7},{20,24},{24,20... | collective-permute-start | bytes 49160 | tf_op jit(solution)/shard_map/ppermute | solution.py:312
  43.7 0.6 copy-start.9
  44.3 0.7 slice-start
  45.0 3.8 %copy-start.10 = (f32[4,8,128]{2,1,0:T(8,128)S(1)}, f32[4,8,128]{2,1,0:T(8,128)}, u32[]{:S(2)}) copy-start(f32[4,8,128]{2,1,0:T(8,128)} %copy-done.9) | copy-start | bytes 49156
  45.0 3.8 %collective-permute-start.10 = (f32[6,8,128]{2,1,0:T(8,128)S(1)}, f32[6,8,128]{2,1,0:T(8,128)S(1)}, u32[]{:S(2)}, u32[]{:S(2)}) collective-permute-start(f32[6,8,128]{2,1,0:T(8,128)S(1)} %pad_maximum_fusion.4), channel_id=1, source_target_pairs={{0,2},{2,0},{1,3},{3,1},{4,6},{6,4},{5,7},{7,5},{8,10},{10,8},{9,1... | collective-permute-start | bytes 73736 | tf_op jit(solution)/shard_map/ppermute | solution.py:319
  48.8 1.4 %collective-permute-start.11 = (f32[26,8,128]{2,1,0:T(8,128)S(1)}, f32[26,8,128]{2,1,0:T(8,128)S(1)}, u32[]{:S(2)}, u32[]{:S(2)}) collective-permute-start(f32[26,8,128]{2,1,0:T(8,128)S(1)} %get-tuple-element.41), channel_id=1, source_target_pairs={{0,1},{1,0},{2,3},{3,2},{4,5},{5,4},{6,7},{7,6},{8,9},{9,8},{10,11... | collective-permute-start | bytes 319496 | tf_op jit(solution)/shard_map/ppermute | solution.py:323
  61.8 1.4 %collective-permute-start.12 = (f32[26,8,128]{2,1,0:T(8,128)S(1)}, f32[26,8,128]{2,1,0:T(8,128)S(1)}, u32[]{:S(2)}, u32[]{:S(2)}) collective-permute-start(f32[26,8,128]{2,1,0:T(8,128)S(1)} %get-tuple-element.29), channel_id=1, source_target_pairs={{0,1},{1,0},{2,3},{3,2},{4,5},{5,4},{6,7},{7,6},{8,9},{9,8},{10,11... | collective-permute-start | bytes 319496 | tf_op jit(solution)/shard_map/ppermute | solution.py:341
  63.2 3.9 %collective-permute-start.13 = (f32[6,8,128]{2,1,0:T(8,128)S(1)}, f32[6,8,128]{2,1,0:T(8,128)S(1)}, u32[]{:S(2)}, u32[]{:S(2)}) collective-permute-start(f32[6,8,128]{2,1,0:T(8,128)S(1)} %pad_maximum_fusion.5), channel_id=1, source_target_pairs={{0,2},{2,0},{1,3},{3,1},{4,6},{6,4},{5,7},{7,5},{8,10},{10,8},{9,1... | collective-permute-start | bytes 73736 | tf_op jit(solution)/shard_map/ppermute | solution.py:352
  67.1 3.9 %collective-permute-start.14 = (f32[4,8,128]{2,1,0:T(8,128)S(1)}, f32[4,8,128]{2,1,0:T(8,128)S(1)}, u32[]{:S(2)}, u32[]{:S(2)}) collective-permute-start(f32[4,8,128]{2,1,0:T(8,128)S(1)} %pad_maximum_fusion.8), channel_id=1, source_target_pairs={{0,4},{4,0},{8,12},{12,8},{1,5},{5,1},{9,13},{13,9},{2,6},{6,2},{1... | collective-permute-start | bytes 49160 | tf_op jit(solution)/shard_map/ppermute | solution.py:357
  67.1 5.6 %collective-permute-start.15 = (f32[4,8,128]{2,1,0:T(8,128)S(1)}, f32[4,8,128]{2,1,0:T(8,128)S(1)}, u32[]{:S(2)}, u32[]{:S(2)}) collective-permute-start(f32[4,8,128]{2,1,0:T(8,128)S(1)} %pad_maximum_fusion.9), channel_id=1, source_target_pairs={{4,8},{8,4},{5,9},{9,5},{6,10},{10,6},{7,11},{11,7},{20,24},{24,20... | collective-permute-start | bytes 49160 | tf_op jit(solution)/shard_map/ppermute | solution.py:357

commit v3 on v2

v3 whole, which is shorter than its diff:
```python
import functools

import jax
import jax.numpy as jnp
from jax import lax
from jax.experimental import pallas as pl
from jax.experimental.pallas import tpu as pltpu
from jax.sharding import PartitionSpec as P

STEPS = 2
F32 = jnp.float32
BF16 = jnp.bfloat16
VMEM = pl.BlockSpec(memory_space=pltpu.VMEM)


def lane_pick(row, lanes):
    return jnp.take_along_axis(row, lanes, axis=1, mode="promise_in_bounds")


def spread(row):
    return jnp.broadcast_to(row, (8, 128))


def split(value):
    high = value.astype(BF16).astype(F32)
    return high, value - high


def padded(tile):
    return jnp.concatenate([tile, jnp.zeros((8 - tile.shape[0], 128), F32)], axis=0)


def pick_lists(field_ref, picks_ref, outs):
    picks = [picks_ref[0:8, :], picks_ref[8:16, :]]
    lanes = [p & 127 for p in picks]
    rows = [lax.shift_right_logical(p, 7) for p in picks]
    found = [[jnp.zeros((8, 128), F32) for _ in range(2)] for _ in range(6)]
    for tile in range(16):
        hit = [r == tile for r in rows]
        for c in range(6):
            row = spread(field_ref[tile, c : c + 1, :])
            for v in range(2):
                found[c][v] = jnp.where(hit[v], lane_pick(row, lanes[v]), found[c][v])
    for c in range(8):
        both = jnp.concatenate(found[c], axis=0) if c < 6 else jnp.zeros((16, 128), F32)
        at = 0
        for out in outs:
            size = out.shape[0]
            out[:, c, :] = both[at : at + size, :]
            at += size


def lists_kernel(U, odd_ref, displace_ref, send_ref, field_ref, picks_ref, *outs):
    r_odd, c_odd = odd_ref[0], odd_ref[1]
    swap = [jnp.where(r_odd == 0, send_ref[2 * t], send_ref[2 - 2 * t]) for t in (1, 0)] + [send_ref[1]]
    at = 0
    for t in range(3):
        lists = [swap[t][1:2]]
        lists += [jnp.where(c_odd == 0, swap[t][2 * u : 2 * u + 1], swap[t][2 - 2 * u : 3 - 2 * u]) for u in (1, 0)]
        for u in range(U):
            if t < 2 or u > 0:
                for half in range(2):
                    picks_ref[at : at + 1, :] = lists[u][:, half * 128 : (half + 1) * 128]
                    at += 1
    if at < 16:
        picks_ref[at:16, :] = jnp.zeros((16 - at, 128), jnp.int32)
    for tile in range(16):
        field_ref[tile] = padded(displace_ref[:, tile * 128 : (tile + 1) * 128])
    pick_lists(field_ref, picks_ref, outs)


def one_hot(lanes):
    lanes = jnp.broadcast_to(lanes.astype(F32), (16, 128)).astype(BF16)
    iota = lax.broadcasted_iota(jnp.int32, (16, 128), 0).astype(F32)
    one, zero = jnp.ones((16, 128), BF16), jnp.zeros((16, 128), BF16)
    return jnp.concatenate(
        [jnp.where((iota + 16.0 * at).astype(BF16) == lanes, one, zero) for at in range(16)], axis=0
    )


def times_one_hot(values, hot):
    return lax.dot_general(values, hot, (((1,), (1,)), ((), ())), preferred_element_type=F32)


def build_hot(e, quad, slots_ref, hot_ref):
    for bb in range(4):
        b = quad * 4 + bb
        for k in range(3):
            slot = slots_ref[3 * e + k : 3 * e + k + 1, b * 128 : (b + 1) * 128]
            at = (e * 48 + b * 3 + k) * 128
            hot_ref[:, at : at + 128] = one_hot(slot & 255)


def fill_table(tiles, table_ref):
    low_at = len(tiles) * 8
    for row in range(0, len(tiles), 2):
        for half in range(2):
            both = jnp.concatenate([tiles[row](half), tiles[row + 1](half)], axis=0)
            for base, piece in zip((0, low_at), split(both)):
                table_ref[base + row * 8 : base + row * 8 + 16, half * 128 : (half + 1) * 128] = piece.astype(BF16)


def gather_step(e, quad, first, rows, table_ref, hot_ref, x_refs, slots_ref, shape_ref, vec_ref, base_ref=None):
    low_at = rows * 8
    start = (4 * e + quad) * 1536
    x_ref = x_refs.at[quad % 2]
    x_ref[...] = jnp.dot(table_ref[...], hot_ref[:, start : start + 1536], preferred_element_type=F32)
    for bb in range(4):
        b = quad * 4 + bb
        cols = slice(b * 128, (b + 1) * 128)
        end = jnp.zeros((8, 128), F32) if base_ref is None else base_ref[:, cols]
        for k in range(3):
            j = 3 * e + k
            hi = spread(lax.shift_right_logical(slots_ref[j : j + 1, cols], 8))
            at = (bb * 3 + k) * 128
            found = jnp.zeros((8, 128), F32)
            for row in range(rows):
                high = x_ref[row * 8 : row * 8 + 8, at : at + 128]
                low = x_ref[low_at + row * 8 : low_at + row * 8 + 8, at : at + 128]
                found = jnp.where(hi == first + row, high + low, found)
            end += found * spread(shape_ref[j : j + 1, cols])
        vec_ref[:, cols] = end


def scatter_step(e, quad, first, rows, force_ref, a_refs, acc_ref, hot_ref, slots_ref, shape_ref, weight_ref):
    low_at = rows * 8
    start = (4 * e + quad) * 1536
    a_ref = a_refs.at[quad % 2]
    for bb in range(4):
        b = quad * 4 + bb
        cols = slice(b * 128, (b + 1) * 128)
        force = force_ref[e * 8 : e * 8 + 8, cols]
        weight = weight_ref[b : b + 1, :]
        for k in range(3):
            j = 3 * e + k
            at = (bb * 3 + k) * 128
            hi = spread(lax.shift_right_logical(slots_ref[j : j + 1, cols], 8))
            pieces = split(force * spread(shape_ref[j : j + 1, cols] * weight))
            for row in range(0, rows, 2):
                hit = [hi == first + row, hi == first + row + 1]
                for base, piece in zip((0, low_at), pieces):
                    a_ref[base + row * 8 : base + row * 8 + 16, at : at + 128] = jnp.concatenate(
                        [jnp.where(hit[0], piece, 0.0), jnp.where(hit[1], piece, 0.0)], axis=0
                    ).astype(BF16)
    acc_ref[...] += times_one_hot(a_ref[...], hot_ref[:, start : start + 1536])


def local_gather_kernel(e, build, *refs):
    if build:
        field_ref, other_ref, slots_ref, shape_ref, vec_ref, table_ref, x_refs, hot_ref = refs
    else:
        field_ref, other_ref, slots_ref, shape_ref, hot_ref, vec_ref, table_ref, x_refs = refs
    tiles = [lambda half, k=k: field_ref[2 * k + half] for k in range(8)]
    tiles += [lambda half, k=k: other_ref[2 * k + half] for k in range(8)]
    fill_table(tiles, table_ref)
    for quad in range(4):
        if build:
            build_hot(e, quad, slots_ref, hot_ref)
        gather_step(e, quad, 0, 16, table_ref, hot_ref, x_refs, slots_ref, shape_ref, vec_ref)


def near_kernel(n, kinds, build, *refs):
    vec0_ref, vec1_ref, near_ref, other_ref, slots_ref, shape_ref, kind_ref, weight_ref, stiff_ref = refs[:9]
    if build:
        own_near_ref, send_ref, force_ref, hot_ref = refs[9:13]
    else:
        hot_ref, own_near_ref, send_ref, force_ref = refs[9:13]
    table_ref, x_refs, vec_ref, cat_ref, kinds_ref, a_refs, acc_ref = refs[13:]
    tiles = [lambda half, k=k: near_ref[2 * k + half] for k in range(n)]
    tiles += [lambda half, k=k: other_ref[2 * k + half] for k in range(n)]
    fill_table(tiles, table_ref)
    for e, base_ref in enumerate((vec0_ref, vec1_ref)):
        for quad in range(4):
            if build:
                build_hot(e, quad, slots_ref, hot_ref)
            gather_step(
                e, quad, 16, 2 * n, table_ref, hot_ref, x_refs, slots_ref, shape_ref, vec_ref.at[e], base_ref
            )

    v1, rest = split(jnp.concatenate([vec_ref[0], vec_ref[1]], axis=0))
    v2, v3 = split(rest)
    for at, piece in enumerate((v1, v2, v1, v2, v3, v1)):
        cat_ref[at * 16 : (at + 1) * 16, :] = piece.astype(BF16)
    s1, rest = split(stiff_ref[...])
    s2, s3 = split(rest)
    block = lax.broadcasted_iota(jnp.int32, s1.shape, 1) // 16
    stiff = jnp.where((block == 2) | (block == 3), s2, jnp.where(block == 5, s3, s1)).astype(BF16)
    kinds_ref[...] = jnp.dot(stiff, cat_ref[...], preferred_element_type=F32)
    for b in range(16):
        cols = slice(b * 128, (b + 1) * 128)
        kind = spread(kind_ref[b : b + 1, :])
        for e in range(2):
            force = jnp.zeros((8, 128), F32)
            for t in range(kinds):
                force = jnp.where(kind == t, kinds_ref[t * 16 + e * 8 : t * 16 + e * 8 + 8, cols], force)
            force_ref[e * 8 : (e + 1) * 8, cols] = force

    acc_ref[...] = jnp.zeros_like(acc_ref)
    for e in range(2):
        for quad in range(4):
            scatter_step(e, quad, 16, 2 * n, force_ref, a_refs, acc_ref, hot_ref, slots_ref, shape_ref, weight_ref)
    for row in range(2 * n):
        total = acc_ref[row * 8 : row * 8 + 8, :] + acc_ref[(2 * n + row) * 8 : (2 * n + row) * 8 + 8, :]
        for half in range(2):
            out, at = (own_near_ref, row) if row < n else (send_ref, row - n)
            out[2 * at + half] = total[:, half * 128 : (half + 1) * 128]


def local_scatter_kernel(force_ref, hot_ref, slots_ref, shape_ref, weight_ref, own_ref, send_ref, a_refs, acc_ref):
    acc_ref[...] = jnp.zeros_like(acc_ref)
    for e in range(2):
        for quad in range(4):
            scatter_step(e, quad, 0, 16, force_ref, a_refs, acc_ref, hot_ref, slots_ref, shape_ref, weight_ref)
    for row in range(16):
        total = acc_ref[row * 8 : row * 8 + 8, :] + acc_ref[128 + row * 8 : 128 + row * 8 + 8, :]
        for half in range(2):
            out, at = (own_ref, row) if row < 8 else (send_ref, row - 8)
            out[2 * at + half] = total[:, half * 128 : (half + 1) * 128]


def update_kernel(n_returns, last, own_ref, recv_ref, field_ref, velocity_ref, mass_ref, picks_ref, *refs):
    returns, refs = refs[:n_returns], refs[n_returns:]
    new_field_ref, new_velocity_ref = refs[0], refs[1]
    a_ref, b_ref = refs[-2], refs[-1]
    outs = refs[2:-2]
    p = 0
    for ret in returns:
        for tile in range(ret.shape[0]):
            pick = picks_ref[p : p + 1, :]
            hi = spread(lax.shift_right_logical(pick, 8))
            at = p * 128
            for base, piece in zip((0, 64), split(ret[tile])):
                a_ref[base : base + 64, at : at + 128] = jnp.concatenate(
                    [jnp.where(hi == row, piece, 0.0) for row in range(8)], axis=0
                ).astype(BF16)
            b_ref[:, at : at + 128] = one_hot(pick & 255)
            p += 1
    back = times_one_hot(a_ref[...], b_ref[...])
    back = back[:64] + back[64:]
    for tile in range(16):
        row, half = tile // 2, tile % 2
        cols = slice(tile * 128, (tile + 1) * 128)
        force = own_ref[tile] + recv_ref[tile] + back[row * 8 : row * 8 + 8, half * 128 : (half + 1) * 128]
        velocity = 0.98 * velocity_ref[:, cols] - 0.2 * force[0:6] / mass_ref[:, cols]
        new_velocity_ref[:, cols] = velocity
        field = field_ref[tile][0:6] + 0.2 * velocity
        if last:
            new_field_ref[:, cols] = field
        else:
            new_field_ref[tile] = padded(field)
    if not last:
        pick_lists(new_field_ref, picks_ref, outs)


def pairs(count, shift):
    out = []
    for i in range(shift, count - 1, 2):
        out += [(i, i + 1), (i + 1, i)]
    return out


def f32_out(*shape):
    return jax.ShapeDtypeStruct(shape, F32)


def params():
    return pltpu.CompilerParams(vmem_limit_bytes=24 * 1024 * 1024)


def cost(us):
    return pl.CostEstimate(flops=us * 10**9, bytes_accessed=us * 10**6, transcendentals=0)


def shards(
    displace,
    velocity,
    nodal_mass,
    send_list,
    beam_slots,
    shape_values,
    beam_kind,
    cluster_weight,
    stiffness,
):
    list_len = send_list.shape[2]
    cols = lax.axis_size("cols")
    U = 2 if cols <= 2 else 3
    n = 3 * U - 1
    kinds = stiffness.shape[0]
    r_odd = lax.axis_index("rows") % 2
    c_odd = lax.axis_index("cols") % 2
    s = lax.axis_index("sub")
    row_perm = [pairs(lax.axis_size("rows"), 0), pairs(lax.axis_size("rows"), 1)]
    col_perm = [pairs(cols, 0), pairs(cols, 1)][: U - 1]
    sub_perm = [(0, 1), (1, 0)]

    slots = beam_slots
    hi = slots >> 8
    remote = hi - 16
    sender = (remote >= 9).astype(jnp.int32)
    direction = remote - 9 * sender
    a = (direction >= 3).astype(jnp.int32) + (direction >= 6).astype(jnp.int32)
    b = direction - 3 * a
    a = jnp.where(r_odd == 0, a, 2 - a)
    b = jnp.where(c_odd == 0, b, 2 - b)
    t = jnp.where(a == 1, 2, a >> 1)
    u = jnp.where(b == 1, 0, (b >> 1) + 1)
    order = jnp.where(t == 2, 2 * U + u - 1, t * U + u)
    rel_near = 16 + n * (sender ^ s) + order
    rel_near = jnp.where(u < U, rel_near, 64)
    rel = jnp.where(hi < 16, hi ^ (8 * s), rel_near)
    slots = rel * 256 + (slots & 255)

    kind = beam_kind.reshape(16, 128)
    weight = cluster_weight.reshape(16, 128)
    stiff = jnp.pad(stiffness.reshape(kinds, 2, 6, 2, 6), ((0, 0), (0, 0), (0, 2), (0, 0), (0, 2)))
    stiff = jnp.tile(stiff.reshape(kinds * 16, 16), (1, 6))
    mass = nodal_mass.reshape(1, -1)

    speed = velocity
    list_outs = [f32_out(2 * U, 8, 128), f32_out(2 * U, 8, 128), f32_out(2 * U - 2, 8, 128)]
    odd = jnp.stack([r_odd, c_odd]).astype(jnp.int32)
    field, picks, *outgoing = pl.pallas_call(
        functools.partial(lists_kernel, U),
        out_shape=[f32_out(16, 8, 128), jax.ShapeDtypeStruct((16, 128), jnp.int32)] + list_outs,
        in_specs=[pl.BlockSpec(memory_space=pltpu.SMEM), VMEM, VMEM],
        out_specs=[VMEM] * 5,
        compiler_params=params(),
    )(odd, displace, send_list)
    hot = None
    tall = 32 * n
    for step in range(STEPS):
        other = lax.ppermute(field, "sub", sub_perm)

        build = hot is None

        def local_gather(e):
            return pl.pallas_call(
                functools.partial(local_gather_kernel, e, build),
                out_shape=f32_out(8, 2048),
                in_specs=[VMEM] * (4 if build else 5),
                out_specs=VMEM,
                scratch_shapes=[pltpu.VMEM((256, 256), BF16), pltpu.VMEM((2, 256, 1536), F32)]
                + ([pltpu.VMEM((256, 12288), BF16)] if build else []),
                compiler_params=params(),
                cost_estimate=cost(2),
            )(field, other, slots, shape_values, *([] if build else [hot]))

        to_rows, own_row = outgoing[:2], outgoing[2]
        arrived = [lax.ppermute(x, "rows", perm) for x, perm in zip(to_rows, row_perm)]
        vec0 = local_gather(0)
        arrived[0], arrived[1], vec0 = lax.optimization_barrier((arrived[0], arrived[1], vec0))
        near = [[x[0:2]] for x in arrived] + [[]]
        for u in range(1, U):
            at = 2 * u
            message = jnp.concatenate(
                [arrived[0][at : at + 2], arrived[1][at : at + 2], own_row[at - 2 : at]], axis=0
            )
            got = lax.ppermute(message, "cols", col_perm[u - 1])
            for t in range(3):
                near[t].append(got[2 * t : 2 * t + 2])
        near = jnp.concatenate(near[0] + near[1] + near[2], axis=0)
        vec1 = local_gather(1)
        near, vec1 = lax.optimization_barrier((near, vec1))
        near_other = lax.ppermute(near, "sub", sub_perm)
        own_near, near_send, force, *made = pl.pallas_call(
            functools.partial(near_kernel, n, kinds, build),
            out_shape=[f32_out(2 * n, 8, 128), f32_out(2 * n, 8, 128), f32_out(16, 2048)]
            + ([jax.ShapeDtypeStruct((256, 12288), BF16)] if build else []),
            in_specs=[VMEM] * (9 if build else 10),
            out_specs=[VMEM] * (4 if build else 3),
            scratch_shapes=[
                pltpu.VMEM((tall, 256), BF16),
                pltpu.VMEM((2, tall, 1536), F32),
                pltpu.VMEM((2, 8, 2048), F32),
                pltpu.VMEM((96, 2048), BF16),
                pltpu.VMEM((16 * kinds, 2048), F32),
                pltpu.VMEM((2, tall, 1536), BF16),
                pltpu.VMEM((tall, 256), F32),
            ],
            compiler_params=params(),
            cost_estimate=cost(5),
        )(vec0, vec1, near, near_other, slots, shape_values, kind, weight, stiff, *([] if build else [hot]))
        hot = made[0] if build else hot

        def local_scatter():
            return pl.pallas_call(
                local_scatter_kernel,
                out_shape=[f32_out(16, 8, 128)] * 2,
                in_specs=[VMEM] * 5,
                out_specs=[VMEM] * 2,
                scratch_shapes=[pltpu.VMEM((2, 256, 1536), BF16), pltpu.VMEM((256, 256), F32)],
                compiler_params=params(),
                cost_estimate=cost(3),
            )(force, hot, slots, shape_values, weight)

        total = own_near + lax.ppermute(near_send, "sub", sub_perm)

        def listed(t, u):
            at = 2 * (t * U + u) if t < 2 else 2 * (2 * U + u - 1)
            return total[at : at + 2]

        back_rows = [[listed(0, 0)], [listed(1, 0)]]
        back_own = []
        for u in range(1, U):
            message = jnp.concatenate([listed(t, u) for t in range(3)], axis=0)
            got = lax.ppermute(message, "cols", col_perm[u - 1])
            if u == 1:
                own, local_send = local_scatter()
                got, local_send = lax.optimization_barrier((got, local_send))
                recv = lax.ppermute(local_send, "sub", sub_perm)
            back_rows[0].append(got[0:2])
            back_rows[1].append(got[2:4])
            back_own.append(got[4:6])
        returns = [
            lax.ppermute(jnp.concatenate(x, axis=0), "rows", perm)
            for x, perm in zip(back_rows, row_perm)
        ] + [jnp.concatenate(back_own, axis=0)]
        last = step == STEPS - 1
        outs = pl.pallas_call(
            functools.partial(update_kernel, 3, last),
            out_shape=[f32_out(6, 2048)] * 2 if last else [f32_out(16, 8, 128), f32_out(6, 2048)] + list_outs,
            in_specs=[VMEM] * 9,
            out_specs=[VMEM] * (2 if last else 5),
            scratch_shapes=[pltpu.VMEM((128, 256 * n), BF16), pltpu.VMEM((256, 256 * n), BF16)],
            compiler_params=params(),
        )(own, recv, field, speed, mass, picks, *returns)
        field, speed = outs[:2]
        outgoing = outs[2:]
    return field, speed


def solution(mesh):
    whole = ("groups", "rows", "cols", "sub")
    in_specs = (
        P(None, whole),
        P(None, whole),
        P(whole),
        P("rows", "cols", ("groups", "sub")),
        P(None, whole),
        P(None, whole),
        P(whole),
        P(whole),
        P(),
    )
    out_specs = (P(None, whole), P(None, whole))
    return jax.shard_map(shards, mesh=mesh, in_specs=in_specs, out_specs=out_specs, check_vma=False)
```

time: 74.7 us -> 61 us (0.82)
  starting transfers between devices: 23.7 us -> 17.7 us
  Pallas kernels: 25.2 us -> 21.2 us
  waiting for transfers between devices: 20 us -> 16.4 us
  other arithmetic: 0.17 us -> 1.08 us
    ppermute x4, waiting for transfers between devices: 8.4 us -> 3.35 us  [shards(): got = lax.ppermute(message, 'cols', col_perm[u - 1])]
    pallas_call x3 -> x9, Pallas kernels: 23.5 us -> 19.4 us  [the longest x2 8.35 us: shards(): pl.pallas_call(functools.partial(near_kernel, n, kinds, build), out_shape...]
    ppermute x4, waiting for transfers between devices: 3.39 us -> 6.84 us  [shards(): lax.ppermute(jnp.concatenate(x, axis=0), 'rows', perm)]
    ppermute x4, starting transfers between devices: 7.85 us -> 4.5 us  [shards(): lax.ppermute(jnp.concatenate(x, axis=0), 'rows', perm)]
    ppermute x4, starting transfers between devices: 9.1 us -> 7.56 us  [shards(): lax.ppermute(x, 'rows', perm)]
    ppermute x4, starting transfers between devices: 6.16 us -> 4.77 us  [shards(): got = lax.ppermute(message, 'cols', col_perm[u - 1])]
    ppermute x4, waiting for transfers between devices: 3.37 us -> 2.22 us  [shards(): lax.ppermute(x, 'rows', perm)]
    ppermute x4 -> x8, waiting for transfers between devices: 4.88 us -> 3.99 us  [the longest x2 2.12 us: shards(): total = own_near + lax.ppermute(near_send, 'sub', sub_perm)]
  transfers between devices with their start and end apart: 16 -> 20, of which waited for: 12 -> 14; matrix products, arithmetic and copies ran while one was open for 1% -> 3% of each run, Pallas kernels for 0% -> 17%
where the time goes in v3:
time: 61 us; the launch traced here: 60.6 us
  Pallas kernels  21.2 us (35%)
  starting transfers between devices  17.7 us (29%)
  waiting for transfers between devices  16.4 us (27%)
  local copies, waits for them, and re-layouts  3.25 us (5%)
  other arithmetic  1.08 us (2%)
  between operations  1.04 us (2%)
    pallas_call x2, Pallas kernels, shards(): pl.pallas_call(functools.partial(near_kernel, n, kinds, build), out_shape...  8.35 us
    ppermute x4, starting transfers between devices, shards(): lax.ppermute(x, 'rows', perm)  7.56 us
    ppermute x4, waiting for transfers between devices, shards(): lax.ppermute(jnp.concatenate(x, axis=0), 'rows', perm)  6.84 us
    pallas_call x2, Pallas kernels, local_scatter(): pl.pallas_call(local_scatter_kernel, out_shape=[f32_out(16, 8, 128)] * 2,...  5.93 us
    ppermute x4, starting transfers between devices, shards(): got = lax.ppermute(message, 'cols', col_perm[u - 1])  4.77 us
    ppermute x4, starting transfers between devices, shards(): lax.ppermute(jnp.concatenate(x, axis=0), 'rows', perm)  4.5 us
    pallas_call x4, Pallas kernels, local_gather(): pl.pallas_call(functools.partial(local_gather_kernel, e, build), out_shap...  4.28 us
    ppermute x4, waiting for transfers between devices, shards(): got = lax.ppermute(message, 'cols', col_perm[u - 1])  3.35 us
  transfers between devices with their start and end apart: 20, of which 14 were waited for; matrix products, arithmetic and copies ran while one was open for 3% of the time, Pallas kernels for 17%

profile of v3, /device:TPU:8, one launch (start us, length us, event | category | flops | bytes accessed | tf_op | source)
XLA Modules:
  0.0 60.6 jit_solution(1365183433093643253)
XLA Ops:
  0.6 0.1 pad_add_fusion.odd_ref
  0.7 0.8 %copy-done.1 = f32[6,2048]{1,0:T(8,128)S(1)} copy-done((f32[6,2048]{1,0:T(8,128)S(1)}, f32[6,2048]{1,0:T(8,128)}, u32[]{:S(2)}) %copy-start.1) | copy-done | bytes 49176
  1.6 0.7 %copy-done.3 = s32[3,3,256]{2,1,0:T(4,128)S(1)} copy-done((s32[3,3,256]{2,1,0:T(4,128)S(1)}, s32[3,3,256]{2,1,0:T(4,128)}, u32[]{:S(2)}) %copy-start.3) | copy-done | bytes 9240
  2.3 0.8 %shard_map.104 = (f32[16,8,128]{2,1,0:T(8,128)S(1)}, s32[16,128]{1,0:T(8,128)S(1)}, f32[4,8,128]{2,1,0:T(8,128)S(1)}, f32[4,8,128]{2,1,0:T(8,128)S(1)}, f32[2,8,128]{2,1,0:T(8,128)S(1)}) custom-call(s32[2]{0:T(128)S(1)} %pad_add_fusion.odd_ref, f32[6,2048]{1,0:T(8,128)S(1)} %copy-done.1, s32[3,3,256]{2,1,0:T(4,128)S(1)} %copy-done.3), custom_call_target="tpu_custom_call" | custom-call | tf_op jit(solution)/shard_map/pallas_call | solution.py:323
  3.1 0.1 collective-permute-start
  3.2 5.0 %collective-permute-start.1 = (f32[4,8,128]{2,1,0:T(8,128)S(1)}, f32[4,8,128]{2,1,0:T(8,128)S(1)}, u32[]{:S(2)}, u32[]{:S(2)}) collective-permute-start(f32[4,8,128]{2,1,0:T(8,128)S(1)} %get-tuple-element.38), channel_id=1, source_target_pairs={{4,8},{8,4},{5,9},{9,5},{6,10},{10,6},{7,11},{11,7},{20,24},{24,20... | collective-permute-start | bytes 49160 | tf_op jit(solution)/shard_map/ppermute | solution.py:350
  8.2 0.1 collective-permute-start.2
  8.3 0.9 %and_add_fusion.refs_2_.refs_4_.slots_ref = s32[6,2048]{1,0:T(8,128)S(1)} fusion(s32[6,2048]{1,0:T(8,128)} %param.13, s32[]{:T(128)S(6)} %axis_index.38, s32[]{:T(128)S(6)} %mul.24, pred[]{:T(512)S(6)} %eq.20, pred[]{:T(512)S(6)} %eq.18), kind=kLoop, calls=%fused_computation.2 | loop fusion | flops 503808 | bytes 98314 | tf_op jit(solution)/shard_map/add | solution.py:312
  9.3 0.3 collective-permute-done.2.refs_1_
  9.6 0.8 %copy-done.4 = f32[6,2048]{1,0:T(8,128)S(1)} copy-done((f32[6,2048]{1,0:T(8,128)S(1)}, f32[6,2048]{1,0:T(8,128)}, u32[]{:S(2)}) %copy-start.4) | copy-done | bytes 49176
  10.4 1.1 %shard_map.105.refs_0_ = f32[8,2048]{1,0:T(8,128)S(1)} custom-call(f32[16,8,128]{2,1,0:T(8,128)S(1)} %get-tuple-element.39.refs_0_.field_ref, f32[16,8,128]{2,1,0:T(8,128)S(1)} %collective-permute-done.2.refs_1_, s32[6,2048]{1,0:T(8,128)S(1)} %and_add_fusion.refs_2_.refs_4_.slots_ref, f32[6,2048]{1,0:T(8,128)S(1)} %copy-done.4), custom_call_target="tpu_custom_call" | custom-call | flops 2000000000 | bytes 2000000 | tf_op jit(solution)/shard_map/pallas_call | solution.py:338
  11.5 0.0 collective-permute-done
  11.6 0.0 collective-permute-done.1
  11.6 1.6 %collective-permute-start.3 = (f32[6,8,128]{2,1,0:T(8,128)S(1)}, f32[6,8,128]{2,1,0:T(8,128)S(1)}, u32[]{:S(2)}, u32[]{:S(2)}) collective-permute-start(f32[6,8,128]{2,1,0:T(8,128)S(1)} %pad_maximum_fusion.2), channel_id=1, source_target_pairs={{0,2},{2,0},{1,3},{3,1},{4,6},{6,4},{5,7},{7,5},{8,10},{10,8},{9,1... | collective-permute-start | bytes 73736 | tf_op jit(solution)/shard_map/ppermute | solution.py:359
  13.2 1.1 %shard_map.106.refs_1_ = f32[8,2048]{1,0:T(8,128)S(1)} custom-call(f32[16,8,128]{2,1,0:T(8,128)S(1)} %get-tuple-element.39.refs_0_.field_ref, f32[16,8,128]{2,1,0:T(8,128)S(1)} %collective-permute-done.2.refs_1_, s32[6,2048]{1,0:T(8,128)S(1)} %and_add_fusion.refs_2_.refs_4_.slots_ref, f32[6,2048]{1,0:T(8,128)S(1)} %copy-done.4), custom_call_target="tpu_custom_call" | custom-call | flops 2000000000 | bytes 2000000 | tf_op jit(solution)/shard_map/pallas_call | solution.py:338
  14.3 1.2 %collective-permute-done.3 = f32[6,8,128]{2,1,0:T(8,128)S(1)} collective-permute-done((f32[6,8,128]{2,1,0:T(8,128)S(1)}, f32[6,8,128]{2,1,0:T(8,128)S(1)}, u32[]{:S(2)}, u32[]{:S(2)}) %collective-permute-start.3) | collective-permute-done | bytes 24608 | tf_op jit(solution)/shard_map/ppermute | solution.py:359
  15.5 0.1 collective-permute-start.4
  15.6 0.0 copy-done.8
  15.6 0.1 reshape.22
  15.7 0.3 copy.14
  16.1 0.2 tile.10
  16.3 0.1 copy.12.refs_8_
  16.4 0.4 collective-permute-done.4.refs_3_
  16.8 0.0 copy-done.7
  16.8 4.8 %shard_map.107 = (f32[10,8,128]{2,1,0:T(8,128)S(1)}, f32[10,8,128]{2,1,0:T(8,128)S(1)}, f32[16,2048]{1,0:T(8,128)S(1)}, bf16[256,12288]{1,0:T(8,128)(2,1)S(1)}) custom-call(f32[8,2048]{1,0:T(8,128)S(1)} %shard_map.105.refs_0_, f32[8,2048]{1,0:T(8,128)S(1)} %shard_map.106.refs_1_, f32[10,8,128]{2,1,0:T(8,128)S(1)} %pad_maximum_fusion.refs_2_, ...), custom_call_target="tpu_custom_call" | custom-call | flops 5000000000 | bytes 5000000 | tf_op jit(solution)/shard_map/pallas_call | solution.py:366
  21.6 0.0 copy-start
  21.6 0.0 copy-start.2
  21.6 0.2 collective-permute-start.5
  21.8 1.1 %collective-permute-done.5 = f32[10,8,128]{2,1,0:T(8,128)S(1)} collective-permute-done((f32[10,8,128]{2,1,0:T(8,128)S(1)}, f32[10,8,128]{2,1,0:T(8,128)S(1)}, u32[]{:S(2)}, u32[]{:S(2)}) %collective-permute-start.5) | collective-permute-done | bytes 40992 | tf_op jit(solution)/shard_map/ppermute | solution.py:397
  22.9 1.6 %collective-permute-start.6 = (f32[6,8,128]{2,1,0:T(8,128)S(1)}, f32[6,8,128]{2,1,0:T(8,128)S(1)}, u32[]{:S(2)}, u32[]{:S(2)}) collective-permute-start(f32[6,8,128]{2,1,0:T(8,128)S(1)} %pad_maximum_fusion.3), channel_id=1, source_target_pairs={{0,2},{2,0},{1,3},{3,1},{4,6},{6,4},{5,7},{7,5},{8,10},{10,8},{9,1... | collective-permute-start | bytes 73736 | tf_op jit(solution)/shard_map/ppermute | solution.py:407
  24.5 3.0 %shard_map.108 = (f32[16,8,128]{2,1,0:T(8,128)S(1)}, f32[16,8,128]{2,1,0:T(8,128)S(1)}) custom-call(f32[16,2048]{1,0:T(8,128)S(1)} %get-tuple-element.46.force_ref, bf16[256,12288]{1,0:T(8,128)(2,1)S(1)} %get-tuple-element.47.hot_ref.refs_4_.refs_9_, s32[6,2048]{1,0:T(8,128)S(1)} %and_add_fusion.refs_2_.refs_4_.slots_ref, f32[6,2048]{1,0:T(8,128)S(1)} %copy-done.5, ...), custom_call_target="tpu_custom_call" | custom-call | flops 3000000000 | bytes 3000000 | tf_op jit(solution)/shard_map/pallas_call | solution.py:387
  27.4 0.0 collective-permute-done.6
  27.5 0.1 collective-permute-start.8
  27.5 0.1 collective-permute-start.7
  27.6 2.2 %collective-permute-start.9 = (f32[4,8,128]{2,1,0:T(8,128)S(1)}, f32[4,8,128]{2,1,0:T(8,128)S(1)}, u32[]{:S(2)}, u32[]{:S(2)}) collective-permute-start(f32[4,8,128]{2,1,0:T(8,128)S(1)} %pad_maximum_fusion.7), channel_id=1, source_target_pairs={{4,8},{8,4},{5,9},{9,5},{6,10},{10,6},{7,11},{11,7},{20,24},{24,20... | collective-permute-start | bytes 49160 | tf_op jit(solution)/shard_map/ppermute | solution.py:416
  29.9 1.4 %collective-permute-done.8.refs_0_ = f32[4,8,128]{2,1,0:T(8,128)S(1)} collective-permute-done((f32[4,8,128]{2,1,0:T(8,128)S(1)}, f32[4,8,128]{2,1,0:T(8,128)S(1)}, u32[]{:S(2)}, u32[]{:S(2)}) %collective-permute-start.8) | collective-permute-done | bytes 16416 | tf_op jit(solution)/shard_map/ppermute | solution.py:416
  31.3 2.0 %collective-permute-done.9.refs_1_ = f32[4,8,128]{2,1,0:T(8,128)S(1)} collective-permute-done((f32[4,8,128]{2,1,0:T(8,128)S(1)}, f32[4,8,128]{2,1,0:T(8,128)S(1)}, u32[]{:S(2)}, u32[]{:S(2)}) %collective-permute-start.9) | collective-permute-done | bytes 16416 | tf_op jit(solution)/shard_map/ppermute | solution.py:416
  33.3 0.0 collective-permute-done.7.recv_ref
  33.3 0.7 %shard_map.109 = (f32[16,8,128]{2,1,0:T(8,128)S(1)}, f32[6,2048]{1,0:T(8,128)S(1)}, f32[4,8,128]{2,1,0:T(8,128)S(1)}, f32[4,8,128]{2,1,0:T(8,128)S(1)}, f32[2,8,128]{2,1,0:T(8,128)S(1)}) custom-call(f32[16,8,128]{2,1,0:T(8,128)S(1)} %get-tuple-element.48.own_ref, f32[16,8,128]{2,1,0:T(8,128)S(1)} %collective-permute-done.7.recv_ref, ...), custom_call_target="tpu_custom_call" | custom-call | tf_op jit(solution)/shard_map/pallas_call | solution.py:420
  34.0 0.1 collective-permute-start.12
  34.1 0.1 collective-permute-start.10
  34.2 2.4 %collective-permute-start.11 = (f32[4,8,128]{2,1,0:T(8,128)S(1)}, f32[4,8,128]{2,1,0:T(8,128)S(1)}, u32[]{:S(2)}, u32[]{:S(2)}) collective-permute-start(f32[4,8,128]{2,1,0:T(8,128)S(1)} %get-tuple-element.56), channel_id=1, source_target_pairs={{4,8},{8,4},{5,9},{9,5},{6,10},{10,6},{7,11},{11,7},{20,24},{24,20... | collective-permute-start | bytes 49160 | tf_op jit(solution)/shard_map/ppermute | solution.py:350
  36.5 0.0 collective-permute-done.12.refs_1_
  36.6 1.0 %shard_map.110.refs_0_ = f32[8,2048]{1,0:T(8,128)S(1)} custom-call(f32[16,8,128]{2,1,0:T(8,128)S(1)} %get-tuple-element.57.refs_0_.field_ref, f32[16,8,128]{2,1,0:T(8,128)S(1)} %collective-permute-done.12.refs_1_, s32[6,2048]{1,0:T(8,128)S(1)} %and_add_fusion.refs_2_.refs_4_.slots_ref, f32[6,2048]{1,0:T(8,128)S(1)} %copy-done.5, ...), custom_call_target="tpu_custom_call" | custom-call | flops 2000000000 | bytes 2000000 | tf_op jit(solution)/shard_map/pallas_call | solution.py:338
  37.6 0.3 collective-permute-done.10
  37.9 1.9 %collective-permute-done.11 = f32[4,8,128]{2,1,0:T(8,128)S(1)} collective-permute-done((f32[4,8,128]{2,1,0:T(8,128)S(1)}, f32[4,8,128]{2,1,0:T(8,128)S(1)}, u32[]{:S(2)}, u32[]{:S(2)}) %collective-permute-start.11) | collective-permute-done | bytes 16416 | tf_op jit(solution)/shard_map/ppermute | solution.py:350
  39.8 0.8 %collective-permute-start.13 = (f32[6,8,128]{2,1,0:T(8,128)S(1)}, f32[6,8,128]{2,1,0:T(8,128)S(1)}, u32[]{:S(2)}, u32[]{:S(2)}) collective-permute-start(f32[6,8,128]{2,1,0:T(8,128)S(1)} %pad_maximum_fusion.4), channel_id=1, source_target_pairs={{0,2},{2,0},{1,3},{3,1},{4,6},{6,4},{5,7},{7,5},{8,10},{10,8},{9,1... | collective-permute-start | bytes 73736 | tf_op jit(solution)/shard_map/ppermute | solution.py:359
  40.6 1.0 %shard_map.111.refs_1_ = f32[8,2048]{1,0:T(8,128)S(1)} custom-call(f32[16,8,128]{2,1,0:T(8,128)S(1)} %get-tuple-element.57.refs_0_.field_ref, f32[16,8,128]{2,1,0:T(8,128)S(1)} %collective-permute-done.12.refs_1_, s32[6,2048]{1,0:T(8,128)S(1)} %and_add_fusion.refs_2_.refs_4_.slots_ref, f32[6,2048]{1,0:T(8,128)S(1)} %copy-done.5, ...), custom_call_target="tpu_custom_call" | custom-call | flops 2000000000 | bytes 2000000 | tf_op jit(solution)/shard_map/pallas_call | solution.py:338
  41.6 2.1 %collective-permute-done.13 = f32[6,8,128]{2,1,0:T(8,128)S(1)} collective-permute-done((f32[6,8,128]{2,1,0:T(8,128)S(1)}, f32[6,8,128]{2,1,0:T(8,128)S(1)}, u32[]{:S(2)}, u32[]{:S(2)}) %collective-permute-start.13) | collective-permute-done | bytes 24608 | tf_op jit(solution)/shard_map/ppermute | solution.py:359
  43.7 0.1 collective-permute-start.14
  43.8 1.2 %collective-permute-done.14.refs_3_ = f32[10,8,128]{2,1,0:T(8,128)S(1)} collective-permute-done((f32[10,8,128]{2,1,0:T(8,128)S(1)}, f32[10,8,128]{2,1,0:T(8,128)S(1)}, u32[]{:S(2)}, u32[]{:S(2)}) %collective-permute-start.14) | collective-permute-done | bytes 40992 | tf_op jit(solution)/shard_map/ppermute | solution.py:365
  45.0 3.6 %shard_map.112 = (f32[10,8,128]{2,1,0:T(8,128)S(1)}, f32[10,8,128]{2,1,0:T(8,128)S(1)}, f32[16,2048]{1,0:T(8,128)S(1)}) custom-call(f32[8,2048]{1,0:T(8,128)S(1)} %shard_map.110.refs_0_, f32[8,2048]{1,0:T(8,128)S(1)} %shard_map.111.refs_1_, f32[10,8,128]{2,1,0:T(8,128)S(1)} %pad_maximum_fusion.1.refs_2_, f32[10,8,128]{2,1,0:T(8,128)S(1)} %collective-permute-done.14.refs_3_, ...), custom_call_target="tpu_custom_call" | custom-call | flops 5000000000 | bytes 5000000 | tf_op jit(solution)/shard_map/pallas_call | solution.py:366
  48.6 0.2 collective-permute-start.15
  48.8 1.1 %collective-permute-done.15 = f32[10,8,128]{2,1,0:T(8,128)S(1)} collective-permute-done((f32[10,8,128]{2,1,0:T(8,128)S(1)}, f32[10,8,128]{2,1,0:T(8,128)S(1)}, u32[]{:S(2)}, u32[]{:S(2)}) %collective-permute-start.15) | collective-permute-done | bytes 40992 | tf_op jit(solution)/shard_map/ppermute | solution.py:397
  49.9 0.8 %collective-permute-start.16 = (f32[6,8,128]{2,1,0:T(8,128)S(1)}, f32[6,8,128]{2,1,0:T(8,128)S(1)}, u32[]{:S(2)}, u32[]{:S(2)}) collective-permute-start(f32[6,8,128]{2,1,0:T(8,128)S(1)} %pad_maximum_fusion.5), channel_id=1, source_target_pairs={{0,2},{2,0},{1,3},{3,1},{4,6},{6,4},{5,7},{7,5},{8,10},{10,8},{9,1... | collective-permute-start | bytes 73736 | tf_op jit(solution)/shard_map/ppermute | solution.py:407
  50.7 3.0 %shard_map.113 = (f32[16,8,128]{2,1,0:T(8,128)S(1)}, f32[16,8,128]{2,1,0:T(8,128)S(1)}) custom-call(f32[16,2048]{1,0:T(8,128)S(1)} %get-tuple-element.64.force_ref, bf16[256,12288]{1,0:T(8,128)(2,1)S(1)} %get-tuple-element.47.hot_ref.refs_4_.refs_9_, s32[6,2048]{1,0:T(8,128)S(1)} %and_add_fusion.refs_2_.refs_4_.slots_ref, f32[6,2048]{1,0:T(8,128)S(1)} %copy-done.5, ...), custom_call_target="tpu_custom_call" | custom-call | flops 3000000000 | bytes 3000000 | tf_op jit(solution)/shard_map/pallas_call | solution.py:387
  53.7 0.1 collective-permute-done.16
  53.8 0.0 collective-permute-start.18
  53.8 0.1 collective-permute-start.17
  53.9 2.2 %collective-permute-start.19 = (f32[4,8,128]{2,1,0:T(8,128)S(1)}, f32[4,8,128]{2,1,0:T(8,128)S(1)}, u32[]{:S(2)}, u32[]{:S(2)}) collective-permute-start(f32[4,8,128]{2,1,0:T(8,128)S(1)} %pad_maximum_fusion.9), channel_id=1, source_target_pairs={{4,8},{8,4},{5,9},{9,5},{6,10},{10,6},{7,11},{11,7},{20,24},{24,20... | collective-permute-start | bytes 49160 | tf_op jit(solution)/shard_map/ppermute | solution.py:416
  56.1 1.4 %collective-permute-done.18.refs_0_ = f32[4,8,128]{2,1,0:T(8,128)S(1)} collective-permute-done((f32[4,8,128]{2,1,0:T(8,128)S(1)}, f32[4,8,128]{2,1,0:T(8,128)S(1)}, u32[]{:S(2)}, u32[]{:S(2)}) %collective-permute-start.18) | collective-permute-done | bytes 16416 | tf_op jit(solution)/shard_map/ppermute | solution.py:416
  57.6 2.0 %collective-permute-done.19.refs_1_ = f32[4,8,128]{2,1,0:T(8,128)S(1)} collective-permute-done((f32[4,8,128]{2,1,0:T(8,128)S(1)}, f32[4,8,128]{2,1,0:T(8,128)S(1)}, u32[]{:S(2)}, u32[]{:S(2)}) %collective-permute-start.19) | collective-permute-done | bytes 16416 | tf_op jit(solution)/shard_map/ppermute | solution.py:416
  59.6 0.0 collective-permute-done.17.recv_ref
  59.6 1.1 %shard_map.114 = (f32[6,2048]{1,0:T(8,128)}, f32[6,2048]{1,0:T(8,128)}) custom-call(f32[16,8,128]{2,1,0:T(8,128)S(1)} %get-tuple-element.65.own_ref, f32[16,8,128]{2,1,0:T(8,128)S(1)} %collective-permute-done.17.recv_ref, f32[16,8,128]{2,1,0:T(8,128)S(1)} %get-tuple-element.57.refs_0_.field_ref, f32[6,2048]{1,0:T(8,128)S(1)} %get-tuple-element.70.velocity_ref, ...), custom_call_target="tpu_custom_call" | custom-call | tf_op jit(solution)/shard_map/pallas_call | solution.py:420
  (38 shorter events, 0.2 us)
Async XLA Ops:
  0.7 0.8 %copy-start.1 = (f32[6,2048]{1,0:T(8,128)S(1)}, f32[6,2048]{1,0:T(8,128)}, u32[]{:S(2)}) copy-start(f32[6,2048]{1,0:T(8,128)} %displace_ref.1) | copy-start | bytes 147460
  1.6 0.7 %copy-start.3 = (s32[3,3,256]{2,1,0:T(4,128)S(1)}, s32[3,3,256]{2,1,0:T(4,128)}, u32[]{:S(2)}) copy-start(s32[3,3,256]{2,1,0:T(4,128)} %send_ref.1) | copy-start | bytes 27652
  3.1 8.4 %collective-permute-start = (f32[4,8,128]{2,1,0:T(8,128)S(1)}, f32[4,8,128]{2,1,0:T(8,128)S(1)}, u32[]{:S(2)}, u32[]{:S(2)}) collective-permute-start(f32[4,8,128]{2,1,0:T(8,128)S(1)} %get-tuple-element.37), channel_id=1, source_target_pairs={{0,4},{4,0},{8,12},{12,8},{1,5},{5,1},{9,13},{13,9},{2,6},{6,2},{1... | collective-permute-start | bytes 49160 | tf_op jit(solution)/shard_map/ppermute | solution.py:350
  3.2 8.4 %collective-permute-start.1 = (f32[4,8,128]{2,1,0:T(8,128)S(1)}, f32[4,8,128]{2,1,0:T(8,128)S(1)}, u32[]{:S(2)}, u32[]{:S(2)}) collective-permute-start(f32[4,8,128]{2,1,0:T(8,128)S(1)} %get-tuple-element.38), channel_id=1, source_target_pairs={{4,8},{8,4},{5,9},{9,5},{6,10},{10,6},{7,11},{11,7},{20,24},{24,20... | collective-permute-start | bytes 49160 | tf_op jit(solution)/shard_map/ppermute | solution.py:350
  8.2 1.3 %collective-permute-start.2 = (f32[16,8,128]{2,1,0:T(8,128)S(1)}, f32[16,8,128]{2,1,0:T(8,128)S(1)}, u32[]{:S(2)}, u32[]{:S(2)}) collective-permute-start(f32[16,8,128]{2,1,0:T(8,128)S(1)} %get-tuple-element.39.refs_0_.field_ref), channel_id=1, source_target_pairs={{0,1},{1,0},{2,3},{3,2},{4,5},{5,4},{6,7},{7,6},{8,9},{9,8},{10,11... | collective-permute-start | bytes 196616 | tf_op jit(solution)/shard_map/ppermute | solution.py:333
  9.6 0.8 %copy-start.4 = (f32[6,2048]{1,0:T(8,128)S(1)}, f32[6,2048]{1,0:T(8,128)}, u32[]{:S(2)}) copy-start(f32[6,2048]{1,0:T(8,128)} %shape_ref.3) | copy-start | bytes 147460
  10.4 5.2 %copy-start.8 = (f32[8,12,12]{2,0,1:T(8,128)S(1)}, f32[8,12,12]{2,0,1:T(8,128)}, u32[]{:S(2)}) copy-start(f32[8,12,12]{2,0,1:T(8,128)} %param.17) | copy-start | bytes 13828
  10.4 6.4 %copy-start.5 = (f32[6,2048]{1,0:T(8,128)S(1)}, f32[6,2048]{1,0:T(8,128)}, u32[]{:S(2)}) copy-start(f32[6,2048]{1,0:T(8,128)} %shape_ref.3) | copy-start | bytes 147460
  10.4 6.4 %copy-start.6 = (s32[2048]{0:T(1024)S(1)}, s32[2048]{0:T(1024)}, u32[]{:S(2)}) copy-start(s32[2048]{0:T(1024)} %param.15) | copy-start | bytes 24580
  10.4 6.4 %copy-start.7 = (f32[2048]{0:T(1024)S(1)}, f32[2048]{0:T(1024)}, u32[]{:S(2)}) copy-start(f32[2048]{0:T(1024)} %param.16) | copy-start | bytes 24580
  11.6 3.9 %collective-permute-start.3 = (f32[6,8,128]{2,1,0:T(8,128)S(1)}, f32[6,8,128]{2,1,0:T(8,128)S(1)}, u32[]{:S(2)}, u32[]{:S(2)}) collective-permute-start(f32[6,8,128]{2,1,0:T(8,128)S(1)} %pad_maximum_fusion.2), channel_id=1, source_target_pairs={{0,2},{2,0},{1,3},{3,1},{4,6},{6,4},{5,7},{7,5},{8,10},{10,8},{9,1... | collective-permute-start | bytes 73736 | tf_op jit(solution)/shard_map/ppermute | solution.py:359
  15.5 1.3 %collective-permute-start.4 = (f32[10,8,128]{2,1,0:T(8,128)S(1)}, f32[10,8,128]{2,1,0:T(8,128)S(1)}, u32[]{:S(2)}, u32[]{:S(2)}) collective-permute-start(f32[10,8,128]{2,1,0:T(8,128)S(1)} %pad_maximum_fusion.refs_2_), channel_id=1, source_target_pairs={{0,1},{1,0},{2,3},{3,2},{4,5},{5,4},{6,7},{7,6},{8,9},{9,8},{10,11... | collective-permute-start | bytes 122888 | tf_op jit(solution)/shard_map/ppermute | solution.py:365
  21.6 11.7 %copy-start = (f32[6,2048]{1,0:T(8,128)S(1)}, f32[6,2048]{1,0:T(8,128)}, u32[]{:S(2)}) copy-start(f32[6,2048]{1,0:T(8,128)} %velocity_ref.1) | copy-start | bytes 147460
  21.6 11.7 %copy-start.2 = (f32[2048]{0:T(1024)S(1)}, f32[2048]{0:T(1024)}, u32[]{:S(2)}) copy-start(f32[2048]{0:T(1024)} %param.11) | copy-start | bytes 24580
  21.6 1.3 %collective-permute-start.5 = (f32[10,8,128]{2,1,0:T(8,128)S(1)}, f32[10,8,128]{2,1,0:T(8,128)S(1)}, u32[]{:S(2)}, u32[]{:S(2)}) collective-permute-start(f32[10,8,128]{2,1,0:T(8,128)S(1)} %get-tuple-element.50), channel_id=1, source_target_pairs={{0,1},{1,0},{2,3},{3,2},{4,5},{5,4},{6,7},{7,6},{8,9},{9,8},{10,11... | collective-permute-start | bytes 122888 | tf_op jit(solution)/shard_map/ppermute | solution.py:397
  22.9 4.5 %collective-permute-start.6 = (f32[6,8,128]{2,1,0:T(8,128)S(1)}, f32[6,8,128]{2,1,0:T(8,128)S(1)}, u32[]{:S(2)}, u32[]{:S(2)}) collective-permute-start(f32[6,8,128]{2,1,0:T(8,128)S(1)} %pad_maximum_fusion.3), channel_id=1, source_target_pairs={{0,2},{2,0},{1,3},{3,1},{4,6},{6,4},{5,7},{7,5},{8,10},{10,8},{9,1... | collective-permute-start | bytes 73736 | tf_op jit(solution)/shard_map/ppermute | solution.py:407
  27.5 3.8 %collective-permute-start.8 = (f32[4,8,128]{2,1,0:T(8,128)S(1)}, f32[4,8,128]{2,1,0:T(8,128)S(1)}, u32[]{:S(2)}, u32[]{:S(2)}) collective-permute-start(f32[4,8,128]{2,1,0:T(8,128)S(1)} %pad_maximum_fusion.6), channel_id=1, source_target_pairs={{0,4},{4,0},{8,12},{12,8},{1,5},{5,1},{9,13},{13,9},{2,6},{6,2},{1... | collective-permute-start | bytes 49160 | tf_op jit(solution)/shard_map/ppermute | solution.py:416
  27.5 5.7 %collective-permute-start.7 = (f32[16,8,128]{2,1,0:T(8,128)S(1)}, f32[16,8,128]{2,1,0:T(8,128)S(1)}, u32[]{:S(2)}, u32[]{:S(2)}) collective-permute-start(f32[16,8,128]{2,1,0:T(8,128)S(1)} %get-tuple-element.52), channel_id=1, source_target_pairs={{0,1},{1,0},{2,3},{3,2},{4,5},{5,4},{6,7},{7,6},{8,9},{9,8},{10,11... | collective-permute-start | bytes 196616 | tf_op jit(solution)/shard_map/ppermute | solution.py:411
  27.6 5.6 %collective-permute-start.9 = (f32[4,8,128]{2,1,0:T(8,128)S(1)}, f32[4,8,128]{2,1,0:T(8,128)S(1)}, u32[]{:S(2)}, u32[]{:S(2)}) collective-permute-start(f32[4,8,128]{2,1,0:T(8,128)S(1)} %pad_maximum_fusion.7), channel_id=1, source_target_pairs={{4,8},{8,4},{5,9},{9,5},{6,10},{10,6},{7,11},{11,7},{20,24},{24,20... | collective-permute-start | bytes 49160 | tf_op jit(solution)/shard_map/ppermute | solution.py:416
  34.0 2.6 %collective-permute-start.12 = (f32[16,8,128]{2,1,0:T(8,128)S(1)}, f32[16,8,128]{2,1,0:T(8,128)S(1)}, u32[]{:S(2)}, u32[]{:S(2)}) collective-permute-start(f32[16,8,128]{2,1,0:T(8,128)S(1)} %get-tuple-element.57.refs_0_.field_ref), channel_id=1, source_target_pairs={{0,1},{1,0},{2,3},{3,2},{4,5},{5,4},{6,7},{7,6},{8,9},{9,8},{10,11... | collective-permute-start | bytes 196616 | tf_op jit(solution)/shard_map/ppermute | solution.py:333
  34.1 3.8 %collective-permute-start.10 = (f32[4,8,128]{2,1,0:T(8,128)S(1)}, f32[4,8,128]{2,1,0:T(8,128)S(1)}, u32[]{:S(2)}, u32[]{:S(2)}) collective-permute-start(f32[4,8,128]{2,1,0:T(8,128)S(1)} %get-tuple-element.55), channel_id=1, source_target_pairs={{0,4},{4,0},{8,12},{12,8},{1,5},{5,1},{9,13},{13,9},{2,6},{6,2},{1... | collective-permute-start | bytes 49160 | tf_op jit(solution)/shard_map/ppermute | solution.py:350
  34.2 5.6 %collective-permute-start.11 = (f32[4,8,128]{2,1,0:T(8,128)S(1)}, f32[4,8,128]{2,1,0:T(8,128)S(1)}, u32[]{:S(2)}, u32[]{:S(2)}) collective-permute-start(f32[4,8,128]{2,1,0:T(8,128)S(1)} %get-tuple-element.56), channel_id=1, source_target_pairs={{4,8},{8,4},{5,9},{9,5},{6,10},{10,6},{7,11},{11,7},{20,24},{24,20... | collective-permute-start | bytes 49160 | tf_op jit(solution)/shard_map/ppermute | solution.py:350
  39.8 3.9 %collective-permute-start.13 = (f32[6,8,128]{2,1,0:T(8,128)S(1)}, f32[6,8,128]{2,1,0:T(8,128)S(1)}, u32[]{:S(2)}, u32[]{:S(2)}) collective-permute-start(f32[6,8,128]{2,1,0:T(8,128)S(1)} %pad_maximum_fusion.4), channel_id=1, source_target_pairs={{0,2},{2,0},{1,3},{3,1},{4,6},{6,4},{5,7},{7,5},{8,10},{10,8},{9,1... | collective-permute-start | bytes 73736 | tf_op jit(solution)/shard_map/ppermute | solution.py:359
  43.7 1.3 %collective-permute-start.14 = (f32[10,8,128]{2,1,0:T(8,128)S(1)}, f32[10,8,128]{2,1,0:T(8,128)S(1)}, u32[]{:S(2)}, u32[]{:S(2)}) collective-permute-start(f32[10,8,128]{2,1,0:T(8,128)S(1)} %pad_maximum_fusion.1.refs_2_), channel_id=1, source_target_pairs={{0,1},{1,0},{2,3},{3,2},{4,5},{5,4},{6,7},{7,6},{8,9},{9,8},{10,11... | collective-permute-start | bytes 122888 | tf_op jit(solution)/shard_map/ppermute | solution.py:365
  48.6 1.3 %collective-permute-start.15 = (f32[10,8,128]{2,1,0:T(8,128)S(1)}, f32[10,8,128]{2,1,0:T(8,128)S(1)}, u32[]{:S(2)}, u32[]{:S(2)}) collective-permute-start(f32[10,8,128]{2,1,0:T(8,128)S(1)} %get-tuple-element.67), channel_id=1, source_target_pairs={{0,1},{1,0},{2,3},{3,2},{4,5},{5,4},{6,7},{7,6},{8,9},{9,8},{10,11... | collective-permute-start | bytes 122888 | tf_op jit(solution)/shard_map/ppermute | solution.py:397
  49.9 3.9 %collective-permute-start.16 = (f32[6,8,128]{2,1,0:T(8,128)S(1)}, f32[6,8,128]{2,1,0:T(8,128)S(1)}, u32[]{:S(2)}, u32[]{:S(2)}) collective-permute-start(f32[6,8,128]{2,1,0:T(8,128)S(1)} %pad_maximum_fusion.5), channel_id=1, source_target_pairs={{0,2},{2,0},{1,3},{3,1},{4,6},{6,4},{5,7},{7,5},{8,10},{10,8},{9,1... | collective-permute-start | bytes 73736 | tf_op jit(solution)/shard_map/ppermute | solution.py:407
  53.8 3.8 %collective-permute-start.18 = (f32[4,8,128]{2,1,0:T(8,128)S(1)}, f32[4,8,128]{2,1,0:T(8,128)S(1)}, u32[]{:S(2)}, u32[]{:S(2)}) collective-permute-start(f32[4,8,128]{2,1,0:T(8,128)S(1)} %pad_maximum_fusion.8), channel_id=1, source_target_pairs={{0,4},{4,0},{8,12},{12,8},{1,5},{5,1},{9,13},{13,9},{2,6},{6,2},{1... | collective-permute-start | bytes 49160 | tf_op jit(solution)/shard_map/ppermute | solution.py:416
  53.8 5.7 %collective-permute-start.17 = (f32[16,8,128]{2,1,0:T(8,128)S(1)}, f32[16,8,128]{2,1,0:T(8,128)S(1)}, u32[]{:S(2)}, u32[]{:S(2)}) collective-permute-start(f32[16,8,128]{2,1,0:T(8,128)S(1)} %get-tuple-element.69), channel_id=1, source_target_pairs={{0,1},{1,0},{2,3},{3,2},{4,5},{5,4},{6,7},{7,6},{8,9},{9,8},{10,11... | collective-permute-start | bytes 196616 | tf_op jit(solution)/shard_map/ppermute | solution.py:411
  53.9 5.6 %collective-permute-start.19 = (f32[4,8,128]{2,1,0:T(8,128)S(1)}, f32[4,8,128]{2,1,0:T(8,128)S(1)}, u32[]{:S(2)}, u32[]{:S(2)}) collective-permute-start(f32[4,8,128]{2,1,0:T(8,128)S(1)} %pad_maximum_fusion.9), channel_id=1, source_target_pairs={{4,8},{8,4},{5,9},{9,5},{6,10},{10,6},{7,11},{11,7},{20,24},{24,20... | collective-permute-start | bytes 49160 | tf_op jit(solution)/shard_map/ppermute | solution.py:416

commit v4 on v3

--- a/solution.py
+++ b/solution.py
@@ -51,22 +51,46 @@
 
 
 def lists_kernel(U, odd_ref, displace_ref, send_ref, field_ref, picks_ref, *outs):
-    r_odd, c_odd = odd_ref[0], odd_ref[1]
-    swap = [jnp.where(r_odd == 0, send_ref[2 * t], send_ref[2 - 2 * t]) for t in (1, 0)] + [send_ref[1]]
-    at = 0
-    for t in range(3):
-        lists = [swap[t][1:2]]
-        lists += [jnp.where(c_odd == 0, swap[t][2 * u : 2 * u + 1], swap[t][2 - 2 * u : 3 - 2 * u]) for u in (1, 0)]
-        for u in range(U):
-            if t < 2 or u > 0:
-                for half in range(2):
-                    picks_ref[at : at + 1, :] = lists[u][:, half * 128 : (half + 1) * 128]
-                    at += 1
+    r_odd, c_odd = odd_ref[0:1, :], odd_ref[1:2, :]
+    for half in range(2):
+        lists = [send_ref[a][:, half * 128 : (half + 1) * 128] for a in range(3)]
+        swap = [jnp.where(r_odd == 0, lists[2 * t], lists[2 - 2 * t]) for t in (1, 0)] + [lists[1]]
+        at = half
+        for t in range(3):
+            ordered = [swap[t][1:2]]
+            ordered += [
+                jnp.where(c_odd == 0, swap[t][2 * u : 2 * u + 1], swap[t][2 - 2 * u : 3 - 2 * u]) for u in (1, 0)
+            ]
+            for u in range(U):
+                if t < 2 or u > 0:
+                    picks_ref[at : at + 1, :] = ordered[u]
+                    at += 2
+    at -= 1
     if at < 16:
         picks_ref[at:16, :] = jnp.zeros((16 - at, 128), jnp.int32)
     for tile in range(16):
         field_ref[tile] = padded(displace_ref[:, tile * 128 : (tile + 1) * 128])
     pick_lists(field_ref, picks_ref, outs)
+
+
+def relative_slots(U, n, odd_ref, raw_ref, slots_ref):
+    r_odd, c_odd, s = odd_ref[0:1, :], odd_ref[1:2, :], odd_ref[2:3, :]
+    for tile in range(16):
+        cols = slice(tile * 128, (tile + 1) * 128)
+        raw = raw_ref[:, cols]
+        hi = lax.shift_right_logical(raw, 8)
+        sender = (hi >= 25).astype(jnp.int32)
+        direction = hi - 16 - 9 * sender
+        a = (direction >= 3).astype(jnp.int32) + (direction >= 6).astype(jnp.int32)
+        b = direction - 3 * a
+        a = jnp.where(r_odd == 0, a, 2 - a)
+        b = jnp.where(c_odd == 0, b, 2 - b)
+        t = jnp.where(a == 1, 2, jnp.where(a == 0, 0, 1))
+        u = jnp.where(b == 1, 0, jnp.where(b == 0, 1, 2))
+        order = jnp.where(t == 2, 2 * U + u - 1, t * U + u)
+        near = jnp.where(u < U, 16 + n * jnp.where(sender == s, 0, 1) + order, 64)
+        own = jnp.where(hi >= 8, hi - 8, hi) + 8 * jnp.where((hi >= 8).astype(jnp.int32) == s, 0, 1)
+        slots_ref[:, cols] = jnp.where(hi < 16, own, near) * 256 + (raw & 255)
 
 
 def one_hot(lanes):
@@ -145,6 +169,16 @@
     acc_ref[...] += times_one_hot(a_ref[...], hot_ref[:, start : start + 1536])
 
 
+def first_gather_kernel(relate, field_ref, other_ref, odd_ref, raw_ref, shape_ref, slots_ref, *refs):
+    relate(odd_ref, raw_ref, slots_ref)
+    local_gather_kernel(0, True, field_ref, other_ref, slots_ref, shape_ref, *refs)
+
+
+def second_gather_kernel(kinds, field_ref, other_ref, slots_ref, shape_ref, stiff_ref, vec_ref, spread_ref, *refs):
+    spread_ref[...] = spread_stiffness(kinds, stiff_ref[...])
+    local_gather_kernel(1, True, field_ref, other_ref, slots_ref, shape_ref, vec_ref, *refs)
+
+
 def local_gather_kernel(e, build, *refs):
     if build:
         field_ref, other_ref, slots_ref, shape_ref, vec_ref, table_ref, x_refs, hot_ref = refs
@@ -159,13 +193,29 @@
         gather_step(e, quad, 0, 16, table_ref, hot_ref, x_refs, slots_ref, shape_ref, vec_ref)
 
 
+def spread_stiffness(kinds, flat):
+    rows = lax.broadcasted_iota(jnp.int32, (16 * kinds, 12 * kinds), 0)
+    cols = lax.broadcasted_iota(jnp.int32, (16 * kinds, 12 * kinds), 1)
+    within = rows & 15
+    component = within & 7
+    source = jnp.where(within >= 8, 6 + component, component) * kinds + lax.shift_right_logical(rows, 4)
+    pick = jnp.where((component < 6) & (cols == source), 1.0, 0.0)
+    place_row = lax.broadcasted_iota(jnp.int32, (12, 96), 0)
+    within = lax.broadcasted_iota(jnp.int32, (12, 96), 1) & 15
+    component = within & 7
+    place = jnp.where((component < 6) & (place_row == jnp.where(within >= 8, 6 + component, component)), 1.0, 0.0)
+    high = lax.Precision.HIGHEST
+    taken = jnp.dot(pick, flat, precision=high, preferred_element_type=F32)
+    return jnp.dot(taken, place, precision=high, preferred_element_type=F32)
+
+
 def near_kernel(n, kinds, build, *refs):
     vec0_ref, vec1_ref, near_ref, other_ref, slots_ref, shape_ref, kind_ref, weight_ref, stiff_ref = refs[:9]
     if build:
-        own_near_ref, send_ref, force_ref, hot_ref = refs[9:13]
+        own_near_ref, send_ref, force_ref, hot_ref, *refs = refs[9:]
     else:
-        hot_ref, own_near_ref, send_ref, force_ref = refs[9:13]
-    table_ref, x_refs, vec_ref, cat_ref, kinds_ref, a_refs, acc_ref = refs[13:]
+        hot_ref, own_near_ref, send_ref, force_ref, *refs = refs[9:]
+    table_ref, x_refs, vec_ref, cat_ref, kinds_ref, a_refs, acc_ref = refs
     tiles = [lambda half, k=k: near_ref[2 * k + half] for k in range(n)]
     tiles += [lambda half, k=k: other_ref[2 * k + half] for k in range(n)]
     fill_table(tiles, table_ref)
@@ -292,38 +342,21 @@
     s = lax.axis_index("sub")
     row_perm = [pairs(lax.axis_size("rows"), 0), pairs(lax.axis_size("rows"), 1)]
     col_perm = [pairs(cols, 0), pairs(cols, 1)][: U - 1]
+    cross_perm = [[(2 * a + k, 2 * b + 1 - k) for a, b in perm for k in range(2)] for perm in col_perm]
     sub_perm = [(0, 1), (1, 0)]
-
-    slots = beam_slots
-    hi = slots >> 8
-    remote = hi - 16
-    sender = (remote >= 9).astype(jnp.int32)
-    direction = remote - 9 * sender
-    a = (direction >= 3).astype(jnp.int32) + (direction >= 6).astype(jnp.int32)
-    b = direction - 3 * a
-    a = jnp.where(r_odd == 0, a, 2 - a)
-    b = jnp.where(c_odd == 0, b, 2 - b)
-    t = jnp.where(a == 1, 2, a >> 1)
-    u = jnp.where(b == 1, 0, (b >> 1) + 1)
-    order = jnp.where(t == 2, 2 * U + u - 1, t * U + u)
-    rel_near = 16 + n * (sender ^ s) + order
-    rel_near = jnp.where(u < U, rel_near, 64)
-    rel = jnp.where(hi < 16, hi ^ (8 * s), rel_near)
-    slots = rel * 256 + (slots & 255)
 
     kind = beam_kind.reshape(16, 128)
     weight = cluster_weight.reshape(16, 128)
-    stiff = jnp.pad(stiffness.reshape(kinds, 2, 6, 2, 6), ((0, 0), (0, 0), (0, 2), (0, 0), (0, 2)))
-    stiff = jnp.tile(stiff.reshape(kinds * 16, 16), (1, 6))
+    stiff = stiffness.transpose(1, 0, 2).reshape(12 * kinds, 12)
     mass = nodal_mass.reshape(1, -1)
 
     speed = velocity
     list_outs = [f32_out(2 * U, 8, 128), f32_out(2 * U, 8, 128), f32_out(2 * U - 2, 8, 128)]
-    odd = jnp.stack([r_odd, c_odd]).astype(jnp.int32)
+    odd = jnp.broadcast_to(jnp.stack([r_odd, c_odd, s]).astype(jnp.int32)[:, None], (3, 128))
     field, picks, *outgoing = pl.pallas_call(
         functools.partial(lists_kernel, U),
         out_shape=[f32_out(16, 8, 128), jax.ShapeDtypeStruct((16, 128), jnp.int32)] + list_outs,
-        in_specs=[pl.BlockSpec(memory_space=pltpu.SMEM), VMEM, VMEM],
+        in_specs=[VMEM] * 3,
         out_specs=[VMEM] * 5,
         compiler_params=params(),
     )(odd, displace, send_list)
@@ -331,38 +364,67 @@
     tall = 32 * n
     for step in range(STEPS):
         other = lax.ppermute(field, "sub", sub_perm)
-
         build = hot is None
 
-        def local_gather(e):
+        def local_gather(kernel, out_shape, specs, *operands):
             return pl.pallas_call(
-                functools.partial(local_gather_kernel, e, build),
-                out_shape=f32_out(8, 2048),
-                in_specs=[VMEM] * (4 if build else 5),
-                out_specs=VMEM,
+                kernel,
+                out_shape=out_shape,
+                in_specs=specs,
+                out_specs=[VMEM] * len(out_shape),
                 scratch_shapes=[pltpu.VMEM((256, 256), BF16), pltpu.VMEM((2, 256, 1536), F32)]
                 + ([pltpu.VMEM((256, 12288), BF16)] if build else []),
                 compiler_params=params(),
                 cost_estimate=cost(2),
-            )(field, other, slots, shape_values, *([] if build else [hot]))
+            )(field, *operands)
+
+        def plain(e, other):
+            kernel = functools.partial(local_gather_kernel, e, False)
+            return local_gather(kernel, [f32_out(8, 2048)], [VMEM] * 5, other, slots, shape_values, hot)[0]
 
         to_rows, own_row = outgoing[:2], outgoing[2]
         arrived = [lax.ppermute(x, "rows", perm) for x, perm in zip(to_rows, row_perm)]
-        vec0 = local_gather(0)
-        arrived[0], arrived[1], vec0 = lax.optimization_barrier((arrived[0], arrived[1], vec0))
-        near = [[x[0:2]] for x in arrived] + [[]]
+        if build:
+            slots, vec0 = local_gather(
+                functools.partial(first_gather_kernel, functools.partial(relative_slots, U, n)),
+                [jax.ShapeDtypeStruct((6, 2048), jnp.int32), f32_out(8, 2048)],
+                [VMEM] * 5,
+                other,
+                odd,
+                beam_slots,
+                shape_values,
+            )
+        else:
+            vec0 = plain(0, other)
+        arrived[0], arrived[1], vec0, other = lax.optimization_barrier((arrived[0], arrived[1], vec0, other))
+        direct = jnp.concatenate([arrived[0][0:2], arrived[1][0:2]], axis=0)
+        direct_other = lax.ppermute(direct, "sub", sub_perm)
+        near = [[direct[0:2]], [direct[2:4]], []]
+        near_other = [[direct_other[0:2]], [direct_other[2:4]], []]
         for u in range(1, U):
             at = 2 * u
             message = jnp.concatenate(
                 [arrived[0][at : at + 2], arrived[1][at : at + 2], own_row[at - 2 : at]], axis=0
             )
             got = lax.ppermute(message, "cols", col_perm[u - 1])
+            crossed = lax.ppermute(message, ("cols", "sub"), cross_perm[u - 1])
             for t in range(3):
                 near[t].append(got[2 * t : 2 * t + 2])
+                near_other[t].append(crossed[2 * t : 2 * t + 2])
         near = jnp.concatenate(near[0] + near[1] + near[2], axis=0)
-        vec1 = local_gather(1)
-        near, vec1 = lax.optimization_barrier((near, vec1))
-        near_other = lax.ppermute(near, "sub", sub_perm)
+        near_other = jnp.concatenate(near_other[0] + near_other[1] + near_other[2], axis=0)
+        if build:
+            vec1, stiff = local_gather(
+                functools.partial(second_gather_kernel, kinds),
+                [f32_out(8, 2048), f32_out(16 * kinds, 96)],
+                [VMEM] * 5,
+                other,
+                slots,
+                shape_values,
+                stiff,
+            )
+        else:
+            vec1 = plain(1, other)
         own_near, near_send, force, *made = pl.pallas_call(
             functools.partial(near_kernel, n, kinds, build),
             out_shape=[f32_out(2 * n, 8, 128), f32_out(2 * n, 8, 128), f32_out(16, 2048)]
@@ -394,17 +456,20 @@
                 cost_estimate=cost(3),
             )(force, hot, slots, shape_values, weight)
 
-        total = own_near + lax.ppermute(near_send, "sub", sub_perm)
-
-        def listed(t, u):
+        def listed(x, t, u):
             at = 2 * (t * U + u) if t < 2 else 2 * (2 * U + u - 1)
-            return total[at : at + 2]
-
-        back_rows = [[listed(0, 0)], [listed(1, 0)]]
+            return x[at : at + 2]
+
+        direct = jnp.concatenate([listed(near_send, 0, 0), listed(near_send, 1, 0)], axis=0)
+        direct = lax.ppermute(direct, "sub", sub_perm)
+        back_rows = [[listed(own_near, t, 0) + direct[2 * t : 2 * t + 2]] for t in range(2)]
         back_own = []
         for u in range(1, U):
-            message = jnp.concatenate([listed(t, u) for t in range(3)], axis=0)
-            got = lax.ppermute(message, "cols", col_perm[u - 1])
+            messages = [
+                jnp.concatenate([listed(x, t, u) for t in range(3)], axis=0) for x in (own_near, near_send)
+            ]
+            got = lax.ppermute(messages[0], "cols", col_perm[u - 1])
+            got += lax.ppermute(messages[1], ("cols", "sub"), cross_perm[u - 1])
             if u == 1:
                 own, local_send = local_scatter()
                 got, local_send = lax.optimization_barrier((got, local_send))

time: 61 us -> 58.9 us (0.966)
  waiting for transfers between devices: 16.4 us -> 11.7 us
  starting transfers between devices: 17.7 us -> 20.9 us
  other arithmetic: 1.08 us -> 0.18 us
    ppermute x4 -> x10, starting transfers between devices: 0.59 us -> 6.49 us  [the longest x2 2.14 us: shards(): got = lax.ppermute(messages[0], 'cols', col_perm[u - 1])]
    ppermute x4 -> x10, waiting for transfers between devices: 3.7 us -> 0.36 us  [the longest x2 0.34 us: shards(): direct = lax.ppermute(direct, 'sub', sub_perm)]
    ppermute x4 -> x2, starting transfers between devices: 4.77 us -> 1.7 us  [shards(): got = lax.ppermute(message, 'cols', col_perm[u - 1])]
    add x3 -> x4, other arithmetic: 0.95 us -> 0.02 us  [the longest x2 0.01 us: shards(): got += lax.ppermute(messages[1], ('cols', 'sub'), cross_perm[u - 1])]
    ppermute x4 -> x2, waiting for transfers between devices: 3.35 us -> 2.55 us  [shards(): got = lax.ppermute(message, 'cols', col_perm[u - 1])]
    pallas_call x4, Pallas kernels: 4.28 us -> 4.92 us  [local_gather(): pl.pallas_call(kernel, out_shape=out_shape, in_specs=specs, out_specs=[VM...]
    unnamed x19 -> x20, local copies, waits for them, and re-layouts: 2.75 us -> 3.25 us
  transfers between devices with their start and end apart: 20 -> 24, of which waited for: 14 -> 9; matrix products, arithmetic and copies ran while one was open for 3% -> 0% of each run, Pallas kernels for 17% -> 19%
where the time goes in v4:
time: 58.9 us; the launch traced here: 58.5 us
  Pallas kernels  21.2 us (36%)
  starting transfers between devices  20.9 us (35%)
  waiting for transfers between devices  11.7 us (20%)
  local copies, waits for them, and re-layouts  3.39 us (6%)
  between operations  1.21 us (2%)
    pallas_call x2, Pallas kernels, shards(): pl.pallas_call(functools.partial(near_kernel, n, kinds, build), out_shape...  8.24 us
    ppermute x4, starting transfers between devices, shards(): lax.ppermute(x, 'rows', perm)  7.67 us
    ppermute x4, waiting for transfers between devices, shards(): lax.ppermute(jnp.concatenate(x, axis=0), 'rows', perm)  6.62 us
    pallas_call x2, Pallas kernels, local_scatter(): pl.pallas_call(local_scatter_kernel, out_shape=[f32_out(16, 8, 128)] * 2,...  5.92 us
    pallas_call x4, Pallas kernels, local_gather(): pl.pallas_call(kernel, out_shape=out_shape, in_specs=specs, out_specs=[VM...  4.92 us
    ppermute x4, starting transfers between devices, shards(): lax.ppermute(jnp.concatenate(x, axis=0), 'rows', perm)  4.77 us
    unnamed x20, local copies, waits for them, and re-layouts  3.25 us
    ppermute x2, waiting for transfers between devices, shards(): got = lax.ppermute(message, 'cols', col_perm[u - 1])  2.55 us
  transfers between devices with their start and end apart: 24, of which 9 were waited for; matrix products, arithmetic and copies ran while one was open for 0% of the time, Pallas kernels for 19%

profile of v4, /device:TPU:8, one launch (start us, length us, event | category | flops | bytes accessed | tf_op | source)
XLA Modules:
  0.0 58.5 jit_solution(2739607383010022507)
XLA Ops:
  0.6 0.0 copy-start.6
  0.7 0.1 pad_add_fusion
  0.7 0.1 broadcast_in_dim.2.odd_ref
  0.8 0.8 %copy-done.1 = f32[6,2048]{1,0:T(8,128)S(1)} copy-done((f32[6,2048]{1,0:T(8,128)S(1)}, f32[6,2048]{1,0:T(8,128)}, u32[]{:S(2)}) %copy-start.1) | copy-done | bytes 49176
  1.7 0.7 %copy-done.3 = s32[3,3,256]{2,1,0:T(4,128)S(1)} copy-done((s32[3,3,256]{2,1,0:T(4,128)S(1)}, s32[3,3,256]{2,1,0:T(4,128)}, u32[]{:S(2)}) %copy-start.3) | copy-done | bytes 9240
  2.4 0.3 shard_map.104
  2.7 0.1 collective-permute-start.2
  2.7 0.1 collective-permute-start
  2.8 5.0 %collective-permute-start.1 = (f32[4,8,128]{2,1,0:T(8,128)S(1)}, f32[4,8,128]{2,1,0:T(8,128)S(1)}, u32[]{:S(2)}, u32[]{:S(2)}) collective-permute-start(f32[4,8,128]{2,1,0:T(8,128)S(1)} %get-tuple-element.40), channel_id=1, source_target_pairs={{4,8},{8,4},{5,9},{9,5},{6,10},{10,6},{7,11},{11,7},{20,24},{24,20... | collective-permute-start | bytes 49160 | tf_op jit(solution)/shard_map/ppermute | solution.py:386
  7.9 0.0 collective-permute-done.2.other_ref
  7.9 0.0 copy-start.4
  7.9 0.8 %copy-done.4 = s32[6,2048]{1,0:T(8,128)S(1)} copy-done((s32[6,2048]{1,0:T(8,128)S(1)}, s32[6,2048]{1,0:T(8,128)}, u32[]{:S(2)}) %copy-start.4) | copy-done | bytes 49176
  8.7 0.8 %copy-done.5 = f32[6,2048]{1,0:T(8,128)S(1)} copy-done((f32[6,2048]{1,0:T(8,128)S(1)}, f32[6,2048]{1,0:T(8,128)}, u32[]{:S(2)}) %copy-start.5) | copy-done | bytes 49176
  9.6 1.4 %shard_map.105 = (s32[6,2048]{1,0:T(8,128)S(1)}, f32[8,2048]{1,0:T(8,128)S(1)}) custom-call(f32[16,8,128]{2,1,0:T(8,128)S(1)} %get-tuple-element.41.field_ref, f32[16,8,128]{2,1,0:T(8,128)S(1)} %collective-permute-done.2.other_ref, s32[3,128]{1,0:T(4,128)S(1)} %broadcast_in_dim.2.odd_ref, s32[6,2048]{1,0:T(8,128)S(1)} %copy-done.4, f32[6,2048]{1,0:T(8,128)S(1)} %copy-done.5), custom_call_target="tpu_custom_call" | custom-call | flops 2000000000 | bytes 2000000 | tf_op jit(solution)/shard_map/pallas_call | solution.py:370
  11.0 0.0 collective-permute-done
  11.0 0.0 collective-permute-done.1
  11.0 1.0 %collective-permute-start.5 = (f32[6,8,128]{2,1,0:T(8,128)S(1)}, f32[6,8,128]{2,1,0:T(8,128)S(1)}, u32[]{:S(2)}, u32[]{:S(2)}) collective-permute-start(f32[6,8,128]{2,1,0:T(8,128)S(1)} %pad_maximum_fusion.4), channel_id=1, source_target_pairs={{0,3},{1,2},{2,1},{3,0},{4,7},{5,6},{6,5},{7,4},{8,11},{9,10},{10,... | collective-permute-start | bytes 73736 | tf_op jit(solution)/shard_map/ppermute | solution.py:410
  12.1 0.6 %collective-permute-start.3 = (f32[6,8,128]{2,1,0:T(8,128)S(1)}, f32[6,8,128]{2,1,0:T(8,128)S(1)}, u32[]{:S(2)}, u32[]{:S(2)}) collective-permute-start(f32[6,8,128]{2,1,0:T(8,128)S(1)} %pad_maximum_fusion.4), channel_id=1, source_target_pairs={{0,2},{2,0},{1,3},{3,1},{4,6},{6,4},{5,7},{7,5},{8,10},{10,8},{9,1... | collective-permute-start | bytes 73736 | tf_op jit(solution)/shard_map/ppermute | solution.py:409
  12.7 0.3 collective-permute-start.4
  13.0 1.5 %shard_map.106 = (f32[8,2048]{1,0:T(8,128)S(1)}, f32[128,96]{1,0:T(8,128)S(1)}) custom-call(f32[16,8,128]{2,1,0:T(8,128)S(1)} %get-tuple-element.41.field_ref, f32[16,8,128]{2,1,0:T(8,128)S(1)} %collective-permute-done.2.other_ref, s32[6,2048]{1,0:T(8,128)S(1)} %get-tuple-element.45.slots_ref.refs_4_.refs_2_, f32[6,2048]{1,0:T(8,128)S(1)} %copy-done.6, ...), custom_call_target="tpu_custom_call" | custom-call | flops 2000000000 | bytes 2000000 | tf_op jit(solution)/shard_map/pallas_call | solution.py:370
  14.5 1.4 %collective-permute-done.3 = f32[6,8,128]{2,1,0:T(8,128)S(1)} collective-permute-done((f32[6,8,128]{2,1,0:T(8,128)S(1)}, f32[6,8,128]{2,1,0:T(8,128)S(1)}, u32[]{:S(2)}, u32[]{:S(2)}) %collective-permute-start.3) | collective-permute-done | bytes 24608 | tf_op jit(solution)/shard_map/ppermute | solution.py:409
  16.0 4.7 %shard_map.107 = (f32[10,8,128]{2,1,0:T(8,128)S(1)}, f32[10,8,128]{2,1,0:T(8,128)S(1)}, f32[16,2048]{1,0:T(8,128)S(1)}, bf16[256,12288]{1,0:T(8,128)(2,1)S(1)}) custom-call(f32[8,2048]{1,0:T(8,128)S(1)} %get-tuple-element.43.refs_0_, f32[8,2048]{1,0:T(8,128)S(1)} %get-tuple-element.46.refs_1_, f32[10,8,128]{2,1,0:T(8,128)S(1)} %pad_maximum_fusion.refs_2_, ...), custom_call_target="tpu_custom_call" | custom-call | flops 5000000000 | bytes 5000000 | tf_op jit(solution)/shard_map/pallas_call | solution.py:428
  20.7 0.0 copy-start
  20.7 0.0 copy-start.2
  20.8 0.1 collective-permute-start.9
  20.9 0.8 %collective-permute-start.7 = (f32[6,8,128]{2,1,0:T(8,128)S(1)}, f32[6,8,128]{2,1,0:T(8,128)S(1)}, u32[]{:S(2)}, u32[]{:S(2)}) collective-permute-start(f32[6,8,128]{2,1,0:T(8,128)S(1)} %pad_maximum_fusion.6), channel_id=1, source_target_pairs={{0,3},{1,2},{2,1},{3,0},{4,7},{5,6},{6,5},{7,4},{8,11},{9,10},{10,... | collective-permute-start | bytes 73736 | tf_op jit(solution)/shard_map/ppermute | solution.py:472
  21.7 0.3 collective-permute-done.9
  22.0 1.0 %collective-permute-start.6 = (f32[6,8,128]{2,1,0:T(8,128)S(1)}, f32[6,8,128]{2,1,0:T(8,128)S(1)}, u32[]{:S(2)}, u32[]{:S(2)}) collective-permute-start(f32[6,8,128]{2,1,0:T(8,128)S(1)} %pad_maximum_fusion.5), channel_id=1, source_target_pairs={{0,2},{2,0},{1,3},{3,1},{4,6},{6,4},{5,7},{7,5},{8,10},{10,8},{9,1... | collective-permute-start | bytes 73736 | tf_op jit(solution)/shard_map/ppermute | solution.py:471
  23.1 3.0 %shard_map.108 = (f32[16,8,128]{2,1,0:T(8,128)S(1)}, f32[16,8,128]{2,1,0:T(8,128)S(1)}) custom-call(f32[16,2048]{1,0:T(8,128)S(1)} %get-tuple-element.51.force_ref, bf16[256,12288]{1,0:T(8,128)(2,1)S(1)} %get-tuple-element.52.hot_ref.refs_4_.refs_9_, s32[6,2048]{1,0:T(8,128)S(1)} %get-tuple-element.45.slots_ref.refs_4_.refs_2_, f32[6,2048]{1,0:T(8,128)S(1)} %copy-done.6, ...), custom_call_target="tpu_custom_call" | custom-call | flops 3000000000 | bytes 3000000 | tf_op jit(solution)/shard_map/pallas_call | solution.py:449
  26.0 0.0 collective-permute-done.7
  26.1 0.1 collective-permute-start.10
  26.2 0.1 collective-permute-start.8
  26.3 2.3 %collective-permute-start.11 = (f32[4,8,128]{2,1,0:T(8,128)S(1)}, f32[4,8,128]{2,1,0:T(8,128)S(1)}, u32[]{:S(2)}, u32[]{:S(2)}) collective-permute-start(f32[4,8,128]{2,1,0:T(8,128)S(1)} %pad_maximum_fusion.13), channel_id=1, source_target_pairs={{4,8},{8,4},{5,9},{9,5},{6,10},{10,6},{7,11},{11,7},{20,24},{24,20... | collective-permute-start | bytes 49160 | tf_op jit(solution)/shard_map/ppermute | solution.py:481
  28.6 1.3 %collective-permute-done.10.refs_0_ = f32[4,8,128]{2,1,0:T(8,128)S(1)} collective-permute-done((f32[4,8,128]{2,1,0:T(8,128)S(1)}, f32[4,8,128]{2,1,0:T(8,128)S(1)}, u32[]{:S(2)}, u32[]{:S(2)}) %collective-permute-start.10) | collective-permute-done | bytes 16416 | tf_op jit(solution)/shard_map/ppermute | solution.py:481
  29.9 2.0 %collective-permute-done.11.refs_1_ = f32[4,8,128]{2,1,0:T(8,128)S(1)} collective-permute-done((f32[4,8,128]{2,1,0:T(8,128)S(1)}, f32[4,8,128]{2,1,0:T(8,128)S(1)}, u32[]{:S(2)}, u32[]{:S(2)}) %collective-permute-start.11) | collective-permute-done | bytes 16416 | tf_op jit(solution)/shard_map/ppermute | solution.py:481
  31.9 0.0 collective-permute-done.8.recv_ref
  31.9 0.7 %shard_map.109 = (f32[16,8,128]{2,1,0:T(8,128)S(1)}, f32[6,2048]{1,0:T(8,128)S(1)}, f32[4,8,128]{2,1,0:T(8,128)S(1)}, f32[4,8,128]{2,1,0:T(8,128)S(1)}, f32[2,8,128]{2,1,0:T(8,128)S(1)}) custom-call(f32[16,8,128]{2,1,0:T(8,128)S(1)} %get-tuple-element.53.own_ref, f32[16,8,128]{2,1,0:T(8,128)S(1)} %collective-permute-done.8.recv_ref, ...), custom_call_target="tpu_custom_call" | custom-call | tf_op jit(solution)/shard_map/pallas_call | solution.py:485
  32.6 0.1 collective-permute-start.14
  32.7 0.1 collective-permute-start.12
  32.8 2.5 %collective-permute-start.13 = (f32[4,8,128]{2,1,0:T(8,128)S(1)}, f32[4,8,128]{2,1,0:T(8,128)S(1)}, u32[]{:S(2)}, u32[]{:S(2)}) collective-permute-start(f32[4,8,128]{2,1,0:T(8,128)S(1)} %get-tuple-element.61), channel_id=1, source_target_pairs={{4,8},{8,4},{5,9},{9,5},{6,10},{10,6},{7,11},{11,7},{20,24},{24,20... | collective-permute-start | bytes 49160 | tf_op jit(solution)/shard_map/ppermute | solution.py:386
  35.3 0.0 collective-permute-done.14.refs_1_
  35.3 1.0 %shard_map.110.refs_0_ = f32[8,2048]{1,0:T(8,128)S(1)} custom-call(f32[16,8,128]{2,1,0:T(8,128)S(1)} %get-tuple-element.62.refs_0_.field_ref, f32[16,8,128]{2,1,0:T(8,128)S(1)} %collective-permute-done.14.refs_1_, s32[6,2048]{1,0:T(8,128)S(1)} %get-tuple-element.45.slots_ref.refs_4_.refs_2_, f32[6,2048]{1,0:T(8,128)S(1)} %copy-done.6, ...), custom_call_target="tpu_custom_call" | custom-call | flops 2000000000 | bytes 2000000 | tf_op jit(solution)/shard_map/pallas_call | solution.py:370
  36.3 0.2 collective-permute-done.12
  36.5 1.9 %collective-permute-done.13 = f32[4,8,128]{2,1,0:T(8,128)S(1)} collective-permute-done((f32[4,8,128]{2,1,0:T(8,128)S(1)}, f32[4,8,128]{2,1,0:T(8,128)S(1)}, u32[]{:S(2)}, u32[]{:S(2)}) %collective-permute-start.13) | collective-permute-done | bytes 16416 | tf_op jit(solution)/shard_map/ppermute | solution.py:386
  38.4 0.1 collective-permute-start.17
  38.5 1.1 %collective-permute-start.15 = (f32[6,8,128]{2,1,0:T(8,128)S(1)}, f32[6,8,128]{2,1,0:T(8,128)S(1)}, u32[]{:S(2)}, u32[]{:S(2)}) collective-permute-start(f32[6,8,128]{2,1,0:T(8,128)S(1)} %pad_maximum_fusion.7), channel_id=1, source_target_pairs={{0,2},{2,0},{1,3},{3,1},{4,6},{6,4},{5,7},{7,5},{8,10},{10,8},{9,1... | collective-permute-start | bytes 73736 | tf_op jit(solution)/shard_map/ppermute | solution.py:409
  39.6 0.7 %collective-permute-start.16 = (f32[4,8,128]{2,1,0:T(8,128)S(1)}, f32[4,8,128]{2,1,0:T(8,128)S(1)}, u32[]{:S(2)}, u32[]{:S(2)}) collective-permute-start(f32[4,8,128]{2,1,0:T(8,128)S(1)} %pad_maximum_fusion.14), channel_id=1, source_target_pairs={{0,1},{1,0},{2,3},{3,2},{4,5},{5,4},{6,7},{7,6},{8,9},{9,8},{10,11... | collective-permute-start | bytes 49160 | tf_op jit(solution)/shard_map/ppermute | solution.py:401
  40.4 1.0 %shard_map.111.refs_1_ = f32[8,2048]{1,0:T(8,128)S(1)} custom-call(f32[16,8,128]{2,1,0:T(8,128)S(1)} %get-tuple-element.62.refs_0_.field_ref, f32[16,8,128]{2,1,0:T(8,128)S(1)} %collective-permute-done.14.refs_1_, s32[6,2048]{1,0:T(8,128)S(1)} %get-tuple-element.45.slots_ref.refs_4_.refs_2_, f32[6,2048]{1,0:T(8,128)S(1)} %copy-done.6, ...), custom_call_target="tpu_custom_call" | custom-call | flops 2000000000 | bytes 2000000 | tf_op jit(solution)/shard_map/pallas_call | solution.py:370
  41.4 0.0 collective-permute-done.16
  41.4 1.2 %collective-permute-done.15 = f32[6,8,128]{2,1,0:T(8,128)S(1)} collective-permute-done((f32[6,8,128]{2,1,0:T(8,128)S(1)}, f32[6,8,128]{2,1,0:T(8,128)S(1)}, u32[]{:S(2)}, u32[]{:S(2)}) %collective-permute-start.15) | collective-permute-done | bytes 24608 | tf_op jit(solution)/shard_map/ppermute | solution.py:409
  42.6 3.5 %shard_map.112 = (f32[10,8,128]{2,1,0:T(8,128)S(1)}, f32[10,8,128]{2,1,0:T(8,128)S(1)}, f32[16,2048]{1,0:T(8,128)S(1)}) custom-call(f32[8,2048]{1,0:T(8,128)S(1)} %shard_map.110.refs_0_, f32[8,2048]{1,0:T(8,128)S(1)} %shard_map.111.refs_1_, f32[10,8,128]{2,1,0:T(8,128)S(1)} %pad_maximum_fusion.2.refs_2_, f32[10,8,128]{2,1,0:T(8,128)S(1)} %pad_maximum_fusion.3.refs_3_, ...), custom_call_target="tpu_custom_call" | custom-call | flops 5000000000 | bytes 5000000 | tf_op jit(solution)/shard_map/pallas_call | solution.py:428
  46.2 0.2 collective-permute-start.21
  46.4 1.1 %collective-permute-start.19 = (f32[6,8,128]{2,1,0:T(8,128)S(1)}, f32[6,8,128]{2,1,0:T(8,128)S(1)}, u32[]{:S(2)}, u32[]{:S(2)}) collective-permute-start(f32[6,8,128]{2,1,0:T(8,128)S(1)} %pad_maximum_fusion.9), channel_id=1, source_target_pairs={{0,3},{1,2},{2,1},{3,0},{4,7},{5,6},{6,5},{7,4},{8,11},{9,10},{10,... | collective-permute-start | bytes 73736 | tf_op jit(solution)/shard_map/ppermute | solution.py:472
  47.5 0.0 collective-permute-done.21
  47.5 1.1 %collective-permute-start.18 = (f32[6,8,128]{2,1,0:T(8,128)S(1)}, f32[6,8,128]{2,1,0:T(8,128)S(1)}, u32[]{:S(2)}, u32[]{:S(2)}) collective-permute-start(f32[6,8,128]{2,1,0:T(8,128)S(1)} %pad_maximum_fusion.8), channel_id=1, source_target_pairs={{0,2},{2,0},{1,3},{3,1},{4,6},{6,4},{5,7},{7,5},{8,10},{10,8},{9,1... | collective-permute-start | bytes 73736 | tf_op jit(solution)/shard_map/ppermute | solution.py:471
  48.6 3.0 %shard_map.113 = (f32[16,8,128]{2,1,0:T(8,128)S(1)}, f32[16,8,128]{2,1,0:T(8,128)S(1)}) custom-call(f32[16,2048]{1,0:T(8,128)S(1)} %get-tuple-element.68.force_ref, bf16[256,12288]{1,0:T(8,128)(2,1)S(1)} %get-tuple-element.52.hot_ref.refs_4_.refs_9_, s32[6,2048]{1,0:T(8,128)S(1)} %get-tuple-element.45.slots_ref.refs_4_.refs_2_, f32[6,2048]{1,0:T(8,128)S(1)} %copy-done.6, ...), custom_call_target="tpu_custom_call" | custom-call | flops 3000000000 | bytes 3000000 | tf_op jit(solution)/shard_map/pallas_call | solution.py:449
  51.6 0.0 collective-permute-done.19
  51.6 0.0 collective-permute-done.18
  51.6 0.1 collective-permute-start.22
  51.7 0.1 collective-permute-start.20
  51.8 2.3 %collective-permute-start.23 = (f32[4,8,128]{2,1,0:T(8,128)S(1)}, f32[4,8,128]{2,1,0:T(8,128)S(1)}, u32[]{:S(2)}, u32[]{:S(2)}) collective-permute-start(f32[4,8,128]{2,1,0:T(8,128)S(1)} %pad_maximum_fusion.17), channel_id=1, source_target_pairs={{4,8},{8,4},{5,9},{9,5},{6,10},{10,6},{7,11},{11,7},{20,24},{24,20... | collective-permute-start | bytes 49160 | tf_op jit(solution)/shard_map/ppermute | solution.py:481
  54.1 1.3 %collective-permute-done.22.refs_0_ = f32[4,8,128]{2,1,0:T(8,128)S(1)} collective-permute-done((f32[4,8,128]{2,1,0:T(8,128)S(1)}, f32[4,8,128]{2,1,0:T(8,128)S(1)}, u32[]{:S(2)}, u32[]{:S(2)}) %collective-permute-start.22) | collective-permute-done | bytes 16416 | tf_op jit(solution)/shard_map/ppermute | solution.py:481
  55.4 2.0 %collective-permute-done.23.refs_1_ = f32[4,8,128]{2,1,0:T(8,128)S(1)} collective-permute-done((f32[4,8,128]{2,1,0:T(8,128)S(1)}, f32[4,8,128]{2,1,0:T(8,128)S(1)}, u32[]{:S(2)}, u32[]{:S(2)}) %collective-permute-start.23) | collective-permute-done | bytes 16416 | tf_op jit(solution)/shard_map/ppermute | solution.py:481
  57.4 1.1 %shard_map.114 = (f32[6,2048]{1,0:T(8,128)}, f32[6,2048]{1,0:T(8,128)}) custom-call(f32[16,8,128]{2,1,0:T(8,128)S(1)} %get-tuple-element.69.own_ref, f32[16,8,128]{2,1,0:T(8,128)S(1)} %collective-permute-done.20.recv_ref, f32[16,8,128]{2,1,0:T(8,128)S(1)} %get-tuple-element.62.refs_0_.field_ref, f32[6,2048]{1,0:T(8,128)S(1)} %get-tuple-element.74.velocity_ref, ...), custom_call_target="tpu_custom_call" | custom-call | tf_op jit(solution)/shard_map/pallas_call | solution.py:485
  (60 shorter events, 0.2 us)
Async XLA Ops:
  0.6 12.3 %copy-start.6 = (f32[6,2048]{1,0:T(8,128)S(1)}, f32[6,2048]{1,0:T(8,128)}, u32[]{:S(2)}) copy-start(f32[6,2048]{1,0:T(8,128)} %shape_ref.7) | copy-start | bytes 147460
  0.8 0.8 %copy-start.1 = (f32[6,2048]{1,0:T(8,128)S(1)}, f32[6,2048]{1,0:T(8,128)}, u32[]{:S(2)}) copy-start(f32[6,2048]{1,0:T(8,128)} %displace_ref.1) | copy-start | bytes 147460
  1.7 0.7 %copy-start.3 = (s32[3,3,256]{2,1,0:T(4,128)S(1)}, s32[3,3,256]{2,1,0:T(4,128)}, u32[]{:S(2)}) copy-start(s32[3,3,256]{2,1,0:T(4,128)} %send_ref.1) | copy-start | bytes 27652
  2.4 10.6 %copy-start.7 = (f32[8,12,12]{2,0,1:T(8,128)S(1)}, f32[8,12,12]{2,0,1:T(8,128)}, u32[]{:S(2)}) copy-start(f32[8,12,12]{2,0,1:T(8,128)} %param.17) | copy-start | bytes 13828
  2.7 5.2 %collective-permute-start.2 = (f32[16,8,128]{2,1,0:T(8,128)S(1)}, f32[16,8,128]{2,1,0:T(8,128)S(1)}, u32[]{:S(2)}, u32[]{:S(2)}) collective-permute-start(f32[16,8,128]{2,1,0:T(8,128)S(1)} %get-tuple-element.41.field_ref), channel_id=1, source_target_pairs={{0,1},{1,0},{2,3},{3,2},{4,5},{5,4},{6,7},{7,6},{8,9},{9,8},{10,11... | collective-permute-start | bytes 196616 | tf_op jit(solution)/shard_map/ppermute | solution.py:366
  2.7 8.2 %collective-permute-start = (f32[4,8,128]{2,1,0:T(8,128)S(1)}, f32[4,8,128]{2,1,0:T(8,128)S(1)}, u32[]{:S(2)}, u32[]{:S(2)}) collective-permute-start(f32[4,8,128]{2,1,0:T(8,128)S(1)} %get-tuple-element.39), channel_id=1, source_target_pairs={{0,4},{4,0},{8,12},{12,8},{1,5},{5,1},{9,13},{13,9},{2,6},{6,2},{1... | collective-permute-start | bytes 49160 | tf_op jit(solution)/shard_map/ppermute | solution.py:386
  2.8 8.2 %collective-permute-start.1 = (f32[4,8,128]{2,1,0:T(8,128)S(1)}, f32[4,8,128]{2,1,0:T(8,128)S(1)}, u32[]{:S(2)}, u32[]{:S(2)}) collective-permute-start(f32[4,8,128]{2,1,0:T(8,128)S(1)} %get-tuple-element.40), channel_id=1, source_target_pairs={{4,8},{8,4},{5,9},{9,5},{6,10},{10,6},{7,11},{11,7},{20,24},{24,20... | collective-permute-start | bytes 49160 | tf_op jit(solution)/shard_map/ppermute | solution.py:386
  7.9 0.8 %copy-start.4 = (s32[6,2048]{1,0:T(8,128)S(1)}, s32[6,2048]{1,0:T(8,128)}, u32[]{:S(2)}) copy-start(s32[6,2048]{1,0:T(8,128)} %raw_ref.1) | copy-start | bytes 147460
  8.7 0.8 %copy-start.5 = (f32[6,2048]{1,0:T(8,128)S(1)}, f32[6,2048]{1,0:T(8,128)}, u32[]{:S(2)}) copy-start(f32[6,2048]{1,0:T(8,128)} %shape_ref.7) | copy-start | bytes 147460
  9.6 6.4 %copy-start.8 = (s32[2048]{0:T(1024)S(1)}, s32[2048]{0:T(1024)}, u32[]{:S(2)}) copy-start(s32[2048]{0:T(1024)} %param.15) | copy-start | bytes 24580
  9.6 6.4 %copy-start.9 = (f32[2048]{0:T(1024)S(1)}, f32[2048]{0:T(1024)}, u32[]{:S(2)}) copy-start(f32[2048]{0:T(1024)} %param.16) | copy-start | bytes 24580
  11.0 4.9 %collective-permute-start.5 = (f32[6,8,128]{2,1,0:T(8,128)S(1)}, f32[6,8,128]{2,1,0:T(8,128)S(1)}, u32[]{:S(2)}, u32[]{:S(2)}) collective-permute-start(f32[6,8,128]{2,1,0:T(8,128)S(1)} %pad_maximum_fusion.4), channel_id=1, source_target_pairs={{0,3},{1,2},{2,1},{3,0},{4,7},{5,6},{6,5},{7,4},{8,11},{9,10},{10,... | collective-permute-start | bytes 73736 | tf_op jit(solution)/shard_map/ppermute | solution.py:410
  12.1 3.8 %collective-permute-start.3 = (f32[6,8,128]{2,1,0:T(8,128)S(1)}, f32[6,8,128]{2,1,0:T(8,128)S(1)}, u32[]{:S(2)}, u32[]{:S(2)}) collective-permute-start(f32[6,8,128]{2,1,0:T(8,128)S(1)} %pad_maximum_fusion.4), channel_id=1, source_target_pairs={{0,2},{2,0},{1,3},{3,1},{4,6},{6,4},{5,7},{7,5},{8,10},{10,8},{9,1... | collective-permute-start | bytes 73736 | tf_op jit(solution)/shard_map/ppermute | solution.py:409
  12.7 1.8 %collective-permute-start.4 = (f32[4,8,128]{2,1,0:T(8,128)S(1)}, f32[4,8,128]{2,1,0:T(8,128)S(1)}, u32[]{:S(2)}, u32[]{:S(2)}) collective-permute-start(f32[4,8,128]{2,1,0:T(8,128)S(1)} %pad_maximum_fusion.10), channel_id=1, source_target_pairs={{0,1},{1,0},{2,3},{3,2},{4,5},{5,4},{6,7},{7,6},{8,9},{9,8},{10,11... | collective-permute-start | bytes 49160 | tf_op jit(solution)/shard_map/ppermute | solution.py:401
  20.7 11.2 %copy-start = (f32[6,2048]{1,0:T(8,128)S(1)}, f32[6,2048]{1,0:T(8,128)}, u32[]{:S(2)}) copy-start(f32[6,2048]{1,0:T(8,128)} %velocity_ref.1) | copy-start | bytes 147460
  20.7 11.2 %copy-start.2 = (f32[2048]{0:T(1024)S(1)}, f32[2048]{0:T(1024)}, u32[]{:S(2)}) copy-start(f32[2048]{0:T(1024)} %param.11) | copy-start | bytes 24580
  20.8 1.2 %collective-permute-start.9 = (f32[4,8,128]{2,1,0:T(8,128)S(1)}, f32[4,8,128]{2,1,0:T(8,128)S(1)}, u32[]{:S(2)}, u32[]{:S(2)}) collective-permute-start(f32[4,8,128]{2,1,0:T(8,128)S(1)} %pad_maximum_fusion.11), channel_id=1, source_target_pairs={{0,1},{1,0},{2,3},{3,2},{4,5},{5,4},{6,7},{7,6},{8,9},{9,8},{10,11... | collective-permute-start | bytes 49160 | tf_op jit(solution)/shard_map/ppermute | solution.py:464
  20.9 5.2 %collective-permute-start.7 = (f32[6,8,128]{2,1,0:T(8,128)S(1)}, f32[6,8,128]{2,1,0:T(8,128)S(1)}, u32[]{:S(2)}, u32[]{:S(2)}) collective-permute-start(f32[6,8,128]{2,1,0:T(8,128)S(1)} %pad_maximum_fusion.6), channel_id=1, source_target_pairs={{0,3},{1,2},{2,1},{3,0},{4,7},{5,6},{6,5},{7,4},{8,11},{9,10},{10,... | collective-permute-start | bytes 73736 | tf_op jit(solution)/shard_map/ppermute | solution.py:472
  22.0 4.0 %collective-permute-start.6 = (f32[6,8,128]{2,1,0:T(8,128)S(1)}, f32[6,8,128]{2,1,0:T(8,128)S(1)}, u32[]{:S(2)}, u32[]{:S(2)}) collective-permute-start(f32[6,8,128]{2,1,0:T(8,128)S(1)} %pad_maximum_fusion.5), channel_id=1, source_target_pairs={{0,2},{2,0},{1,3},{3,1},{4,6},{6,4},{5,7},{7,5},{8,10},{10,8},{9,1... | collective-permute-start | bytes 73736 | tf_op jit(solution)/shard_map/ppermute | solution.py:471
  26.1 3.8 %collective-permute-start.10 = (f32[4,8,128]{2,1,0:T(8,128)S(1)}, f32[4,8,128]{2,1,0:T(8,128)S(1)}, u32[]{:S(2)}, u32[]{:S(2)}) collective-permute-start(f32[4,8,128]{2,1,0:T(8,128)S(1)} %pad_maximum_fusion.12), channel_id=1, source_target_pairs={{0,4},{4,0},{8,12},{12,8},{1,5},{5,1},{9,13},{13,9},{2,6},{6,2},{1... | collective-permute-start | bytes 49160 | tf_op jit(solution)/shard_map/ppermute | solution.py:481
  26.2 5.7 %collective-permute-start.8 = (f32[16,8,128]{2,1,0:T(8,128)S(1)}, f32[16,8,128]{2,1,0:T(8,128)S(1)}, u32[]{:S(2)}, u32[]{:S(2)}) collective-permute-start(f32[16,8,128]{2,1,0:T(8,128)S(1)} %get-tuple-element.57), channel_id=1, source_target_pairs={{0,1},{1,0},{2,3},{3,2},{4,5},{5,4},{6,7},{7,6},{8,9},{9,8},{10,11... | collective-permute-start | bytes 196616 | tf_op jit(solution)/shard_map/ppermute | solution.py:476
  26.3 5.6 %collective-permute-start.11 = (f32[4,8,128]{2,1,0:T(8,128)S(1)}, f32[4,8,128]{2,1,0:T(8,128)S(1)}, u32[]{:S(2)}, u32[]{:S(2)}) collective-permute-start(f32[4,8,128]{2,1,0:T(8,128)S(1)} %pad_maximum_fusion.13), channel_id=1, source_target_pairs={{4,8},{8,4},{5,9},{9,5},{6,10},{10,6},{7,11},{11,7},{20,24},{24,20... | collective-permute-start | bytes 49160 | tf_op jit(solution)/shard_map/ppermute | solution.py:481
  32.6 2.7 %collective-permute-start.14 = (f32[16,8,128]{2,1,0:T(8,128)S(1)}, f32[16,8,128]{2,1,0:T(8,128)S(1)}, u32[]{:S(2)}, u32[]{:S(2)}) collective-permute-start(f32[16,8,128]{2,1,0:T(8,128)S(1)} %get-tuple-element.62.refs_0_.field_ref), channel_id=1, source_target_pairs={{0,1},{1,0},{2,3},{3,2},{4,5},{5,4},{6,7},{7,6},{8,9},{9,8},{10,11... | collective-permute-start | bytes 196616 | tf_op jit(solution)/shard_map/ppermute | solution.py:366
  32.7 3.8 %collective-permute-start.12 = (f32[4,8,128]{2,1,0:T(8,128)S(1)}, f32[4,8,128]{2,1,0:T(8,128)S(1)}, u32[]{:S(2)}, u32[]{:S(2)}) collective-permute-start(f32[4,8,128]{2,1,0:T(8,128)S(1)} %get-tuple-element.60), channel_id=1, source_target_pairs={{0,4},{4,0},{8,12},{12,8},{1,5},{5,1},{9,13},{13,9},{2,6},{6,2},{1... | collective-permute-start | bytes 49160 | tf_op jit(solution)/shard_map/ppermute | solution.py:386
  32.8 5.6 %collective-permute-start.13 = (f32[4,8,128]{2,1,0:T(8,128)S(1)}, f32[4,8,128]{2,1,0:T(8,128)S(1)}, u32[]{:S(2)}, u32[]{:S(2)}) collective-permute-start(f32[4,8,128]{2,1,0:T(8,128)S(1)} %get-tuple-element.61), channel_id=1, source_target_pairs={{4,8},{8,4},{5,9},{9,5},{6,10},{10,6},{7,11},{11,7},{20,24},{24,20... | collective-permute-start | bytes 49160 | tf_op jit(solution)/shard_map/ppermute | solution.py:386
  38.4 4.1 %collective-permute-start.17 = (f32[6,8,128]{2,1,0:T(8,128)S(1)}, f32[6,8,128]{2,1,0:T(8,128)S(1)}, u32[]{:S(2)}, u32[]{:S(2)}) collective-permute-start(f32[6,8,128]{2,1,0:T(8,128)S(1)} %pad_maximum_fusion.7), channel_id=1, source_target_pairs={{0,3},{1,2},{2,1},{3,0},{4,7},{5,6},{6,5},{7,4},{8,11},{9,10},{10,... | collective-permute-start | bytes 73736 | tf_op jit(solution)/shard_map/ppermute | solution.py:410
  38.5 4.0 %collective-permute-start.15 = (f32[6,8,128]{2,1,0:T(8,128)S(1)}, f32[6,8,128]{2,1,0:T(8,128)S(1)}, u32[]{:S(2)}, u32[]{:S(2)}) collective-permute-start(f32[6,8,128]{2,1,0:T(8,128)S(1)} %pad_maximum_fusion.7), channel_id=1, source_target_pairs={{0,2},{2,0},{1,3},{3,1},{4,6},{6,4},{5,7},{7,5},{8,10},{10,8},{9,1... | collective-permute-start | bytes 73736 | tf_op jit(solution)/shard_map/ppermute | solution.py:409
  39.6 1.7 %collective-permute-start.16 = (f32[4,8,128]{2,1,0:T(8,128)S(1)}, f32[4,8,128]{2,1,0:T(8,128)S(1)}, u32[]{:S(2)}, u32[]{:S(2)}) collective-permute-start(f32[4,8,128]{2,1,0:T(8,128)S(1)} %pad_maximum_fusion.14), channel_id=1, source_target_pairs={{0,1},{1,0},{2,3},{3,2},{4,5},{5,4},{6,7},{7,6},{8,9},{9,8},{10,11... | collective-permute-start | bytes 49160 | tf_op jit(solution)/shard_map/ppermute | solution.py:401
  46.2 1.3 %collective-permute-start.21 = (f32[4,8,128]{2,1,0:T(8,128)S(1)}, f32[4,8,128]{2,1,0:T(8,128)S(1)}, u32[]{:S(2)}, u32[]{:S(2)}) collective-permute-start(f32[4,8,128]{2,1,0:T(8,128)S(1)} %pad_maximum_fusion.15), channel_id=1, source_target_pairs={{0,1},{1,0},{2,3},{3,2},{4,5},{5,4},{6,7},{7,6},{8,9},{9,8},{10,11... | collective-permute-start | bytes 49160 | tf_op jit(solution)/shard_map/ppermute | solution.py:464
  46.4 5.2 %collective-permute-start.19 = (f32[6,8,128]{2,1,0:T(8,128)S(1)}, f32[6,8,128]{2,1,0:T(8,128)S(1)}, u32[]{:S(2)}, u32[]{:S(2)}) collective-permute-start(f32[6,8,128]{2,1,0:T(8,128)S(1)} %pad_maximum_fusion.9), channel_id=1, source_target_pairs={{0,3},{1,2},{2,1},{3,0},{4,7},{5,6},{6,5},{7,4},{8,11},{9,10},{10,... | collective-permute-start | bytes 73736 | tf_op jit(solution)/shard_map/ppermute | solution.py:472
  47.5 4.1 %collective-permute-start.18 = (f32[6,8,128]{2,1,0:T(8,128)S(1)}, f32[6,8,128]{2,1,0:T(8,128)S(1)}, u32[]{:S(2)}, u32[]{:S(2)}) collective-permute-start(f32[6,8,128]{2,1,0:T(8,128)S(1)} %pad_maximum_fusion.8), channel_id=1, source_target_pairs={{0,2},{2,0},{1,3},{3,1},{4,6},{6,4},{5,7},{7,5},{8,10},{10,8},{9,1... | collective-permute-start | bytes 73736 | tf_op jit(solution)/shard_map/ppermute | solution.py:471
  51.6 3.8 %collective-permute-start.22 = (f32[4,8,128]{2,1,0:T(8,128)S(1)}, f32[4,8,128]{2,1,0:T(8,128)S(1)}, u32[]{:S(2)}, u32[]{:S(2)}) collective-permute-start(f32[4,8,128]{2,1,0:T(8,128)S(1)} %pad_maximum_fusion.16), channel_id=1, source_target_pairs={{0,4},{4,0},{8,12},{12,8},{1,5},{5,1},{9,13},{13,9},{2,6},{6,2},{1... | collective-permute-start | bytes 49160 | tf_op jit(solution)/shard_map/ppermute | solution.py:481
  51.7 5.7 %collective-permute-start.20 = (f32[16,8,128]{2,1,0:T(8,128)S(1)}, f32[16,8,128]{2,1,0:T(8,128)S(1)}, u32[]{:S(2)}, u32[]{:S(2)}) collective-permute-start(f32[16,8,128]{2,1,0:T(8,128)S(1)} %get-tuple-element.73), channel_id=1, source_target_pairs={{0,1},{1,0},{2,3},{3,2},{4,5},{5,4},{6,7},{7,6},{8,9},{9,8},{10,11... | collective-permute-start | bytes 196616 | tf_op jit(solution)/shard_map/ppermute | solution.py:476
  51.8 5.6 %collective-permute-start.23 = (f32[4,8,128]{2,1,0:T(8,128)S(1)}, f32[4,8,128]{2,1,0:T(8,128)S(1)}, u32[]{:S(2)}, u32[]{:S(2)}) collective-permute-start(f32[4,8,128]{2,1,0:T(8,128)S(1)} %pad_maximum_fusion.17), channel_id=1, source_target_pairs={{4,8},{8,4},{5,9},{9,5},{6,10},{10,6},{7,11},{11,7},{20,24},{24,20... | collective-permute-start | bytes 49160 | tf_op jit(solution)/shard_map/ppermute | solution.py:481

commit v5 on v4

--- a/solution.py
+++ b/solution.py
@@ -174,9 +174,11 @@
     local_gather_kernel(0, True, field_ref, other_ref, slots_ref, shape_ref, *refs)
 
 
-def second_gather_kernel(kinds, field_ref, other_ref, slots_ref, shape_ref, stiff_ref, vec_ref, spread_ref, *refs):
+def second_gather_kernel(kinds, field_ref, other_ref, slots_ref, shape_ref, stiff_ref, vec_ref, spread_ref, hot_ref, *refs):
     spread_ref[...] = spread_stiffness(kinds, stiff_ref[...])
-    local_gather_kernel(1, True, field_ref, other_ref, slots_ref, shape_ref, vec_ref, *refs)
+    for quad in range(4):
+        build_hot(0, quad, slots_ref, hot_ref)
+    local_gather_kernel(1, True, field_ref, other_ref, slots_ref, shape_ref, vec_ref, *refs, hot_ref)
 
 
 def local_gather_kernel(e, build, *refs):
@@ -209,20 +211,15 @@
     return jnp.dot(taken, place, precision=high, preferred_element_type=F32)
 
 
-def near_kernel(n, kinds, build, *refs):
+def near_kernel(n, kinds, *refs):
     vec0_ref, vec1_ref, near_ref, other_ref, slots_ref, shape_ref, kind_ref, weight_ref, stiff_ref = refs[:9]
-    if build:
-        own_near_ref, send_ref, force_ref, hot_ref, *refs = refs[9:]
-    else:
-        hot_ref, own_near_ref, send_ref, force_ref, *refs = refs[9:]
+    hot_ref, own_near_ref, send_ref, force_ref, *refs = refs[9:]
     table_ref, x_refs, vec_ref, cat_ref, kinds_ref, a_refs, acc_ref = refs
     tiles = [lambda half, k=k: near_ref[2 * k + half] for k in range(n)]
     tiles += [lambda half, k=k: other_ref[2 * k + half] for k in range(n)]
     fill_table(tiles, table_ref)
     for e, base_ref in enumerate((vec0_ref, vec1_ref)):
         for quad in range(4):
-            if build:
-                build_hot(e, quad, slots_ref, hot_ref)
             gather_step(
                 e, quad, 16, 2 * n, table_ref, hot_ref, x_refs, slots_ref, shape_ref, vec_ref.at[e], base_ref
             )
@@ -366,21 +363,21 @@
         other = lax.ppermute(field, "sub", sub_perm)
         build = hot is None
 
-        def local_gather(kernel, out_shape, specs, *operands):
+        def local_gather(kernel, out_shape, specs, scratch, *operands):
             return pl.pallas_call(
                 kernel,
                 out_shape=out_shape,
                 in_specs=specs,
                 out_specs=[VMEM] * len(out_shape),
                 scratch_shapes=[pltpu.VMEM((256, 256), BF16), pltpu.VMEM((2, 256, 1536), F32)]
-                + ([pltpu.VMEM((256, 12288), BF16)] if build else []),
+                + scratch,
                 compiler_params=params(),
                 cost_estimate=cost(2),
             )(field, *operands)
 
         def plain(e, other):
             kernel = functools.partial(local_gather_kernel, e, False)
-            return local_gather(kernel, [f32_out(8, 2048)], [VMEM] * 5, other, slots, shape_values, hot)[0]
+            return local_gather(kernel, [f32_out(8, 2048)], [VMEM] * 5, [], other, slots, shape_values, hot)[0]
 
         to_rows, own_row = outgoing[:2], outgoing[2]
         arrived = [lax.ppermute(x, "rows", perm) for x, perm in zip(to_rows, row_perm)]
@@ -389,6 +386,7 @@
                 functools.partial(first_gather_kernel, functools.partial(relative_slots, U, n)),
                 [jax.ShapeDtypeStruct((6, 2048), jnp.int32), f32_out(8, 2048)],
                 [VMEM] * 5,
+                [pltpu.VMEM((256, 12288), BF16)],
                 other,
                 odd,
                 beam_slots,
@@ -414,10 +412,11 @@
         near = jnp.concatenate(near[0] + near[1] + near[2], axis=0)
         near_other = jnp.concatenate(near_other[0] + near_other[1] + near_other[2], axis=0)
         if build:
-            vec1, stiff = local_gather(
+            vec1, stiff, hot = local_gather(
                 functools.partial(second_gather_kernel, kinds),
-                [f32_out(8, 2048), f32_out(16 * kinds, 96)],
+                [f32_out(8, 2048), f32_out(16 * kinds, 96), jax.ShapeDtypeStruct((256, 12288), BF16)],
                 [VMEM] * 5,
+                [],
                 other,
                 slots,
                 shape_values,
@@ -425,12 +424,11 @@
             )
         else:
             vec1 = plain(1, other)
-        own_near, near_send, force, *made = pl.pallas_call(
-            functools.partial(near_kernel, n, kinds, build),
-            out_shape=[f32_out(2 * n, 8, 128), f32_out(2 * n, 8, 128), f32_out(16, 2048)]
-            + ([jax.ShapeDtypeStruct((256, 12288), BF16)] if build else []),
-            in_specs=[VMEM] * (9 if build else 10),
-            out_specs=[VMEM] * (4 if build else 3),
+        own_near, near_send, force = pl.pallas_call(
+            functools.partial(near_kernel, n, kinds),
+            out_shape=[f32_out(2 * n, 8, 128), f32_out(2 * n, 8, 128), f32_out(16, 2048)],
+            in_specs=[VMEM] * 10,
+            out_specs=[VMEM] * 3,
             scratch_shapes=[
                 pltpu.VMEM((tall, 256), BF16),
                 pltpu.VMEM((2, tall, 1536), F32),
@@ -442,8 +440,7 @@
             ],
             compiler_params=params(),
             cost_estimate=cost(5),
-        )(vec0, vec1, near, near_other, slots, shape_values, kind, weight, stiff, *([] if build else [hot]))
-        hot = made[0] if build else hot
+        )(vec0, vec1, near, near_other, slots, shape_values, kind, weight, stiff, hot)
 
         def local_scatter():
             return pl.pallas_call(

time: 58.9 us -> 57.7 us (0.980)
  Pallas kernels: 21.2 us -> 20.5 us
  waiting for transfers between devices: 11.7 us -> 11 us
    pallas_call x2, Pallas kernels: 8.24 us -> 7.02 us  [shards(): pl.pallas_call(functools.partial(near_kernel, n, kinds), out_shape=[f32_o...]
    pallas_call x4, Pallas kernels: 4.92 us -> 5.52 us  [local_gather(): pl.pallas_call(kernel, out_shape=out_shape, in_specs=specs, out_specs=[VM...]
    ppermute x2, waiting for transfers between devices: 2.55 us -> 1.95 us  [shards(): got = lax.ppermute(message, 'cols', col_perm[u - 1])]
  transfers between devices with their start and end apart: 24 -> 24, of which waited for: 9 -> 9; matrix products, arithmetic and copies ran while one was open for 0% -> 0% of each run, Pallas kernels for 19% -> 20%
where the time goes in v5:
time: 57.7 us; the launch traced here: 57.3 us
  starting transfers between devices  21 us (36%)
  Pallas kernels  20.5 us (36%)
  waiting for transfers between devices  11 us (19%)
  local copies, waits for them, and re-layouts  3.39 us (6%)
  between operations  1.21 us (2%)
    ppermute x4, starting transfers between devices, shards(): lax.ppermute(x, 'rows', perm)  7.68 us
    pallas_call x2, Pallas kernels, shards(): pl.pallas_call(functools.partial(near_kernel, n, kinds), out_shape=[f32_o...  7.02 us
    ppermute x4, waiting for transfers between devices, shards(): lax.ppermute(jnp.concatenate(x, axis=0), 'rows', perm)  6.61 us
    pallas_call x2, Pallas kernels, local_scatter(): pl.pallas_call(local_scatter_kernel, out_shape=[f32_out(16, 8, 128)] * 2,...  5.92 us
    pallas_call x4, Pallas kernels, local_gather(): pl.pallas_call(kernel, out_shape=out_shape, in_specs=specs, out_specs=[VM...  5.52 us
    ppermute x4, starting transfers between devices, shards(): lax.ppermute(jnp.concatenate(x, axis=0), 'rows', perm)  4.78 us
    unnamed x20, local copies, waits for them, and re-layouts  3.25 us
    ppermute x2, starting transfers between devices, shards(): got = lax.ppermute(messages[0], 'cols', col_perm[u - 1])  2.17 us
  transfers between devices with their start and end apart: 24, of which 9 were waited for; matrix products, arithmetic and copies ran while one was open for 0% of the time, Pallas kernels for 20%

profile of v5, /device:TPU:8, one launch (start us, length us, event | category | flops | bytes accessed | tf_op | source)
XLA Modules:
  0.0 57.3 jit_solution(10486714795618262171)
XLA Ops:
  0.6 0.0 copy-start.6
  0.7 0.1 pad_add_fusion
  0.7 0.1 broadcast_in_dim.2.odd_ref
  0.8 0.8 %copy-done.1 = f32[6,2048]{1,0:T(8,128)S(1)} copy-done((f32[6,2048]{1,0:T(8,128)S(1)}, f32[6,2048]{1,0:T(8,128)}, u32[]{:S(2)}) %copy-start.1) | copy-done | bytes 49176
  1.7 0.7 %copy-done.3 = s32[3,3,256]{2,1,0:T(4,128)S(1)} copy-done((s32[3,3,256]{2,1,0:T(4,128)S(1)}, s32[3,3,256]{2,1,0:T(4,128)}, u32[]{:S(2)}) %copy-start.3) | copy-done | bytes 9240
  2.4 0.3 shard_map.104
  2.7 0.1 collective-permute-start.2
  2.7 0.1 collective-permute-start
  2.8 5.0 %collective-permute-start.1 = (f32[4,8,128]{2,1,0:T(8,128)S(1)}, f32[4,8,128]{2,1,0:T(8,128)S(1)}, u32[]{:S(2)}, u32[]{:S(2)}) collective-permute-start(f32[4,8,128]{2,1,0:T(8,128)S(1)} %get-tuple-element.40), channel_id=1, source_target_pairs={{4,8},{8,4},{5,9},{9,5},{6,10},{10,6},{7,11},{11,7},{20,24},{24,20... | collective-permute-start | bytes 49160 | tf_op jit(solution)/shard_map/ppermute | solution.py:383
  7.9 0.0 collective-permute-done.2.other_ref
  7.9 0.0 copy-start.4
  7.9 0.8 %copy-done.4 = s32[6,2048]{1,0:T(8,128)S(1)} copy-done((s32[6,2048]{1,0:T(8,128)S(1)}, s32[6,2048]{1,0:T(8,128)}, u32[]{:S(2)}) %copy-start.4) | copy-done | bytes 49176
  8.7 0.8 %copy-done.5 = f32[6,2048]{1,0:T(8,128)S(1)} copy-done((f32[6,2048]{1,0:T(8,128)S(1)}, f32[6,2048]{1,0:T(8,128)}, u32[]{:S(2)}) %copy-start.5) | copy-done | bytes 49176
  9.6 1.4 %shard_map.105 = (s32[6,2048]{1,0:T(8,128)S(1)}, f32[8,2048]{1,0:T(8,128)S(1)}) custom-call(f32[16,8,128]{2,1,0:T(8,128)S(1)} %get-tuple-element.41.field_ref, f32[16,8,128]{2,1,0:T(8,128)S(1)} %collective-permute-done.2.other_ref, s32[3,128]{1,0:T(4,128)S(1)} %broadcast_in_dim.2.odd_ref, s32[6,2048]{1,0:T(8,128)S(1)} %copy-done.4, f32[6,2048]{1,0:T(8,128)S(1)} %copy-done.5), custom_call_target="tpu_custom_call" | custom-call | flops 2000000000 | bytes 2000000 | tf_op jit(solution)/shard_map/pallas_call | solution.py:367
  11.0 0.0 collective-permute-done
  11.0 0.0 collective-permute-done.1
  11.0 1.0 %collective-permute-start.5 = (f32[6,8,128]{2,1,0:T(8,128)S(1)}, f32[6,8,128]{2,1,0:T(8,128)S(1)}, u32[]{:S(2)}, u32[]{:S(2)}) collective-permute-start(f32[6,8,128]{2,1,0:T(8,128)S(1)} %pad_maximum_fusion.4), channel_id=1, source_target_pairs={{0,3},{1,2},{2,1},{3,0},{4,7},{5,6},{6,5},{7,4},{8,11},{9,10},{10,... | collective-permute-start | bytes 73736 | tf_op jit(solution)/shard_map/ppermute | solution.py:408
  12.1 0.6 %collective-permute-start.3 = (f32[6,8,128]{2,1,0:T(8,128)S(1)}, f32[6,8,128]{2,1,0:T(8,128)S(1)}, u32[]{:S(2)}, u32[]{:S(2)}) collective-permute-start(f32[6,8,128]{2,1,0:T(8,128)S(1)} %pad_maximum_fusion.4), channel_id=1, source_target_pairs={{0,2},{2,0},{1,3},{3,1},{4,6},{6,4},{5,7},{7,5},{8,10},{10,8},{9,1... | collective-permute-start | bytes 73736 | tf_op jit(solution)/shard_map/ppermute | solution.py:407
  12.7 0.3 collective-permute-start.4
  13.0 2.1 %shard_map.106 = (f32[8,2048]{1,0:T(8,128)S(1)}, f32[128,96]{1,0:T(8,128)S(1)}, bf16[256,12288]{1,0:T(8,128)(2,1)S(1)}) custom-call(f32[16,8,128]{2,1,0:T(8,128)S(1)} %get-tuple-element.41.field_ref, f32[16,8,128]{2,1,0:T(8,128)S(1)} %collective-permute-done.2.other_ref, s32[6,2048]{1,0:T(8,128)S(1)} %get-tuple-element.45.slots_ref.refs_4_.refs_2_, ...), custom_call_target="tpu_custom_call" | custom-call | flops 2000000000 | bytes 2000000 | tf_op jit(solution)/shard_map/pallas_call | solution.py:367
  15.1 0.0 collective-permute-done.4
  15.1 0.8 %collective-permute-done.3 = f32[6,8,128]{2,1,0:T(8,128)S(1)} collective-permute-done((f32[6,8,128]{2,1,0:T(8,128)S(1)}, f32[6,8,128]{2,1,0:T(8,128)S(1)}, u32[]{:S(2)}, u32[]{:S(2)}) %collective-permute-start.3) | collective-permute-done | bytes 24608 | tf_op jit(solution)/shard_map/ppermute | solution.py:407
  15.9 0.0 collective-permute-done.5
  16.0 3.5 %shard_map.107 = (f32[10,8,128]{2,1,0:T(8,128)S(1)}, f32[10,8,128]{2,1,0:T(8,128)S(1)}, f32[16,2048]{1,0:T(8,128)S(1)}) custom-call(f32[8,2048]{1,0:T(8,128)S(1)} %get-tuple-element.43.refs_0_, f32[8,2048]{1,0:T(8,128)S(1)} %get-tuple-element.46.refs_1_, f32[10,8,128]{2,1,0:T(8,128)S(1)} %pad_maximum_fusion.refs_2_, ...), custom_call_target="tpu_custom_call" | custom-call | flops 5000000000 | bytes 5000000 | tf_op jit(solution)/shard_map/pallas_call | solution.py:427
  19.5 0.0 copy-start
  19.5 0.0 copy-start.2
  19.6 0.1 collective-permute-start.9
  19.7 0.8 %collective-permute-start.7 = (f32[6,8,128]{2,1,0:T(8,128)S(1)}, f32[6,8,128]{2,1,0:T(8,128)S(1)}, u32[]{:S(2)}, u32[]{:S(2)}) collective-permute-start(f32[6,8,128]{2,1,0:T(8,128)S(1)} %pad_maximum_fusion.6), channel_id=1, source_target_pairs={{0,3},{1,2},{2,1},{3,0},{4,7},{5,6},{6,5},{7,4},{8,11},{9,10},{10,... | collective-permute-start | bytes 73736 | tf_op jit(solution)/shard_map/ppermute | solution.py:469
  20.5 0.3 collective-permute-done.9
  20.8 1.0 %collective-permute-start.6 = (f32[6,8,128]{2,1,0:T(8,128)S(1)}, f32[6,8,128]{2,1,0:T(8,128)S(1)}, u32[]{:S(2)}, u32[]{:S(2)}) collective-permute-start(f32[6,8,128]{2,1,0:T(8,128)S(1)} %pad_maximum_fusion.5), channel_id=1, source_target_pairs={{0,2},{2,0},{1,3},{3,1},{4,6},{6,4},{5,7},{7,5},{8,10},{10,8},{9,1... | collective-permute-start | bytes 73736 | tf_op jit(solution)/shard_map/ppermute | solution.py:468
  21.9 3.0 %shard_map.108 = (f32[16,8,128]{2,1,0:T(8,128)S(1)}, f32[16,8,128]{2,1,0:T(8,128)S(1)}) custom-call(f32[16,2048]{1,0:T(8,128)S(1)} %get-tuple-element.52.force_ref, bf16[256,12288]{1,0:T(8,128)(2,1)S(1)} %get-tuple-element.51.refs_9_.hot_ref.refs_4_, s32[6,2048]{1,0:T(8,128)S(1)} %get-tuple-element.45.slots_ref.refs_4_.refs_2_, f32[6,2048]{1,0:T(8,128)S(1)} %copy-done.6, ...), custom_call_target="tpu_custom_call" | custom-call | flops 3000000000 | bytes 3000000 | tf_op jit(solution)/shard_map/pallas_call | solution.py:446
  24.8 0.0 collective-permute-done.7
  24.8 0.0 collective-permute-done.6
  24.9 0.1 collective-permute-start.10
  25.0 0.1 collective-permute-start.8
  25.1 2.3 %collective-permute-start.11 = (f32[4,8,128]{2,1,0:T(8,128)S(1)}, f32[4,8,128]{2,1,0:T(8,128)S(1)}, u32[]{:S(2)}, u32[]{:S(2)}) collective-permute-start(f32[4,8,128]{2,1,0:T(8,128)S(1)} %pad_maximum_fusion.13), channel_id=1, source_target_pairs={{4,8},{8,4},{5,9},{9,5},{6,10},{10,6},{7,11},{11,7},{20,24},{24,20... | collective-permute-start | bytes 49160 | tf_op jit(solution)/shard_map/ppermute | solution.py:478
  27.4 1.3 %collective-permute-done.10.refs_0_ = f32[4,8,128]{2,1,0:T(8,128)S(1)} collective-permute-done((f32[4,8,128]{2,1,0:T(8,128)S(1)}, f32[4,8,128]{2,1,0:T(8,128)S(1)}, u32[]{:S(2)}, u32[]{:S(2)}) %collective-permute-start.10) | collective-permute-done | bytes 16416 | tf_op jit(solution)/shard_map/ppermute | solution.py:478
  28.7 2.0 %collective-permute-done.11.refs_1_ = f32[4,8,128]{2,1,0:T(8,128)S(1)} collective-permute-done((f32[4,8,128]{2,1,0:T(8,128)S(1)}, f32[4,8,128]{2,1,0:T(8,128)S(1)}, u32[]{:S(2)}, u32[]{:S(2)}) %collective-permute-start.11) | collective-permute-done | bytes 16416 | tf_op jit(solution)/shard_map/ppermute | solution.py:478
  30.7 0.7 %shard_map.109 = (f32[16,8,128]{2,1,0:T(8,128)S(1)}, f32[6,2048]{1,0:T(8,128)S(1)}, f32[4,8,128]{2,1,0:T(8,128)S(1)}, f32[4,8,128]{2,1,0:T(8,128)S(1)}, f32[2,8,128]{2,1,0:T(8,128)S(1)}) custom-call(f32[16,8,128]{2,1,0:T(8,128)S(1)} %get-tuple-element.53.own_ref, f32[16,8,128]{2,1,0:T(8,128)S(1)} %collective-permute-done.8.recv_ref, ...), custom_call_target="tpu_custom_call" | custom-call | tf_op jit(solution)/shard_map/pallas_call | solution.py:482
  31.4 0.1 collective-permute-start.14
  31.5 0.1 collective-permute-start.12
  31.6 2.5 %collective-permute-start.13 = (f32[4,8,128]{2,1,0:T(8,128)S(1)}, f32[4,8,128]{2,1,0:T(8,128)S(1)}, u32[]{:S(2)}, u32[]{:S(2)}) collective-permute-start(f32[4,8,128]{2,1,0:T(8,128)S(1)} %get-tuple-element.61), channel_id=1, source_target_pairs={{4,8},{8,4},{5,9},{9,5},{6,10},{10,6},{7,11},{11,7},{20,24},{24,20... | collective-permute-start | bytes 49160 | tf_op jit(solution)/shard_map/ppermute | solution.py:383
  34.1 0.0 collective-permute-done.14.refs_1_
  34.1 1.0 %shard_map.110.refs_0_ = f32[8,2048]{1,0:T(8,128)S(1)} custom-call(f32[16,8,128]{2,1,0:T(8,128)S(1)} %get-tuple-element.62.refs_0_.field_ref, f32[16,8,128]{2,1,0:T(8,128)S(1)} %collective-permute-done.14.refs_1_, s32[6,2048]{1,0:T(8,128)S(1)} %get-tuple-element.45.slots_ref.refs_4_.refs_2_, f32[6,2048]{1,0:T(8,128)S(1)} %copy-done.6, ...), custom_call_target="tpu_custom_call" | custom-call | flops 2000000000 | bytes 2000000 | tf_op jit(solution)/shard_map/pallas_call | solution.py:367
  35.1 0.2 collective-permute-done.12
  35.3 1.9 %collective-permute-done.13 = f32[4,8,128]{2,1,0:T(8,128)S(1)} collective-permute-done((f32[4,8,128]{2,1,0:T(8,128)S(1)}, f32[4,8,128]{2,1,0:T(8,128)S(1)}, u32[]{:S(2)}, u32[]{:S(2)}) %collective-permute-start.13) | collective-permute-done | bytes 16416 | tf_op jit(solution)/shard_map/ppermute | solution.py:383
  37.2 0.1 collective-permute-start.17
  37.3 1.1 %collective-permute-start.15 = (f32[6,8,128]{2,1,0:T(8,128)S(1)}, f32[6,8,128]{2,1,0:T(8,128)S(1)}, u32[]{:S(2)}, u32[]{:S(2)}) collective-permute-start(f32[6,8,128]{2,1,0:T(8,128)S(1)} %pad_maximum_fusion.7), channel_id=1, source_target_pairs={{0,2},{2,0},{1,3},{3,1},{4,6},{6,4},{5,7},{7,5},{8,10},{10,8},{9,1... | collective-permute-start | bytes 73736 | tf_op jit(solution)/shard_map/ppermute | solution.py:407
  38.4 0.7 %collective-permute-start.16 = (f32[4,8,128]{2,1,0:T(8,128)S(1)}, f32[4,8,128]{2,1,0:T(8,128)S(1)}, u32[]{:S(2)}, u32[]{:S(2)}) collective-permute-start(f32[4,8,128]{2,1,0:T(8,128)S(1)} %pad_maximum_fusion.14), channel_id=1, source_target_pairs={{0,1},{1,0},{2,3},{3,2},{4,5},{5,4},{6,7},{7,6},{8,9},{9,8},{10,11... | collective-permute-start | bytes 49160 | tf_op jit(solution)/shard_map/ppermute | solution.py:399
  39.1 1.0 %shard_map.111.refs_1_ = f32[8,2048]{1,0:T(8,128)S(1)} custom-call(f32[16,8,128]{2,1,0:T(8,128)S(1)} %get-tuple-element.62.refs_0_.field_ref, f32[16,8,128]{2,1,0:T(8,128)S(1)} %collective-permute-done.14.refs_1_, s32[6,2048]{1,0:T(8,128)S(1)} %get-tuple-element.45.slots_ref.refs_4_.refs_2_, f32[6,2048]{1,0:T(8,128)S(1)} %copy-done.6, ...), custom_call_target="tpu_custom_call" | custom-call | flops 2000000000 | bytes 2000000 | tf_op jit(solution)/shard_map/pallas_call | solution.py:367
  40.2 1.2 %collective-permute-done.15 = f32[6,8,128]{2,1,0:T(8,128)S(1)} collective-permute-done((f32[6,8,128]{2,1,0:T(8,128)S(1)}, f32[6,8,128]{2,1,0:T(8,128)S(1)}, u32[]{:S(2)}, u32[]{:S(2)}) %collective-permute-start.15) | collective-permute-done | bytes 24608 | tf_op jit(solution)/shard_map/ppermute | solution.py:407
  41.4 3.5 %shard_map.112 = (f32[10,8,128]{2,1,0:T(8,128)S(1)}, f32[10,8,128]{2,1,0:T(8,128)S(1)}, f32[16,2048]{1,0:T(8,128)S(1)}) custom-call(f32[8,2048]{1,0:T(8,128)S(1)} %shard_map.110.refs_0_, f32[8,2048]{1,0:T(8,128)S(1)} %shard_map.111.refs_1_, f32[10,8,128]{2,1,0:T(8,128)S(1)} %pad_maximum_fusion.2.refs_2_, f32[10,8,128]{2,1,0:T(8,128)S(1)} %pad_maximum_fusion.3.refs_3_, ...), custom_call_target="tpu_custom_call" | custom-call | flops 5000000000 | bytes 5000000 | tf_op jit(solution)/shard_map/pallas_call | solution.py:427
  44.9 0.2 collective-permute-start.21
  45.1 1.1 %collective-permute-start.19 = (f32[6,8,128]{2,1,0:T(8,128)S(1)}, f32[6,8,128]{2,1,0:T(8,128)S(1)}, u32[]{:S(2)}, u32[]{:S(2)}) collective-permute-start(f32[6,8,128]{2,1,0:T(8,128)S(1)} %pad_maximum_fusion.9), channel_id=1, source_target_pairs={{0,3},{1,2},{2,1},{3,0},{4,7},{5,6},{6,5},{7,4},{8,11},{9,10},{10,... | collective-permute-start | bytes 73736 | tf_op jit(solution)/shard_map/ppermute | solution.py:469
  46.3 1.1 %collective-permute-start.18 = (f32[6,8,128]{2,1,0:T(8,128)S(1)}, f32[6,8,128]{2,1,0:T(8,128)S(1)}, u32[]{:S(2)}, u32[]{:S(2)}) collective-permute-start(f32[6,8,128]{2,1,0:T(8,128)S(1)} %pad_maximum_fusion.8), channel_id=1, source_target_pairs={{0,2},{2,0},{1,3},{3,1},{4,6},{6,4},{5,7},{7,5},{8,10},{10,8},{9,1... | collective-permute-start | bytes 73736 | tf_op jit(solution)/shard_map/ppermute | solution.py:468
  47.4 3.0 %shard_map.113 = (f32[16,8,128]{2,1,0:T(8,128)S(1)}, f32[16,8,128]{2,1,0:T(8,128)S(1)}) custom-call(f32[16,2048]{1,0:T(8,128)S(1)} %get-tuple-element.68.force_ref, bf16[256,12288]{1,0:T(8,128)(2,1)S(1)} %get-tuple-element.51.refs_9_.hot_ref.refs_4_, s32[6,2048]{1,0:T(8,128)S(1)} %get-tuple-element.45.slots_ref.refs_4_.refs_2_, f32[6,2048]{1,0:T(8,128)S(1)} %copy-done.6, ...), custom_call_target="tpu_custom_call" | custom-call | flops 3000000000 | bytes 3000000 | tf_op jit(solution)/shard_map/pallas_call | solution.py:446
  50.4 0.0 collective-permute-done.19
  50.4 0.1 collective-permute-start.22
  50.5 0.1 collective-permute-start.20
  50.6 2.3 %collective-permute-start.23 = (f32[4,8,128]{2,1,0:T(8,128)S(1)}, f32[4,8,128]{2,1,0:T(8,128)S(1)}, u32[]{:S(2)}, u32[]{:S(2)}) collective-permute-start(f32[4,8,128]{2,1,0:T(8,128)S(1)} %pad_maximum_fusion.17), channel_id=1, source_target_pairs={{4,8},{8,4},{5,9},{9,5},{6,10},{10,6},{7,11},{11,7},{20,24},{24,20... | collective-permute-start | bytes 49160 | tf_op jit(solution)/shard_map/ppermute | solution.py:478
  52.9 1.3 %collective-permute-done.22.refs_0_ = f32[4,8,128]{2,1,0:T(8,128)S(1)} collective-permute-done((f32[4,8,128]{2,1,0:T(8,128)S(1)}, f32[4,8,128]{2,1,0:T(8,128)S(1)}, u32[]{:S(2)}, u32[]{:S(2)}) %collective-permute-start.22) | collective-permute-done | bytes 16416 | tf_op jit(solution)/shard_map/ppermute | solution.py:478
  54.2 2.0 %collective-permute-done.23.refs_1_ = f32[4,8,128]{2,1,0:T(8,128)S(1)} collective-permute-done((f32[4,8,128]{2,1,0:T(8,128)S(1)}, f32[4,8,128]{2,1,0:T(8,128)S(1)}, u32[]{:S(2)}, u32[]{:S(2)}) %collective-permute-start.23) | collective-permute-done | bytes 16416 | tf_op jit(solution)/shard_map/ppermute | solution.py:478
  56.2 0.0 collective-permute-done.20.recv_ref
  56.2 1.1 %shard_map.114 = (f32[6,2048]{1,0:T(8,128)}, f32[6,2048]{1,0:T(8,128)}) custom-call(f32[16,8,128]{2,1,0:T(8,128)S(1)} %get-tuple-element.69.own_ref, f32[16,8,128]{2,1,0:T(8,128)S(1)} %collective-permute-done.20.recv_ref, f32[16,8,128]{2,1,0:T(8,128)S(1)} %get-tuple-element.62.refs_0_.field_ref, f32[6,2048]{1,0:T(8,128)S(1)} %get-tuple-element.74.velocity_ref, ...), custom_call_target="tpu_custom_call" | custom-call | tf_op jit(solution)/shard_map/pallas_call | solution.py:482
  (60 shorter events, 0.2 us)
Async XLA Ops:
  0.6 12.3 %copy-start.6 = (f32[6,2048]{1,0:T(8,128)S(1)}, f32[6,2048]{1,0:T(8,128)}, u32[]{:S(2)}) copy-start(f32[6,2048]{1,0:T(8,128)} %shape_ref.7) | copy-start | bytes 147460
  0.8 0.8 %copy-start.1 = (f32[6,2048]{1,0:T(8,128)S(1)}, f32[6,2048]{1,0:T(8,128)}, u32[]{:S(2)}) copy-start(f32[6,2048]{1,0:T(8,128)} %displace_ref.1) | copy-start | bytes 147460
  1.7 0.7 %copy-start.3 = (s32[3,3,256]{2,1,0:T(4,128)S(1)}, s32[3,3,256]{2,1,0:T(4,128)}, u32[]{:S(2)}) copy-start(s32[3,3,256]{2,1,0:T(4,128)} %send_ref.1) | copy-start | bytes 27652
  2.4 10.6 %copy-start.7 = (f32[8,12,12]{2,0,1:T(8,128)S(1)}, f32[8,12,12]{2,0,1:T(8,128)}, u32[]{:S(2)}) copy-start(f32[8,12,12]{2,0,1:T(8,128)} %param.17) | copy-start | bytes 13828
  2.7 5.2 %collective-permute-start.2 = (f32[16,8,128]{2,1,0:T(8,128)S(1)}, f32[16,8,128]{2,1,0:T(8,128)S(1)}, u32[]{:S(2)}, u32[]{:S(2)}) collective-permute-start(f32[16,8,128]{2,1,0:T(8,128)S(1)} %get-tuple-element.41.field_ref), channel_id=1, source_target_pairs={{0,1},{1,0},{2,3},{3,2},{4,5},{5,4},{6,7},{7,6},{8,9},{9,8},{10,11... | collective-permute-start | bytes 196616 | tf_op jit(solution)/shard_map/ppermute | solution.py:363
  2.7 8.2 %collective-permute-start = (f32[4,8,128]{2,1,0:T(8,128)S(1)}, f32[4,8,128]{2,1,0:T(8,128)S(1)}, u32[]{:S(2)}, u32[]{:S(2)}) collective-permute-start(f32[4,8,128]{2,1,0:T(8,128)S(1)} %get-tuple-element.39), channel_id=1, source_target_pairs={{0,4},{4,0},{8,12},{12,8},{1,5},{5,1},{9,13},{13,9},{2,6},{6,2},{1... | collective-permute-start | bytes 49160 | tf_op jit(solution)/shard_map/ppermute | solution.py:383
  2.8 8.2 %collective-permute-start.1 = (f32[4,8,128]{2,1,0:T(8,128)S(1)}, f32[4,8,128]{2,1,0:T(8,128)S(1)}, u32[]{:S(2)}, u32[]{:S(2)}) collective-permute-start(f32[4,8,128]{2,1,0:T(8,128)S(1)} %get-tuple-element.40), channel_id=1, source_target_pairs={{4,8},{8,4},{5,9},{9,5},{6,10},{10,6},{7,11},{11,7},{20,24},{24,20... | collective-permute-start | bytes 49160 | tf_op jit(solution)/shard_map/ppermute | solution.py:383
  7.9 0.8 %copy-start.4 = (s32[6,2048]{1,0:T(8,128)S(1)}, s32[6,2048]{1,0:T(8,128)}, u32[]{:S(2)}) copy-start(s32[6,2048]{1,0:T(8,128)} %raw_ref.1) | copy-start | bytes 147460
  8.7 0.8 %copy-start.5 = (f32[6,2048]{1,0:T(8,128)S(1)}, f32[6,2048]{1,0:T(8,128)}, u32[]{:S(2)}) copy-start(f32[6,2048]{1,0:T(8,128)} %shape_ref.7) | copy-start | bytes 147460
  9.6 6.4 %copy-start.8 = (s32[2048]{0:T(1024)S(1)}, s32[2048]{0:T(1024)}, u32[]{:S(2)}) copy-start(s32[2048]{0:T(1024)} %param.15) | copy-start | bytes 24580
  9.6 6.4 %copy-start.9 = (f32[2048]{0:T(1024)S(1)}, f32[2048]{0:T(1024)}, u32[]{:S(2)}) copy-start(f32[2048]{0:T(1024)} %param.16) | copy-start | bytes 24580
  11.0 4.9 %collective-permute-start.5 = (f32[6,8,128]{2,1,0:T(8,128)S(1)}, f32[6,8,128]{2,1,0:T(8,128)S(1)}, u32[]{:S(2)}, u32[]{:S(2)}) collective-permute-start(f32[6,8,128]{2,1,0:T(8,128)S(1)} %pad_maximum_fusion.4), channel_id=1, source_target_pairs={{0,3},{1,2},{2,1},{3,0},{4,7},{5,6},{6,5},{7,4},{8,11},{9,10},{10,... | collective-permute-start | bytes 73736 | tf_op jit(solution)/shard_map/ppermute | solution.py:408
  12.1 3.8 %collective-permute-start.3 = (f32[6,8,128]{2,1,0:T(8,128)S(1)}, f32[6,8,128]{2,1,0:T(8,128)S(1)}, u32[]{:S(2)}, u32[]{:S(2)}) collective-permute-start(f32[6,8,128]{2,1,0:T(8,128)S(1)} %pad_maximum_fusion.4), channel_id=1, source_target_pairs={{0,2},{2,0},{1,3},{3,1},{4,6},{6,4},{5,7},{7,5},{8,10},{10,8},{9,1... | collective-permute-start | bytes 73736 | tf_op jit(solution)/shard_map/ppermute | solution.py:407
  12.7 2.4 %collective-permute-start.4 = (f32[4,8,128]{2,1,0:T(8,128)S(1)}, f32[4,8,128]{2,1,0:T(8,128)S(1)}, u32[]{:S(2)}, u32[]{:S(2)}) collective-permute-start(f32[4,8,128]{2,1,0:T(8,128)S(1)} %pad_maximum_fusion.10), channel_id=1, source_target_pairs={{0,1},{1,0},{2,3},{3,2},{4,5},{5,4},{6,7},{7,6},{8,9},{9,8},{10,11... | collective-permute-start | bytes 49160 | tf_op jit(solution)/shard_map/ppermute | solution.py:399
  19.5 11.2 %copy-start = (f32[6,2048]{1,0:T(8,128)S(1)}, f32[6,2048]{1,0:T(8,128)}, u32[]{:S(2)}) copy-start(f32[6,2048]{1,0:T(8,128)} %velocity_ref.1) | copy-start | bytes 147460
  19.5 11.2 %copy-start.2 = (f32[2048]{0:T(1024)S(1)}, f32[2048]{0:T(1024)}, u32[]{:S(2)}) copy-start(f32[2048]{0:T(1024)} %param.11) | copy-start | bytes 24580
  19.6 1.2 %collective-permute-start.9 = (f32[4,8,128]{2,1,0:T(8,128)S(1)}, f32[4,8,128]{2,1,0:T(8,128)S(1)}, u32[]{:S(2)}, u32[]{:S(2)}) collective-permute-start(f32[4,8,128]{2,1,0:T(8,128)S(1)} %pad_maximum_fusion.11), channel_id=1, source_target_pairs={{0,1},{1,0},{2,3},{3,2},{4,5},{5,4},{6,7},{7,6},{8,9},{9,8},{10,11... | collective-permute-start | bytes 49160 | tf_op jit(solution)/shard_map/ppermute | solution.py:461
  19.7 5.2 %collective-permute-start.7 = (f32[6,8,128]{2,1,0:T(8,128)S(1)}, f32[6,8,128]{2,1,0:T(8,128)S(1)}, u32[]{:S(2)}, u32[]{:S(2)}) collective-permute-start(f32[6,8,128]{2,1,0:T(8,128)S(1)} %pad_maximum_fusion.6), channel_id=1, source_target_pairs={{0,3},{1,2},{2,1},{3,0},{4,7},{5,6},{6,5},{7,4},{8,11},{9,10},{10,... | collective-permute-start | bytes 73736 | tf_op jit(solution)/shard_map/ppermute | solution.py:469
  20.8 4.0 %collective-permute-start.6 = (f32[6,8,128]{2,1,0:T(8,128)S(1)}, f32[6,8,128]{2,1,0:T(8,128)S(1)}, u32[]{:S(2)}, u32[]{:S(2)}) collective-permute-start(f32[6,8,128]{2,1,0:T(8,128)S(1)} %pad_maximum_fusion.5), channel_id=1, source_target_pairs={{0,2},{2,0},{1,3},{3,1},{4,6},{6,4},{5,7},{7,5},{8,10},{10,8},{9,1... | collective-permute-start | bytes 73736 | tf_op jit(solution)/shard_map/ppermute | solution.py:468
  24.9 3.8 %collective-permute-start.10 = (f32[4,8,128]{2,1,0:T(8,128)S(1)}, f32[4,8,128]{2,1,0:T(8,128)S(1)}, u32[]{:S(2)}, u32[]{:S(2)}) collective-permute-start(f32[4,8,128]{2,1,0:T(8,128)S(1)} %pad_maximum_fusion.12), channel_id=1, source_target_pairs={{0,4},{4,0},{8,12},{12,8},{1,5},{5,1},{9,13},{13,9},{2,6},{6,2},{1... | collective-permute-start | bytes 49160 | tf_op jit(solution)/shard_map/ppermute | solution.py:478
  25.0 5.7 %collective-permute-start.8 = (f32[16,8,128]{2,1,0:T(8,128)S(1)}, f32[16,8,128]{2,1,0:T(8,128)S(1)}, u32[]{:S(2)}, u32[]{:S(2)}) collective-permute-start(f32[16,8,128]{2,1,0:T(8,128)S(1)} %get-tuple-element.57), channel_id=1, source_target_pairs={{0,1},{1,0},{2,3},{3,2},{4,5},{5,4},{6,7},{7,6},{8,9},{9,8},{10,11... | collective-permute-start | bytes 196616 | tf_op jit(solution)/shard_map/ppermute | solution.py:473
  25.1 5.6 %collective-permute-start.11 = (f32[4,8,128]{2,1,0:T(8,128)S(1)}, f32[4,8,128]{2,1,0:T(8,128)S(1)}, u32[]{:S(2)}, u32[]{:S(2)}) collective-permute-start(f32[4,8,128]{2,1,0:T(8,128)S(1)} %pad_maximum_fusion.13), channel_id=1, source_target_pairs={{4,8},{8,4},{5,9},{9,5},{6,10},{10,6},{7,11},{11,7},{20,24},{24,20... | collective-permute-start | bytes 49160 | tf_op jit(solution)/shard_map/ppermute | solution.py:478
  31.4 2.7 %collective-permute-start.14 = (f32[16,8,128]{2,1,0:T(8,128)S(1)}, f32[16,8,128]{2,1,0:T(8,128)S(1)}, u32[]{:S(2)}, u32[]{:S(2)}) collective-permute-start(f32[16,8,128]{2,1,0:T(8,128)S(1)} %get-tuple-element.62.refs_0_.field_ref), channel_id=1, source_target_pairs={{0,1},{1,0},{2,3},{3,2},{4,5},{5,4},{6,7},{7,6},{8,9},{9,8},{10,11... | collective-permute-start | bytes 196616 | tf_op jit(solution)/shard_map/ppermute | solution.py:363
  31.5 3.8 %collective-permute-start.12 = (f32[4,8,128]{2,1,0:T(8,128)S(1)}, f32[4,8,128]{2,1,0:T(8,128)S(1)}, u32[]{:S(2)}, u32[]{:S(2)}) collective-permute-start(f32[4,8,128]{2,1,0:T(8,128)S(1)} %get-tuple-element.60), channel_id=1, source_target_pairs={{0,4},{4,0},{8,12},{12,8},{1,5},{5,1},{9,13},{13,9},{2,6},{6,2},{1... | collective-permute-start | bytes 49160 | tf_op jit(solution)/shard_map/ppermute | solution.py:383
  31.6 5.6 %collective-permute-start.13 = (f32[4,8,128]{2,1,0:T(8,128)S(1)}, f32[4,8,128]{2,1,0:T(8,128)S(1)}, u32[]{:S(2)}, u32[]{:S(2)}) collective-permute-start(f32[4,8,128]{2,1,0:T(8,128)S(1)} %get-tuple-element.61), channel_id=1, source_target_pairs={{4,8},{8,4},{5,9},{9,5},{6,10},{10,6},{7,11},{11,7},{20,24},{24,20... | collective-permute-start | bytes 49160 | tf_op jit(solution)/shard_map/ppermute | solution.py:383
  37.2 4.1 %collective-permute-start.17 = (f32[6,8,128]{2,1,0:T(8,128)S(1)}, f32[6,8,128]{2,1,0:T(8,128)S(1)}, u32[]{:S(2)}, u32[]{:S(2)}) collective-permute-start(f32[6,8,128]{2,1,0:T(8,128)S(1)} %pad_maximum_fusion.7), channel_id=1, source_target_pairs={{0,3},{1,2},{2,1},{3,0},{4,7},{5,6},{6,5},{7,4},{8,11},{9,10},{10,... | collective-permute-start | bytes 73736 | tf_op jit(solution)/shard_map/ppermute | solution.py:408
  37.3 4.0 %collective-permute-start.15 = (f32[6,8,128]{2,1,0:T(8,128)S(1)}, f32[6,8,128]{2,1,0:T(8,128)S(1)}, u32[]{:S(2)}, u32[]{:S(2)}) collective-permute-start(f32[6,8,128]{2,1,0:T(8,128)S(1)} %pad_maximum_fusion.7), channel_id=1, source_target_pairs={{0,2},{2,0},{1,3},{3,1},{4,6},{6,4},{5,7},{7,5},{8,10},{10,8},{9,1... | collective-permute-start | bytes 73736 | tf_op jit(solution)/shard_map/ppermute | solution.py:407
  38.4 1.7 %collective-permute-start.16 = (f32[4,8,128]{2,1,0:T(8,128)S(1)}, f32[4,8,128]{2,1,0:T(8,128)S(1)}, u32[]{:S(2)}, u32[]{:S(2)}) collective-permute-start(f32[4,8,128]{2,1,0:T(8,128)S(1)} %pad_maximum_fusion.14), channel_id=1, source_target_pairs={{0,1},{1,0},{2,3},{3,2},{4,5},{5,4},{6,7},{7,6},{8,9},{9,8},{10,11... | collective-permute-start | bytes 49160 | tf_op jit(solution)/shard_map/ppermute | solution.py:399
  44.9 1.3 %collective-permute-start.21 = (f32[4,8,128]{2,1,0:T(8,128)S(1)}, f32[4,8,128]{2,1,0:T(8,128)S(1)}, u32[]{:S(2)}, u32[]{:S(2)}) collective-permute-start(f32[4,8,128]{2,1,0:T(8,128)S(1)} %pad_maximum_fusion.15), channel_id=1, source_target_pairs={{0,1},{1,0},{2,3},{3,2},{4,5},{5,4},{6,7},{7,6},{8,9},{9,8},{10,11... | collective-permute-start | bytes 49160 | tf_op jit(solution)/shard_map/ppermute | solution.py:461
  45.1 5.2 %collective-permute-start.19 = (f32[6,8,128]{2,1,0:T(8,128)S(1)}, f32[6,8,128]{2,1,0:T(8,128)S(1)}, u32[]{:S(2)}, u32[]{:S(2)}) collective-permute-start(f32[6,8,128]{2,1,0:T(8,128)S(1)} %pad_maximum_fusion.9), channel_id=1, source_target_pairs={{0,3},{1,2},{2,1},{3,0},{4,7},{5,6},{6,5},{7,4},{8,11},{9,10},{10,... | collective-permute-start | bytes 73736 | tf_op jit(solution)/shard_map/ppermute | solution.py:469
  46.3 4.1 %collective-permute-start.18 = (f32[6,8,128]{2,1,0:T(8,128)S(1)}, f32[6,8,128]{2,1,0:T(8,128)S(1)}, u32[]{:S(2)}, u32[]{:S(2)}) collective-permute-start(f32[6,8,128]{2,1,0:T(8,128)S(1)} %pad_maximum_fusion.8), channel_id=1, source_target_pairs={{0,2},{2,0},{1,3},{3,1},{4,6},{6,4},{5,7},{7,5},{8,10},{10,8},{9,1... | collective-permute-start | bytes 73736 | tf_op jit(solution)/shard_map/ppermute | solution.py:468
  50.4 3.8 %collective-permute-start.22 = (f32[4,8,128]{2,1,0:T(8,128)S(1)}, f32[4,8,128]{2,1,0:T(8,128)S(1)}, u32[]{:S(2)}, u32[]{:S(2)}) collective-permute-start(f32[4,8,128]{2,1,0:T(8,128)S(1)} %pad_maximum_fusion.16), channel_id=1, source_target_pairs={{0,4},{4,0},{8,12},{12,8},{1,5},{5,1},{9,13},{13,9},{2,6},{6,2},{1... | collective-permute-start | bytes 49160 | tf_op jit(solution)/shard_map/ppermute | solution.py:478
  50.5 5.7 %collective-permute-start.20 = (f32[16,8,128]{2,1,0:T(8,128)S(1)}, f32[16,8,128]{2,1,0:T(8,128)S(1)}, u32[]{:S(2)}, u32[]{:S(2)}) collective-permute-start(f32[16,8,128]{2,1,0:T(8,128)S(1)} %get-tuple-element.73), channel_id=1, source_target_pairs={{0,1},{1,0},{2,3},{3,2},{4,5},{5,4},{6,7},{7,6},{8,9},{9,8},{10,11... | collective-permute-start | bytes 196616 | tf_op jit(solution)/shard_map/ppermute | solution.py:473
  50.6 5.6 %collective-permute-start.23 = (f32[4,8,128]{2,1,0:T(8,128)S(1)}, f32[4,8,128]{2,1,0:T(8,128)S(1)}, u32[]{:S(2)}, u32[]{:S(2)}) collective-permute-start(f32[4,8,128]{2,1,0:T(8,128)S(1)} %pad_maximum_fusion.17), channel_id=1, source_target_pairs={{4,8},{8,4},{5,9},{9,5},{6,10},{10,6},{7,11},{11,7},{20,24},{24,20... | collective-permute-start | bytes 49160 | tf_op jit(solution)/shard_map/ppermute | solution.py:478
